TPU v7x, 256 devices: a whole 4x4x8 slice. The times are simulated.
256 devices in a mesh: dp: 32 (over x, y, z_hi), mp: 8 (over z_lo, core).
Axes of the slice: x: 4, y: 4, z: 8 (z_hi: 2, z_lo: 4; z = z_hi * 4 + z_lo), core: 2. Of those that a mesh axis runs over, the one named last changes fastest.
Arguments:
- activations: bfloat16 [16384, 8192], P('dp'), may hold values from -6 to 6
- cotangent: bfloat16 [16384, 2, 1024], P('dp', None, 'mp'), may hold values from -6 to 6
- param_shard: bfloat16 [8192, 2, 1024], P('dp', None, 'mp'), may hold values from -0.0625 to 0.0625
- master_store: float32 [8192, 2, 1024], P('dp', None, 'mp'), may hold values from -0.0625 to 0.0625
- first_store: float32 [8192, 2, 1024], P('dp', None, 'mp'), may hold values from -768 to 768
- second_store: float32 [8192, 2, 1024], P('dp', None, 'mp'), may hold values from 1024 to 32768
Outputs:
- input_grad: bfloat16 [16384, 8192], P('dp', 'mp')
- new_master: float32 [8192, 2, 1024], P('dp', None, 'mp')
- new_first: float32 [8192, 2, 1024], P('dp', None, 'mp')
- new_second: float32 [8192, 2, 1024], P('dp', None, 'mp')
- new_layer: bfloat16 [8192, 2, 1024], P(None, None, 'mp')
All inputs are finite; a program needn't handle non-finite values.
Results may differ from a plain program's by a relative error of at most 0.0075.
Values may be sent and summed in bfloat16 or wider, within the bound.
No kernel may reach another device: no remote copies, remote signals or barrier semaphores. Data moves between devices by JAX's collectives and lax.ppermute only.
A program may use at most 128 MiB of HBM per device.

v0:
```python
import jax
import jax.numpy as jnp
from jax import lax
from jax.sharding import PartitionSpec as P

learn_rate = 0.001
beta_one = 0.9
beta_two = 0.95
decay_rate = 0.1
epsilon = 1e-08
step_number = 10


def from_behind(array, axis, by):
    devices = lax.axis_size(axis)
    return lax.ppermute(array, axis, [(i, (i + by) % devices) for i in range(devices)])


def per_device(activations, cotangent, param_shard, master_store, first_store, second_store):
    master, first, second = from_behind((master_store, first_store, second_store), "dp", -1)
    terms = jnp.einsum(
        "tjc,rjc->tr",
        cotangent,
        lax.all_gather(param_shard, "dp", axis=0, tiled=True),
        preferred_element_type=jnp.float32,
    )
    input_grad = lax.psum_scatter(terms, "mp", scatter_dimension=1, tiled=True).astype(jnp.bfloat16)
    weight_grad = lax.psum_scatter(
        jnp.einsum(
            "td,tjc->djc", activations, cotangent, preferred_element_type=jnp.float32
        ).astype(jnp.bfloat16),
        "dp",
        scatter_dimension=0,
        tiled=True,
    ).astype(jnp.float32)
    new_first = beta_one * first + (1.0 - beta_one) * weight_grad
    new_second = beta_two * second + (1.0 - beta_two) * weight_grad * weight_grad
    first_hat = new_first / (1.0 - beta_one**step_number)
    second_hat = new_second / (1.0 - beta_two**step_number)
    new_master = master - learn_rate * (
        first_hat / (jnp.sqrt(second_hat) + epsilon) + decay_rate * master
    )
    new_layer = lax.all_gather(new_master.astype(jnp.bfloat16), "dp", axis=0, tiled=True)
    return (input_grad, new_master, new_first, new_second, new_layer)


def solution(mesh):
    return jax.shard_map(
        per_device,
        mesh=mesh,
        in_specs=(
            P("dp", None),
            P("dp", None, "mp"),
            P("dp", None, "mp"),
            P("dp", None, "mp"),
            P("dp", None, "mp"),
            P("dp", None, "mp"),
        ),
        out_specs=(
            P("dp", "mp"),
            P("dp", None, "mp"),
            P("dp", None, "mp"),
            P("dp", None, "mp"),
            P(None, None, "mp"),
        ),
        check_vma=False,
    )
```

profile of v0, /device:TPU:32, one launch (start us, length us, event | category | flops | bytes accessed | tf_op | source)
XLA Modules:
  0.0 706.0 jit_solution(6095611352963279086)
XLA Ops:
  7.2 0.0 reduce-scatter.5.cloned.1.call-start
  7.2 7.8 %convolution_convert_fusion = bf16[8192,2,128]{2,0,1:T(8,128)(2,1)} fusion(bf16[512,8192]{1,0:T(8,128)(2,1)} %param.6, bf16[512,2,128]{2,1,0:T(2,128)(2,1)} %param.7), kind=kOutput, calls=%fused_computation.1 | convolution fusion | flops 2149580800 | bytes 12845056 | tf_op jit(solution)/shard_map/td,tjc->djc/dot_general | solution.py:29
  15.0 0.0 copy-start.4
  15.0 0.0 copy-start
  15.0 0.0 copy-start.1
  15.0 0.0 copy-start.2
  15.0 0.0 copy-start.3
  15.0 0.0 reduce-scatter.5.cloned.1.call-update
  15.1 0.0 all-gather.3.cloned.1.call-start
  15.1 0.8 copy-done.4
  15.9 0.7 copy.11
  16.6 0.0 all-gather.3.cloned.1.call-update
  16.6 0.0 all-gather.5.cloned.1.call-start
  16.7 0.0 copy-done
  16.7 11.0 %collective-permute-start = (f32[256,2,128]{2,0,1:T(8,128)S(1)}, f32[256,2,128]{2,0,1:T(8,128)S(1)}, u32[]{:S(2)}, u32[]{:S(2)}) collective-permute-start(f32[256,2,128]{2,0,1:T(8,128)S(1)} %copy.13), channel_id=1, source_target_pairs={{0,248},{8,0},{16,8},{24,16},{32,24},{40,32},{48,40},{56,48},{64,5... | collective-permute-start | bytes 786440 | tf_op jit(solution)/shard_map/ppermute | solution.py:16
  27.7 0.0 copy-done.1
  27.8 0.1 collective-permute-start.1
  27.9 0.0 copy-done.2
  27.9 6.2 collective-permute-start.2
  34.0 10.1 %collective-permute-done = f32[256,2,128]{2,0,1:T(8,128)S(1)} collective-permute-done((f32[256,2,128]{2,0,1:T(8,128)S(1)}, f32[256,2,128]{2,0,1:T(8,128)S(1)}, u32[]{:S(2)}, u32[]{:S(2)}) %collective-permute-start) | collective-permute-done | bytes 262176 | tf_op jit(solution)/shard_map/ppermute | solution.py:16
  44.1 15.0 %collective-permute-done.1 = f32[256,2,128]{2,0,1:T(8,128)S(1)} collective-permute-done((f32[256,2,128]{2,0,1:T(8,128)S(1)}, f32[256,2,128]{2,0,1:T(8,128)S(1)}, u32[]{:S(2)}, u32[]{:S(2)}) %collective-permute-start.1) | collective-permute-done | bytes 262176 | tf_op jit(solution)/shard_map/ppermute | solution.py:16
  59.1 14.5 %collective-permute-done.2 = f32[256,2,128]{2,0,1:T(8,128)S(1)} collective-permute-done((f32[256,2,128]{2,0,1:T(8,128)S(1)}, f32[256,2,128]{2,0,1:T(8,128)S(1)}, u32[]{:S(2)}, u32[]{:S(2)}) %collective-permute-start.2) | collective-permute-done | bytes 262176 | tf_op jit(solution)/shard_map/ppermute | solution.py:16
  73.6 232.0 %reduce-scatter.5.cloned.1.call-done = bf16[256,2,128]{2,0,1:T(8,128)(2,1)} async-done(((bf16[8192,2,128]{2,0,1:T(8,128)(2,1)}), bf16[256,2,128]{2,0,1:T(8,128)(2,1)}) %reduce-scatter.5.cloned.1.call-update) | async-done | bytes 131088 | tf_op jit(solution)/shard_map/reduce_scatter | solution.py:28
  305.6 1.8 fusion.5
  307.4 0.0 all-gather.5.cloned.1.call-update
  307.4 0.0 reduce-scatter.3.cloned.1.call-start
  307.5 111.9 %all-gather.3.cloned.1.call-done = bf16[8192,2,128]{2,0,1:T(8,128)(2,1)} async-done(((bf16[256,2,128]{2,0,1:T(8,128)(2,1)}), bf16[8192,2,128]{2,0,1:T(8,128)(2,1)}) %all-gather.3.cloned.1.call-update) | async-done | bytes 4194320 | tf_op jit(solution)/shard_map/all_gather | solution.py:24
  419.4 0.0 copy-done.3
  419.4 10.3 %convolution_bitcast_fusion = f32[512,8192]{1,0:T(8,128)} fusion(bf16[8192,2,128]{2,0,1:T(8,128)(2,1)} %all-gather.3.cloned.1.call-done, bf16[512,2,128]{2,1,0:T(2,128)(2,1)S(1)} %copy-done.3), kind=kOutput, calls=%fused_computation | convolution fusion | flops 2147483648 | bytes 21233664 | tf_op jit(solution)/shard_map/tjc,rjc->tr/dot_general | solution.py:21
  429.7 0.0 reduce-scatter.3.cloned.1.call-update
  429.7 0.9 copy.18
  430.6 0.9 copy.19
  431.5 0.9 copy.20
  432.4 97.4 %all-gather.5.cloned.1.call-done = bf16[8192,2,128]{2,0,1:T(8,128)(2,1)} async-done(((bf16[256,2,128]{2,0,1:T(8,128)(2,1)}), bf16[8192,2,128]{2,0,1:T(8,128)(2,1)}) %all-gather.5.cloned.1.call-update) | async-done | bytes 4194320 | tf_op jit(solution)/shard_map/all_gather | solution.py:43
  529.8 10.1 %copy.21 = bf16[8192,2,128]{2,1,0:T(2,128)(2,1)} copy(bf16[8192,2,128]{2,0,1:T(8,128)(2,1)} %all-gather.5.cloned.1.call-done) | data formatting | bytes 8388608
  539.9 156.9 %reduce-scatter.3.cloned.1.call-done = f32[512,1024]{1,0:T(8,128)} async-done(((f32[512,8192]{1,0:T(8,128)}), f32[512,1024]{1,0:T(8,128)}) %reduce-scatter.3.cloned.1.call-update) | async-done | bytes 2097168 | tf_op jit(solution)/shard_map/reduce_scatter | solution.py:27
  696.7 2.7 convert_element_type.12
  (3 shorter events, 0.1 us)
Async XLA Ops:
  7.2 298.5 %reduce-scatter.5.cloned.1.call-start = ((), (), s32[]{:S(2)}) async-start(), calls=%async_computation.4 | async-start | bytes 4325376 | tf_op jit(solution)/shard_map/reduce_scatter | solution.py:28
  15.0 0.9 copy-start.4
  15.0 1.7 copy-start
  15.0 12.7 %copy-start.1 = (f32[256,2,128]{2,1,0:T(2,128)S(1)}, f32[256,2,128]{2,1,0:T(2,128)}, u32[]{:S(2)}) copy-start(f32[256,2,128]{2,1,0:T(2,128)} %param.10) | copy-start | bytes 786436
  15.0 12.8 %copy-start.2 = (f32[256,2,128]{2,1,0:T(2,128)S(1)}, f32[256,2,128]{2,1,0:T(2,128)}, u32[]{:S(2)}) copy-start(f32[256,2,128]{2,1,0:T(2,128)} %param.11) | copy-start | bytes 786436
  15.0 404.3 %copy-start.3 = (bf16[512,2,128]{2,1,0:T(2,128)(2,1)S(1)}, bf16[512,2,128]{2,1,0:T(2,128)(2,1)}, u32[]{:S(2)}) copy-start(bf16[512,2,128]{2,1,0:T(2,128)(2,1)} %param.7) | copy-start | bytes 786436
  15.1 404.3 %all-gather.3.cloned.1.call-start = ((), (), s32[]{:S(2)}) async-start(), calls=%async_computation.2 | async-start | bytes 4325376 | tf_op jit(solution)/shard_map/all_gather | solution.py:24
  16.6 513.2 %all-gather.5.cloned.1.call-start = ((), (), s32[]{:S(2)}) async-start(), calls=%async_computation.5 | async-start | bytes 4325376 | tf_op jit(solution)/shard_map/all_gather | solution.py:43
  16.7 27.4 %collective-permute-start = (f32[256,2,128]{2,0,1:T(8,128)S(1)}, f32[256,2,128]{2,0,1:T(8,128)S(1)}, u32[]{:S(2)}, u32[]{:S(2)}) collective-permute-start(f32[256,2,128]{2,0,1:T(8,128)S(1)} %copy.13), channel_id=1, source_target_pairs={{0,248},{8,0},{16,8},{24,16},{32,24},{40,32},{48,40},{56,48},{64,5... | collective-permute-start | bytes 786440 | tf_op jit(solution)/shard_map/ppermute | solution.py:16
  27.8 31.4 %collective-permute-start.1 = (f32[256,2,128]{2,0,1:T(8,128)S(1)}, f32[256,2,128]{2,0,1:T(8,128)S(1)}, u32[]{:S(2)}, u32[]{:S(2)}) collective-permute-start(f32[256,2,128]{2,0,1:T(8,128)S(1)} %copy.14), channel_id=1, source_target_pairs={{0,248},{8,0},{16,8},{24,16},{32,24},{40,32},{48,40},{56,48},{64,5... | collective-permute-start | bytes 786440 | tf_op jit(solution)/shard_map/ppermute | solution.py:16
  27.9 45.7 %collective-permute-start.2 = (f32[256,2,128]{2,0,1:T(8,128)S(1)}, f32[256,2,128]{2,0,1:T(8,128)S(1)}, u32[]{:S(2)}, u32[]{:S(2)}) collective-permute-start(f32[256,2,128]{2,0,1:T(8,128)S(1)} %copy.17), channel_id=1, source_target_pairs={{0,248},{8,0},{16,8},{24,16},{32,24},{40,32},{48,40},{56,48},{64,5... | collective-permute-start | bytes 786440 | tf_op jit(solution)/shard_map/ppermute | solution.py:16
  307.4 389.3 %reduce-scatter.3.cloned.1.call-start = ((), (), s32[]{:S(2)}) async-start(), calls=%async_computation.3 | async-start | bytes 18874368 | tf_op jit(solution)/shard_map/reduce_scatter | solution.py:27
Sparse Core Ops, SparseCore 0:
  15.2 290.3 reduce-scatter.4
  309.8 109.5 all-gather.2
  423.5 106.2 all-gather.4
  532.3 164.4 reduce-scatter.2
where the time goes:
time: 711 us; the launch traced here: 706 us
  waiting for transfers between devices  638 us (90%)
  matrix products  18.1 us (3%)
  starting transfers between devices  17.4 us (2%)
  local copies, waits for them, and re-layouts  14.4 us (2%)
  between operations  13.8 us (2%)
    reduce_scatter x1, waiting for transfers between devices, per_device(): lax.psum_scatter(jnp.einsum('td,tjc->djc', activations, cotangent, prefer...  232 us
    reduce_scatter x1, waiting for transfers between devices, per_device(): lax.psum_scatter(terms, 'mp', scatter_dimension=1, tiled=True)  157 us
    all_gather x1, waiting for transfers between devices, per_device(): lax.all_gather(param_shard, 'dp', axis=0, tiled=True)  112 us
    all_gather x1, waiting for transfers between devices, per_device(): lax.all_gather(new_master.astype(jnp.bfloat16), 'dp', axis=0, tiled=True)  97.4 us
    ppermute x3, waiting for transfers between devices, from_behind(): lax.ppermute(array, axis, [(i, (i + by) % devices) for i in range(devices)])  39.6 us
    ppermute x3, starting transfers between devices, from_behind(): lax.ppermute(array, axis, [(i, (i + by) % devices) for i in range(devices)])  17.3 us
    unnamed x18, local copies, waits for them, and re-layouts  14.4 us
  transfers between devices with their start and end apart: 7, of which 7 were waited for; matrix products, arithmetic and copies ran while one was open for 4% of the time, Pallas kernels for 0%

commit v1 on v0

v1 whole, which is shorter than its diff:
```python
import functools

import jax
import jax.numpy as jnp
import numpy as np
from jax import lax
from jax.experimental import pallas as pl
from jax.experimental.pallas import tpu as pltpu
from jax.sharding import Mesh, PartitionSpec as P

learn_rate = 0.001
beta_one = 0.9
beta_two = 0.95
decay_rate = 0.1
epsilon = 1e-08
step_number = 10

SIZES = {"x": 4, "y": 4, "h": 2, "l": 4, "c": 2}
AXES = tuple(SIZES)
DP = ("x", "y", "h")
MP = ("l", "c")
MOST = pltpu.CompilerParams(vmem_limit_bytes=56 * 2**20)
WIDE = pltpu.CompilerParams(vmem_limit_bytes=32 * 2**20)


def move(value, target):
    shape = tuple(SIZES.values())
    pairs = []
    for source in range(int(np.prod(shape))):
        at = dict(zip(AXES, (int(i) for i in np.unravel_index(source, shape))))
        to = target(**at)
        pairs.append((source, int(np.ravel_multi_index([to[a] % SIZES[a] for a in AXES], shape))))
    return lax.ppermute(value, AXES, pairs)


def along_first(by):
    def target(x, y, h, l, c):
        return dict(x=x + by * (1 - c), y=y + by * c, h=h, l=l, c=c)

    return target


def along_second(by):
    def target(x, y, h, l, c):
        return dict(x=x + by * c, y=y + by * (1 - c), h=h, l=l, c=c)

    return target


def other_half(x, y, h, l, c):
    return dict(x=x, y=y, h=h + 1, l=l, c=c)


def other_core(x, y, h, l, c):
    return dict(x=x, y=y, h=h, l=l, c=c + 1)


def next_in_line(x, y, h, l, c):
    return dict(x=x, y=y, h=h, l=l + 1, c=c)


def back_in_line(x, y, h, l, c):
    return dict(x=x, y=y, h=h, l=l - 1, c=c)


def previous_block(x, y, h, l, c):
    block = (x * 8 + y * 2 + h - 1) % 32
    return dict(x=block // 8, y=block // 2 % 4, h=block % 2, l=l, c=c)


def to_user(x, y, h, l, c):
    return dict(x=l, y=2 * c + y % 2, h=h, l=x, c=y // 2)


def to_user_across(x, y, h, l, c):
    return dict(to_user(x, y, h, l, c), h=h + 1)


def pair_at(here, first, second):
    x, y, c = here[0], here[1], here[4]
    first, second = (x + c * (y - x) + first) % 4, (y + c * (x - y) + second) % 4
    return 4 * (first + c * (second - first)) + second + c * (first - second)


def block_at(here, first, second, s, blocks):
    return (2 * pair_at(here, first, second) + blocks - 1 + s) % blocks


def fetch(here, activations, held, sems, g, first, second, s):
    rows = held.shape[2] // 2
    block = block_at(here, first, second, s, activations.shape[1] // rows)
    return pltpu.make_async_copy(
        activations.at[:, pl.ds(pl.multiple_of(block * rows, rows), rows)],
        held.at[g, :, pl.ds(s * rows, rows)],
        sems.at[g, s],
    )


def fetch_all(groups, here, activations, held, sems):
    g = 0
    for first, second, count in groups:
        for i in range(count):
            for s in range(2):
                fetch(here, activations, held, sems, g, first, second + i, s).start()
            g += 1


def multiply_all(groups, here, cot, activations, outs, held, sems, received=()):
    rows = held.shape[2] // 2
    done = 0
    for n, (first, second, count) in enumerate(groups):
        out = outs[n // 2] if received else outs[n]
        base = 2 * (n % 2) if received else 0
        got = received[n // 2] if received and n in (0, 3) else None

        def step(i, carry, out=out, base=base, got=got, done=done, first=first, second=second):
            for s in range(2):
                fetch(here, activations, held, sems, done + i, first, second + i, s).wait()
            both = jnp.dot(cot[...], held[done + i], preferred_element_type=jnp.float32)
            for s in range(2):
                term = both[:, s * rows : (s + 1) * rows]
                if got is not None:
                    term += got[i, here[2] ^ s].astype(jnp.float32)
                out[base + i, here[2] ^ s] = term.astype(out.dtype)
            return carry

        lax.fori_loop(0, count, step, 0)
        done += count


def first_kernel(groups, here, cot_in, par_in, activations, *refs):
    cot, cot_t, par_t, *outs = refs[: 3 + len(groups)]
    held, sems, cot_raw, par_raw, raw_sems, wide = refs[3 + len(groups) :]
    raw = (
        pltpu.make_async_copy(cot_in, cot_raw, raw_sems.at[0]),
        pltpu.make_async_copy(par_in, par_raw, raw_sems.at[1]),
    )
    raw[0].start()
    fetch_all(groups, here, activations, held, sems)
    raw[1].start()
    for copy, source, plain, turned in ((raw[0], cot_raw, cot, cot_t), (raw[1], par_raw, None, par_t)):
        copy.wait()
        rows, width = source.shape[0] // 2, source.shape[1]
        wide[: 2 * rows, :] = source[...].astype(jnp.float32)
        for j in range(2):
            part = wide[pl.ds(j, rows, stride=2), :]
            at = slice(j * width, (j + 1) * width)
            if plain is not None:
                plain[:, at] = part.astype(plain.dtype)
            turned[at, :] = part.T.astype(turned.dtype)
    multiply_all(groups, here, cot_t, activations, outs, held, sems)


def first_terms(here, groups, cotangent, param_shard, activations):
    tokens, rows = cotangent.shape[0], param_shard.shape[0]
    width = cotangent.shape[2]
    total = sum(count for _, _, count in groups)
    any_space = pl.BlockSpec(memory_space=pl.ANY)
    shapes = [(tokens, 2 * width), (2 * width, tokens), (2 * width, rows)]
    shapes += [(count, 2, 2 * width, rows) for _, _, count in groups]
    return pl.pallas_call(
        functools.partial(first_kernel, groups),
        out_shape=[jax.ShapeDtypeStruct(shape, jnp.bfloat16) for shape in shapes],
        in_specs=[pl.BlockSpec(memory_space=pltpu.SMEM), any_space, any_space, any_space],
        scratch_shapes=[
            pltpu.VMEM((total, tokens, 2 * rows), jnp.bfloat16),
            pltpu.SemaphoreType.DMA((total, 2)),
            pltpu.VMEM((2 * tokens, width), jnp.bfloat16),
            pltpu.VMEM((2 * rows, width), jnp.bfloat16),
            pltpu.SemaphoreType.DMA((2,)),
            pltpu.VMEM((2 * max(tokens, rows), width), jnp.float32),
        ],
        compiler_params=MOST,
        cost_estimate=pl.CostEstimate(
            flops=8 * total * width * tokens * rows,
            bytes_accessed=4 * total * rows * (tokens + 2 * width) + 12 * width * tokens,
            transcendentals=0,
        ),
    )(here, cotangent.reshape(2 * tokens, width), param_shard.reshape(2 * rows, width), activations)


def other_kernel(groups, here, cot, activations, up_one, down_one, *refs):
    outs, held, sems = refs[:-2], refs[-2], refs[-1]
    fetch_all(groups, here, activations, held, sems)
    multiply_all(groups, here, cot, activations, outs, held, sems, (up_one, down_one))


def other_terms(here, groups, cot_t, activations, up_one, down_one, rows):
    total = sum(count for _, _, count in groups)
    columns, tokens = cot_t.shape
    in_vmem = pl.BlockSpec(memory_space=pltpu.VMEM)
    return pl.pallas_call(
        functools.partial(other_kernel, groups),
        out_shape=[
            jax.ShapeDtypeStruct((4, 2, columns, rows), jnp.bfloat16) for _ in range(len(groups) // 2)
        ],
        in_specs=[
            pl.BlockSpec(memory_space=pltpu.SMEM),
            in_vmem,
            pl.BlockSpec(memory_space=pl.ANY),
            in_vmem,
            in_vmem,
        ],
        scratch_shapes=[
            pltpu.VMEM((total, tokens, 2 * rows), jnp.bfloat16),
            pltpu.SemaphoreType.DMA((total, 2)),
        ],
        compiler_params=MOST,
        cost_estimate=pl.CostEstimate(
            flops=4 * total * columns * tokens * rows,
            bytes_accessed=4 * total * rows * (tokens + columns) + 2 * columns * tokens,
            transcendentals=0,
        ),
    )(here, cot_t, activations, up_one, down_one)


def adam_kernel(mine, theirs, master_in, first_in, second_in, new_master, moments, layer):
    grad = (mine[...].astype(jnp.float32) + theirs[...].astype(jnp.float32)).T
    rows = grad.shape[0]
    width = grad.shape[1] // 2
    for j in range(2):
        at = pl.ds(j, rows, stride=2)
        weight_grad = grad[:, j * width : (j + 1) * width]
        master = master_in[at, :]
        first = beta_one * first_in[at, :] + (1.0 - beta_one) * weight_grad
        second = beta_two * second_in[at, :] + (1.0 - beta_two) * weight_grad * weight_grad
        first_hat = first / (1.0 - beta_one**step_number)
        second_hat = second / (1.0 - beta_two**step_number)
        new_master[at, :] = master - learn_rate * (
            first_hat / (jnp.sqrt(second_hat) + epsilon) + decay_rate * master
        )
        moments[0, j] = first.astype(jnp.bfloat16)
        moments[1, j] = second.astype(jnp.bfloat16)
    layer[...] = new_master[...].astype(jnp.bfloat16)


def adam(mine, theirs, master, first, second):
    rows, width = master.shape
    return pl.pallas_call(
        adam_kernel,
        out_shape=(
            jax.ShapeDtypeStruct((rows, width), jnp.float32),
            jax.ShapeDtypeStruct((2, 2, rows // 2, width), jnp.bfloat16),
            jax.ShapeDtypeStruct((rows, width), jnp.bfloat16),
        ),
        compiler_params=WIDE,
        cost_estimate=pl.CostEstimate(
            flops=20 * rows * width, bytes_accessed=30 * rows * width, transcendentals=2 * rows * width
        ),
    )(mine, theirs, master, first, second)


def place_kernel(groups, here, *refs):
    sources, out, sems = refs[: len(groups)], refs[-2], refs[-1]
    copies = []
    for source, (first, second) in zip(sources, groups):
        for i in range(source.shape[0]):
            for s in range(2):
                at = block_at(here, first, second + i, s, out.shape[0])
                copies.append(pltpu.make_async_copy(source.at[i, s], out.at[at], sems.at[len(copies)]))
    for copy in copies:
        copy.start()
    for copy in copies:
        copy.wait()


def place(here, groups, sources, total, into=None):
    block = sources[0].shape[2:]
    held = [] if into is None else [into]
    count = 2 * sum(source.shape[0] for source in sources)
    any_space = pl.BlockSpec(memory_space=pl.ANY)
    return pl.pallas_call(
        functools.partial(place_kernel, groups),
        out_shape=jax.ShapeDtypeStruct((total,) + block, sources[0].dtype),
        in_specs=[pl.BlockSpec(memory_space=pltpu.SMEM)]
        + [pl.BlockSpec(memory_space=pltpu.VMEM)] * len(sources)
        + [any_space] * len(held),
        out_specs=any_space,
        scratch_shapes=[pltpu.SemaphoreType.DMA((count,))],
        input_output_aliases={} if into is None else {1 + len(sources): 0},
        compiler_params=WIDE,
        cost_estimate=pl.CostEstimate(flops=0, bytes_accessed=0, transcendentals=0),
    )(here, *sources, *held)


def input_kernel(here, cot_mine, cot_theirs, params, out, total):
    step = pl.program_id(0)
    rows = params.shape[3]
    c = here[4]

    @pl.when(step == 0)
    def _():
        total[...] = jnp.zeros_like(total)

    for part in range(2):
        for s in range(2):
            at = slice((2 * part + s) * rows, (2 * part + s + 1) * rows)
            total[:, at] += jnp.dot(
                cot_mine[0], params[2 * c + part, s], preferred_element_type=jnp.float32
            ) + jnp.dot(cot_theirs[0], params[2 - 2 * c + part, s], preferred_element_type=jnp.float32)

    @pl.when(step == pl.num_programs(0) - 1)
    def _():
        out[...] = total[...].astype(out.dtype)


def input_matmul(here, cot_mine, cot_theirs, params):
    chips, tokens, columns = cot_mine.shape
    rows = params.shape[3]
    cot_spec = pl.BlockSpec((1, tokens, columns), lambda k, here: (k, 0, 0))
    return pl.pallas_call(
        input_kernel,
        out_shape=jax.ShapeDtypeStruct((tokens, 4 * rows), jnp.bfloat16),
        grid_spec=pltpu.PrefetchScalarGridSpec(
            num_scalar_prefetch=1,
            grid=(chips,),
            in_specs=[
                cot_spec,
                cot_spec,
                pl.BlockSpec((4, 2, columns, rows), lambda k, here: ((here[3] + 4 - k) % 4, 0, 0, 0)),
            ],
            out_specs=pl.BlockSpec((tokens, 4 * rows), lambda k, here: (0, 0)),
            scratch_shapes=[pltpu.VMEM((tokens, 4 * rows), jnp.float32)],
        ),
        compiler_params=MOST,
        cost_estimate=pl.CostEstimate(flops=0, bytes_accessed=0, transcendentals=0),
    )(here, cot_mine, cot_theirs, params)


def add(*terms):
    total = terms[0].astype(jnp.float32)
    for term in terms[1:]:
        total = total + term.astype(jnp.float32)
    return total.astype(jnp.bfloat16)


def tie(*values):
    return lax.optimization_barrier(values)


def per_device(activations, cotangent, param_shard, master_store, first_store, second_store):
    x, y, h, l, c = (lax.axis_index(a) for a in AXES)
    tokens, _, width = cotangent.shape
    rows = param_shard.shape[0]
    columns = 2 * width
    here = jnp.stack([x, y, h, l, c]).astype(jnp.int32)

    flat_cot, cot_t, par, up, down = first_terms(
        here, ((2, 0, 2), (2, 2, 2)), cotangent, param_shard, activations
    )
    up_one, down_one = move(up, along_first(1)), move(down, along_first(-1))
    par_same, par_other = move(par, to_user), move(par, to_user_across)
    cots = [flat_cot, move(flat_cot, next_in_line)]
    up, down, own = other_terms(
        here,
        ((1, 0, 2), (1, 2, 2), (3, 0, 2), (3, 2, 2), (0, 0, 2), (0, 2, 2)),
        cot_t,
        activations,
        up_one,
        down_one,
        rows,
    )
    up, down, par_same, par_other, cots[1] = tie(up, down, par_same, par_other, cots[1])
    up_two, down_two = move(up, along_first(1)), move(down, along_first(-1))
    pair = jnp.where(h == 0, jnp.stack([par_same, par_other]), jnp.stack([par_other, par_same]))
    params = lax.all_gather(pair, ("x", "y"), axis=0)
    cots += [move(cots[1], next_in_line), move(flat_cot, back_in_line)]
    sums = [add(own[i], up_two[i], down_two[i]) for i in range(4)]

    sums[1], sums[2], sums[3], cots[2], cots[3] = tie(*sums[1:], cots[2], cots[3])
    cot_mine = jnp.stack(cots)
    cot_theirs = move(cot_mine, other_core)
    got = [
        move(sums[1], along_second(1)),
        move(sums[3], along_second(-1)),
        move(sums[2], along_second(2)),
    ]
    far = add(sums[0][1], *(g[1] for g in got))
    near = add(sums[0][0], *(g[0] for g in got))
    far, cot_theirs = tie(far, cot_theirs)
    state = [v.reshape(2 * rows, width) for v in (master_store, first_store, second_store)]
    new_master, moments, layer = adam(near, move(far, other_half), *state)

    layer_other = move(layer, other_half)
    layer_other, moments = tie(layer_other, moments)
    moments = move(moments, previous_block)
    pair = jnp.where(h == 0, jnp.stack([layer, layer_other]), jnp.stack([layer_other, layer]))
    from_up = move(pair, along_second(-1))
    from_down = move(pair, along_second(1))
    from_far = move(pair, along_second(2))
    four = jnp.stack([pair, from_up, from_far, from_down])
    four, new_master = tie(four, new_master)
    four_down, four_up = move(four, along_first(1)), move(four, along_first(-1))
    new_master = move(new_master, previous_block)
    low, high, new_master = tie(four_down[:2], four_up[2:], new_master)
    low_far, high_far = move(low, along_first(1)), move(high, along_first(-1))
    input_grad = input_matmul(here, cot_mine, cot_theirs, params)
    new_layer = place(here, ((0, 0), (1, 0), (-1, 0)), [four, four_up, four_down], 32)
    new_layer, input_grad = tie(new_layer, input_grad)
    new_layer = place(here, ((2, 0), (2, 2)), [low_far, high_far], 32, new_layer)

    shape = (rows, 2, width)
    moments = moments.astype(jnp.float32).transpose(0, 2, 1, 3)
    return (
        input_grad,
        new_master.reshape(shape),
        moments[0],
        moments[1],
        new_layer.reshape(32 * rows, 2, width),
    )


def solution(mesh):
    fine = Mesh(mesh.devices.reshape(tuple(SIZES.values())), AXES)
    return jax.shard_map(
        per_device,
        mesh=fine,
        in_specs=(
            P(DP, None),
            P(DP, None, MP),
            P(DP, None, MP),
            P(DP, None, MP),
            P(DP, None, MP),
            P(DP, None, MP),
        ),
        out_specs=(
            P(DP, MP),
            P(DP, None, MP),
            P(DP, None, MP),
            P(DP, None, MP),
            P(None, None, MP),
        ),
        check_vma=False,
    )
```

time: 711 us -> 162 us (0.23)
  waiting for transfers between devices: 638 us -> 53.1 us
  starting transfers between devices: 17.4 us -> 61.9 us
  Pallas kernels: 0 us -> 23.7 us
  matrix products: 18.1 us -> 0 us
  local copies, waits for them, and re-layouts: 14.4 us -> 5.89 us
    reduce_scatter x2 -> x0, waiting for transfers between devices: 389 us -> none  [the longest x1 232 us: per_device(): lax.psum_scatter(jnp.einsum('td,tjc->djc', activations, cotangent, prefer...]
    all_gather x2 -> x1, waiting for transfers between devices: 209 us -> 0.02 us  [per_device(): params = lax.all_gather(pair, ('x', 'y'), axis=0)]
    ppermute x3 -> x24, starting transfers between devices: 17.3 us -> 61.8 us  [move(): return lax.ppermute(value, AXES, pairs)]
    pallas_call x0 -> x6, Pallas kernels: none -> 23.7 us  [the longest x1 7.79 us: other_terms(): pl.pallas_call(functools.partial(other_kernel, groups), out_shape=[jax.Sh...]
    dot_general x2 -> x0, matrix products: 18.1 us -> none  [the longest x1 10.3 us: per_device(): jnp.einsum('tjc,rjc->tr', cotangent, lax.all_gather(param_shard, 'dp', ax...]
    ppermute x3 -> x24, waiting for transfers between devices: 39.6 us -> 53.1 us  [move(): return lax.ppermute(value, AXES, pairs)]
    unnamed x18 -> x23, local copies, waits for them, and re-layouts: 14.4 us -> 3.52 us
  transfers between devices with their start and end apart: 7 -> 25, of which waited for: 7 -> 13; matrix products, arithmetic and copies ran while one was open for 4% -> 3% of each run, Pallas kernels for 0% -> 11%
where the time goes in v1:
time: 162 us
  starting transfers between devices  61.9 us (38%)
  waiting for transfers between devices  53.1 us (33%)
  Pallas kernels  23.7 us (15%)
  between operations  14.3 us (9%)
  local copies, waits for them, and re-layouts  5.89 us (4%)
  other arithmetic  2.84 us (2%)
    ppermute x24, starting transfers between devices, move(): return lax.ppermute(value, AXES, pairs)  61.8 us
    ppermute x24, waiting for transfers between devices, move(): return lax.ppermute(value, AXES, pairs)  53.1 us
    pallas_call x1, Pallas kernels, other_terms(): pl.pallas_call(functools.partial(other_kernel, groups), out_shape=[jax.Sh...  7.79 us
    pallas_call x1, Pallas kernels, input_matmul(): pl.pallas_call(input_kernel, out_shape=jax.ShapeDtypeStruct((tokens, 4 *...  7 us
    pallas_call x1, Pallas kernels, first_terms(): pl.pallas_call(functools.partial(first_kernel, groups), out_shape=[jax.Sh...  4.59 us
    pallas_call x2, Pallas kernels, place(): pl.pallas_call(functools.partial(place_kernel, groups), out_shape=jax.Sha...  4 us
    unnamed x23, local copies, waits for them, and re-layouts  3.52 us
  transfers between devices with their start and end apart: 25, of which 13 were waited for; matrix products, arithmetic and copies ran while one was open for 3% of the time, Pallas kernels for 11%

profile of v1, /device:TPU:32, one launch (start us, length us, event | category | flops | bytes accessed | tf_op | source)
XLA Modules:
  0.0 161.7 jit_solution(16234634925614111347)
XLA Ops:
  7.2 0.0 all-gather.2.cloned.1.call-start
  7.2 0.7 stack.87.here
  7.9 4.6 %shard_map.101 = (bf16[512,256]{1,0:T(8,128)(2,1)}, bf16[256,512]{1,0:T(8,128)(2,1)}, bf16[256,256]{1,0:T(8,128)(2,1)}, bf16[2,2,256,256]{3,2,1,0:T(8,128)(2,1)}, bf16[2,2,256,256]{3,2,1,0:T(8,128)(2,1)}) custom-call(s32[5]{0:T(128)} %stack.87.here, bf16[1024,128]{1,0:T(8,128)(2,1)} %bitcast.59, bf16[512,128]{1,0:T(8,128)(2,1)} %bitcast.68, ...), custom_call_target="tpu_custom_call" | custom-call | flops 536870912 | bytes 3932160 | tf_op jit(solution)/shard_map/pallas_call | solution.py:161
  12.5 1.6 collective-permute-start
  14.0 1.7 %collective-permute-start.1 = (bf16[2,2,256,256]{3,2,1,0:T(8,128)(2,1)}, bf16[2,2,256,256]{3,2,1,0:T(8,128)(2,1)S(1)}, u32[]{:S(2)}, u32[]{:S(2)}) collective-permute-start(bf16[2,2,256,256]{3,2,1,0:T(8,128)(2,1)} %get-tuple-element.39), channel_id=1, source_target_pairs={{0,192},{1,49},{2,194},{3,51},{4,196},{5,53},{6,198},{7,55},{8,200... | collective-permute-start | bytes 1572872 | tf_op jit(solution)/shard_map/ppermute | solution.py:33
  15.8 1.9 %collective-permute-start.4 = (bf16[512,256]{1,0:T(8,128)(2,1)}, bf16[512,256]{1,0:T(8,128)(2,1)S(1)}, u32[]{:S(2)}, u32[]{:S(2)}) collective-permute-start(bf16[512,256]{1,0:T(8,128)(2,1)} %get-tuple-element.44), channel_id=1, source_target_pairs={{0,2},{1,3},{2,4},{3,5},{4,6},{5,7},{6,0},{7,1},{8,10},{9,11},{10,... | collective-permute-start | bytes 786440 | tf_op jit(solution)/shard_map/ppermute | solution.py:33
  17.7 4.7 %collective-permute-start.3 = (bf16[256,256]{1,0:T(8,128)(2,1)}, bf16[256,256]{1,0:T(8,128)(2,1)S(1)}, u32[]{:S(2)}, u32[]{:S(2)}) collective-permute-start(bf16[256,256]{1,0:T(8,128)(2,1)} %get-tuple-element.43), channel_id=1, source_target_pairs={{0,8},{1,40},{2,72},{3,104},{4,136},{5,168},{6,200},{7,232},{8,0},... | collective-permute-start | bytes 393224 | tf_op jit(solution)/shard_map/ppermute | solution.py:33
  22.4 4.1 %collective-permute-start.2 = (bf16[256,256]{1,0:T(8,128)(2,1)}, bf16[256,256]{1,0:T(8,128)(2,1)S(1)}, u32[]{:S(2)}, u32[]{:S(2)}) collective-permute-start(bf16[256,256]{1,0:T(8,128)(2,1)} %get-tuple-element.43), channel_id=1, source_target_pairs={{0,0},{1,32},{2,64},{3,96},{4,128},{5,160},{6,192},{7,224},{8,8},{... | collective-permute-start | bytes 393224 | tf_op jit(solution)/shard_map/ppermute | solution.py:33
  26.5 0.8 copy-done.7
  27.3 0.2 copy-done.8
  27.5 7.8 %shard_map.102 = (bf16[4,2,256,256]{3,2,1,0:T(8,128)(2,1)}, bf16[4,2,256,256]{3,2,1,0:T(8,128)(2,1)}, bf16[4,2,256,256]{3,2,1,0:T(8,128)(2,1)}) custom-call(s32[5]{0:T(128)} %stack.87.here, bf16[256,512]{1,0:T(8,128)(2,1)} %get-tuple-element.37.cot, bf16[512,8192]{1,0:T(8,128)(2,1)} %activations.3, bf16[2,2,256,256]{3,2,1,0:T(8,128)(2,1)} %copy-done.7, ...), custom_call_target="tpu_custom_call" | custom-call | flops 1610612736 | bytes 9699328 | tf_op jit(solution)/shard_map/pallas_call | solution.py:192
  35.3 0.0 collective-permute-done.3
  35.3 1.7 %collective-permute-done.2 = bf16[256,256]{1,0:T(8,128)(2,1)S(1)} collective-permute-done((bf16[256,256]{1,0:T(8,128)(2,1)}, bf16[256,256]{1,0:T(8,128)(2,1)S(1)}, u32[]{:S(2)}, u32[]{:S(2)}) %collective-permute-start.2) | collective-permute-done | bytes 131104 | tf_op jit(solution)/shard_map/ppermute | solution.py:33
  36.9 0.0 collective-permute-done.4
  37.0 0.7 maximum_select_fusion.2
  37.7 0.0 all-gather.2.cloned.1.call-update
  37.7 0.1 collective-permute-start.5
  37.8 3.2 %collective-permute-start.6 = (bf16[4,2,256,256]{3,2,1,0:T(8,128)(2,1)}, bf16[4,2,256,256]{3,2,1,0:T(8,128)(2,1)S(1)}, u32[]{:S(2)}, u32[]{:S(2)}) collective-permute-start(bf16[4,2,256,256]{3,2,1,0:T(8,128)(2,1)} %get-tuple-element.46), channel_id=1, source_target_pairs={{0,192},{1,49},{2,194},{3,51},{4,196},{5,53},{6,198},{7,55},{8,200... | collective-permute-start | bytes 3145736 | tf_op jit(solution)/shard_map/ppermute | solution.py:33
  41.0 1.0 collective-permute-start.8
  42.0 2.2 %collective-permute-start.7 = (bf16[512,256]{1,0:T(8,128)(2,1)S(1)}, bf16[512,256]{1,0:T(8,128)(2,1)S(1)}, u32[]{:S(2)}, u32[]{:S(2)}) collective-permute-start(bf16[512,256]{1,0:T(8,128)(2,1)S(1)} %collective-permute-done.4), channel_id=1, source_target_pairs={{0,2},{1,3},{2,4},{3,5},{4,6},{5,7},{6,0},{7,1},{8,10},{9,11},{10,... | collective-permute-start | bytes 786440 | tf_op jit(solution)/shard_map/ppermute | solution.py:33
  44.2 9.8 %collective-permute-done.5 = bf16[4,2,256,256]{3,2,1,0:T(8,128)(2,1)S(1)} collective-permute-done((bf16[4,2,256,256]{3,2,1,0:T(8,128)(2,1)}, bf16[4,2,256,256]{3,2,1,0:T(8,128)(2,1)S(1)}, u32[]{:S(2)}, u32[]{:S(2)}) %collective-permute-start.5) | collective-permute-done | bytes 1048608 | tf_op jit(solution)/shard_map/ppermute | solution.py:33
  54.0 0.0 collective-permute-done.6
  54.0 1.6 add_convert_fusion.3
  55.6 0.0 collective-permute-done.8
  55.6 1.4 collective-permute-done.7
  57.0 0.1 pad_maximum_fusion.cot_mine
  57.1 0.1 collective-permute-start.12
  57.2 0.1 collective-permute-start.9
  57.3 4.2 %collective-permute-start.10 = (bf16[2,256,256]{2,1,0:T(8,128)(2,1)S(1)}, bf16[2,256,256]{2,1,0:T(8,128)(2,1)S(1)}, u32[]{:S(2)}, u32[]{:S(2)}) collective-permute-start(bf16[2,256,256]{2,1,0:T(8,128)(2,1)S(1)} %get-tuple-element.49), channel_id=1, source_target_pairs={{0,48},{1,193},{2,50},{3,195},{4,52},{5,197},{6,54},{7,199},{8,56}... | collective-permute-start | bytes 786440 | tf_op jit(solution)/shard_map/ppermute | solution.py:33
  61.5 2.0 %collective-permute-start.11 = (bf16[2,256,256]{2,1,0:T(8,128)(2,1)S(1)}, bf16[2,256,256]{2,1,0:T(8,128)(2,1)S(1)}, u32[]{:S(2)}, u32[]{:S(2)}) collective-permute-start(bf16[2,256,256]{2,1,0:T(8,128)(2,1)S(1)} %get-tuple-element.50), channel_id=1, source_target_pairs={{0,32},{1,129},{2,34},{3,131},{4,36},{5,133},{6,38},{7,135},{8,40}... | collective-permute-start | bytes 786440 | tf_op jit(solution)/shard_map/ppermute | solution.py:33
  63.6 2.9 %collective-permute-done.9 = bf16[2,256,256]{2,1,0:T(8,128)(2,1)S(1)} collective-permute-done((bf16[2,256,256]{2,1,0:T(8,128)(2,1)S(1)}, bf16[2,256,256]{2,1,0:T(8,128)(2,1)S(1)}, u32[]{:S(2)}, u32[]{:S(2)}) %collective-permute-start.9) | collective-permute-done | bytes 262176 | tf_op jit(solution)/shard_map/ppermute | solution.py:33
  66.4 1.0 collective-permute-done.10
  67.4 5.4 %collective-permute-done.11 = bf16[2,256,256]{2,1,0:T(8,128)(2,1)S(1)} collective-permute-done((bf16[2,256,256]{2,1,0:T(8,128)(2,1)S(1)}, bf16[2,256,256]{2,1,0:T(8,128)(2,1)S(1)}, u32[]{:S(2)}, u32[]{:S(2)}) %collective-permute-start.11) | collective-permute-done | bytes 262176 | tf_op jit(solution)/shard_map/ppermute | solution.py:33
  72.9 0.1 fusion.10
  73.0 10.0 %collective-permute-start.13 = (bf16[256,256]{1,0:T(8,128)(2,1)S(1)}, bf16[256,256]{1,0:T(8,128)(2,1)S(1)}, u32[]{:S(2)}, u32[]{:S(2)}) collective-permute-start(bf16[256,256]{1,0:T(8,128)(2,1)S(1)} %get-tuple-element.53), channel_id=1, source_target_pairs={{0,8},{1,9},{2,10},{3,11},{4,12},{5,13},{6,14},{7,15},{8,0},{9,1},... | collective-permute-start | bytes 393224 | tf_op jit(solution)/shard_map/ppermute | solution.py:33
  83.0 4.8 %collective-permute-done.13.theirs = bf16[256,256]{1,0:T(8,128)(2,1)S(1)} collective-permute-done((bf16[256,256]{1,0:T(8,128)(2,1)S(1)}, bf16[256,256]{1,0:T(8,128)(2,1)S(1)}, u32[]{:S(2)}, u32[]{:S(2)}) %collective-permute-start.13) | collective-permute-done | bytes 131104 | tf_op jit(solution)/shard_map/ppermute | solution.py:33
  87.9 0.3 shard_map.103
  88.2 4.5 %collective-permute-start.14 = (bf16[512,128]{1,0:T(8,128)(2,1)S(1)}, bf16[512,128]{1,0:T(8,128)(2,1)S(1)}, u32[]{:S(2)}, u32[]{:S(2)}) collective-permute-start(bf16[512,128]{1,0:T(8,128)(2,1)S(1)} %get-tuple-element.54), channel_id=1, source_target_pairs={{0,8},{1,9},{2,10},{3,11},{4,12},{5,13},{6,14},{7,15},{8,0},{9,1},... | collective-permute-start | bytes 393224 | tf_op jit(solution)/shard_map/ppermute | solution.py:33
  92.7 4.5 %collective-permute-done.14 = bf16[512,128]{1,0:T(8,128)(2,1)S(1)} collective-permute-done((bf16[512,128]{1,0:T(8,128)(2,1)S(1)}, bf16[512,128]{1,0:T(8,128)(2,1)S(1)}, u32[]{:S(2)}, u32[]{:S(2)}) %collective-permute-start.14) | collective-permute-done | bytes 131104 | tf_op jit(solution)/shard_map/ppermute | solution.py:33
  97.2 1.4 collective-permute-start.17
  98.6 3.2 %collective-permute-start.16 = (bf16[2,512,128]{2,1,0:T(8,128)(2,1)S(1)}, bf16[2,512,128]{2,1,0:T(8,128)(2,1)S(1)}, u32[]{:S(2)}, u32[]{:S(2)}) collective-permute-start(bf16[2,512,128]{2,1,0:T(8,128)(2,1)S(1)} %maximum_select_fusion.1), channel_id=1, source_target_pairs={{0,32},{1,129},{2,34},{3,131},{4,36},{5,133},{6,38},{7,135},{8,40}... | collective-permute-start | bytes 786440 | tf_op jit(solution)/shard_map/ppermute | solution.py:33
  101.9 4.2 %collective-permute-done.17 = bf16[2,512,128]{2,1,0:T(8,128)(2,1)S(1)} collective-permute-done((bf16[2,512,128]{2,1,0:T(8,128)(2,1)S(1)}, bf16[2,512,128]{2,1,0:T(8,128)(2,1)S(1)}, u32[]{:S(2)}, u32[]{:S(2)}) %collective-permute-start.17) | collective-permute-done | bytes 262176 | tf_op jit(solution)/shard_map/ppermute | solution.py:33
  106.1 3.1 %collective-permute-done.16 = bf16[2,512,128]{2,1,0:T(8,128)(2,1)S(1)} collective-permute-done((bf16[2,512,128]{2,1,0:T(8,128)(2,1)S(1)}, bf16[2,512,128]{2,1,0:T(8,128)(2,1)S(1)}, u32[]{:S(2)}, u32[]{:S(2)}) %collective-permute-start.16) | collective-permute-done | bytes 262176 | tf_op jit(solution)/shard_map/ppermute | solution.py:33
  109.2 0.1 pad_maximum_fusion.1.refs_0_
  109.3 1.5 collective-permute-start.19
  110.9 1.8 %collective-permute-start.18 = (bf16[4,2,512,128]{3,2,1,0:T(8,128)(2,1)S(1)}, bf16[4,2,512,128]{3,2,1,0:T(8,128)(2,1)S(1)}, u32[]{:S(2)}, u32[]{:S(2)}) collective-permute-start(bf16[4,2,512,128]{3,2,1,0:T(8,128)(2,1)S(1)} %pad_maximum_fusion.1.refs_0_), channel_id=1, source_target_pairs={{0,192},{1,49},{2,194},{3,51},{4,196},{5,53},{6,198},{7,55},{8,200... | collective-permute-start | bytes 3145736 | tf_op jit(solution)/shard_map/ppermute | solution.py:33
  112.6 9.3 %collective-permute-start.20 = (f32[512,128]{1,0:T(8,128)S(1)}, f32[512,128]{1,0:T(8,128)S(1)}, u32[]{:S(2)}, u32[]{:S(2)}) collective-permute-start(f32[512,128]{1,0:T(8,128)S(1)} %get-tuple-element.63), channel_id=1, source_target_pairs={{0,248},{1,249},{2,250},{3,251},{4,252},{5,253},{6,254},{7,255},{8... | collective-permute-start | bytes 786440 | tf_op jit(solution)/shard_map/ppermute | solution.py:33
  121.9 0.0 collective-permute-start.21
  122.0 3.4 %collective-permute-done.19.refs_2_ = bf16[4,2,512,128]{3,2,1,0:T(8,128)(2,1)S(1)} collective-permute-done((bf16[4,2,512,128]{3,2,1,0:T(8,128)(2,1)S(1)}, bf16[4,2,512,128]{3,2,1,0:T(8,128)(2,1)S(1)}, u32[]{:S(2)}, u32[]{:S(2)}) %collective-permute-start.19) | collective-permute-done | bytes 1048608 | tf_op jit(solution)/shard_map/ppermute | solution.py:33
  125.4 0.8 slice.120
  126.2 0.0 collective-permute-done.18.refs_1_
  126.2 0.8 slice.121
  127.1 8.9 %collective-permute-done.20 = f32[512,128]{1,0:T(8,128)S(1)} collective-permute-done((f32[512,128]{1,0:T(8,128)S(1)}, f32[512,128]{1,0:T(8,128)S(1)}, u32[]{:S(2)}, u32[]{:S(2)}) %collective-permute-start.20) | collective-permute-done | bytes 262176 | tf_op jit(solution)/shard_map/ppermute | solution.py:33
  135.9 1.3 collective-permute-start.22
  137.3 1.9 %collective-permute-start.23 = (bf16[2,2,512,128]{3,2,1,0:T(8,128)(2,1)}, bf16[2,2,512,128]{3,2,1,0:T(8,128)(2,1)S(1)}, u32[]{:S(2)}, u32[]{:S(2)}) collective-permute-start(bf16[2,2,512,128]{3,2,1,0:T(8,128)(2,1)} %slice.121), channel_id=1, source_target_pairs={{0,192},{1,49},{2,194},{3,51},{4,196},{5,53},{6,198},{7,55},{8,200... | collective-permute-start | bytes 1572872 | tf_op jit(solution)/shard_map/ppermute | solution.py:33
  139.2 2.0 %collective-permute-done.21 = bf16[2,2,256,128]{3,2,1,0:T(8,128)(2,1)S(1)} collective-permute-done((bf16[2,2,256,128]{3,2,1,0:T(8,128)(2,1)S(1)}, bf16[2,2,256,128]{3,2,1,0:T(8,128)(2,1)S(1)}, u32[]{:S(2)}, u32[]{:S(2)}) %collective-permute-start.21) | collective-permute-done | bytes 262176 | tf_op jit(solution)/shard_map/ppermute | solution.py:33
  141.3 0.9 copy.15
  142.2 0.9 copy.14
  143.1 2.4 %shard_map.104.refs_2_ = bf16[32,512,128]{2,1,0:T(8,128)(2,1)} custom-call(s32[5]{0:T(128)S(1)} %copy-done.3, bf16[4,2,512,128]{3,2,1,0:T(8,128)(2,1)S(1)} %pad_maximum_fusion.1.refs_0_, bf16[4,2,512,128]{3,2,1,0:T(8,128)(2,1)S(1)} %collective-permute-done.18.refs_1_, bf16[4,2,512,128]{3,2,1,0:T(8,128)(2,1)S(1)} %collective-permute-done.19.refs_2_), custom_call_target="tpu_custom_call" | custom-call | tf_op jit(solution)/shard_map/pallas_call | solution.py:272
  145.5 0.0 all-gather.2.cloned.1.call-done.params
  145.5 7.0 %shard_map.105 = bf16[512,1024]{1,0:T(8,128)(2,1)} custom-call(s32[5]{0:T(128)} %stack.87.here, bf16[4,512,256]{2,1,0:T(8,128)(2,1)} %copy-done.5, bf16[4,512,256]{2,1,0:T(8,128)(2,1)} %copy-done.6, bf16[16,2,256,256]{3,2,1,0:T(8,128)(2,1)} %all-gather.2.cloned.1.call-done.params), custom_call_target="tpu_custom_call" | custom-call | tf_op jit(solution)/shard_map/pallas_call | solution.py:311
  152.5 0.0 collective-permute-done.22.refs_0_
  152.6 1.6 shard_map.106
  154.2 0.7 copy.18
  (28 shorter events, 0.2 us)
Async XLA Ops:
  7.2 138.4 %all-gather.2.cloned.1.call-start = ((), (), s32[]{:S(2)}) async-start(), calls=%async_computation | async-start | bytes 4456448 | tf_op jit(solution)/shard_map/all_gather | solution.py:366
  12.5 14.0 %collective-permute-start = (bf16[2,2,256,256]{3,2,1,0:T(8,128)(2,1)}, bf16[2,2,256,256]{3,2,1,0:T(8,128)(2,1)S(1)}, u32[]{:S(2)}, u32[]{:S(2)}) collective-permute-start(bf16[2,2,256,256]{3,2,1,0:T(8,128)(2,1)} %get-tuple-element.38), channel_id=1, source_target_pairs={{0,64},{1,17},{2,66},{3,19},{4,68},{5,21},{6,70},{7,23},{8,72},{9,... | collective-permute-start | bytes 1572872 | tf_op jit(solution)/shard_map/ppermute | solution.py:33
  14.0 12.4 %collective-permute-start.1 = (bf16[2,2,256,256]{3,2,1,0:T(8,128)(2,1)}, bf16[2,2,256,256]{3,2,1,0:T(8,128)(2,1)S(1)}, u32[]{:S(2)}, u32[]{:S(2)}) collective-permute-start(bf16[2,2,256,256]{3,2,1,0:T(8,128)(2,1)} %get-tuple-element.39), channel_id=1, source_target_pairs={{0,192},{1,49},{2,194},{3,51},{4,196},{5,53},{6,198},{7,55},{8,200... | collective-permute-start | bytes 1572872 | tf_op jit(solution)/shard_map/ppermute | solution.py:33
  15.8 21.2 %collective-permute-start.4 = (bf16[512,256]{1,0:T(8,128)(2,1)}, bf16[512,256]{1,0:T(8,128)(2,1)S(1)}, u32[]{:S(2)}, u32[]{:S(2)}) collective-permute-start(bf16[512,256]{1,0:T(8,128)(2,1)} %get-tuple-element.44), channel_id=1, source_target_pairs={{0,2},{1,3},{2,4},{3,5},{4,6},{5,7},{6,0},{7,1},{8,10},{9,11},{10,... | collective-permute-start | bytes 786440 | tf_op jit(solution)/shard_map/ppermute | solution.py:33
  17.7 17.6 %collective-permute-start.3 = (bf16[256,256]{1,0:T(8,128)(2,1)}, bf16[256,256]{1,0:T(8,128)(2,1)S(1)}, u32[]{:S(2)}, u32[]{:S(2)}) collective-permute-start(bf16[256,256]{1,0:T(8,128)(2,1)} %get-tuple-element.43), channel_id=1, source_target_pairs={{0,8},{1,40},{2,72},{3,104},{4,136},{5,168},{6,200},{7,232},{8,0},... | collective-permute-start | bytes 393224 | tf_op jit(solution)/shard_map/ppermute | solution.py:33
  22.4 14.6 %collective-permute-start.2 = (bf16[256,256]{1,0:T(8,128)(2,1)}, bf16[256,256]{1,0:T(8,128)(2,1)S(1)}, u32[]{:S(2)}, u32[]{:S(2)}) collective-permute-start(bf16[256,256]{1,0:T(8,128)(2,1)} %get-tuple-element.43), channel_id=1, source_target_pairs={{0,0},{1,32},{2,64},{3,96},{4,128},{5,160},{6,192},{7,224},{8,8},{... | collective-permute-start | bytes 393224 | tf_op jit(solution)/shard_map/ppermute | solution.py:33
  26.5 0.8 copy-start.7
  26.5 1.0 copy-start.8
  27.5 13.5 %copy-start.9 = (bf16[512,256]{1,0:T(8,128)(2,1)S(1)}, bf16[512,256]{1,0:T(8,128)(2,1)}, u32[]{:S(2)}) copy-start(bf16[512,256]{1,0:T(8,128)(2,1)} %get-tuple-element.44) | copy-start | bytes 786436
  36.9 50.9 %copy-start = (f32[256,2,128]{2,1,0:T(2,128)S(1)}, f32[256,2,128]{2,1,0:T(2,128)}, u32[]{:S(2)}) copy-start(f32[256,2,128]{2,1,0:T(2,128)} %param.9) | copy-start | bytes 786436
  37.0 50.9 %copy-start.1 = (f32[256,2,128]{2,1,0:T(2,128)S(1)}, f32[256,2,128]{2,1,0:T(2,128)}, u32[]{:S(2)}) copy-start(f32[256,2,128]{2,1,0:T(2,128)} %param.10) | copy-start | bytes 786436
  37.0 50.9 %copy-start.2 = (f32[256,2,128]{2,1,0:T(2,128)S(1)}, f32[256,2,128]{2,1,0:T(2,128)}, u32[]{:S(2)}) copy-start(f32[256,2,128]{2,1,0:T(2,128)} %param.11) | copy-start | bytes 786436
  37.7 16.3 %collective-permute-start.5 = (bf16[4,2,256,256]{3,2,1,0:T(8,128)(2,1)}, bf16[4,2,256,256]{3,2,1,0:T(8,128)(2,1)S(1)}, u32[]{:S(2)}, u32[]{:S(2)}) collective-permute-start(bf16[4,2,256,256]{3,2,1,0:T(8,128)(2,1)} %get-tuple-element.45), channel_id=1, source_target_pairs={{0,64},{1,17},{2,66},{3,19},{4,68},{5,21},{6,70},{7,23},{8,72},{9,... | collective-permute-start | bytes 3145736 | tf_op jit(solution)/shard_map/ppermute | solution.py:33
  37.8 16.2 %collective-permute-start.6 = (bf16[4,2,256,256]{3,2,1,0:T(8,128)(2,1)}, bf16[4,2,256,256]{3,2,1,0:T(8,128)(2,1)S(1)}, u32[]{:S(2)}, u32[]{:S(2)}) collective-permute-start(bf16[4,2,256,256]{3,2,1,0:T(8,128)(2,1)} %get-tuple-element.46), channel_id=1, source_target_pairs={{0,192},{1,49},{2,194},{3,51},{4,196},{5,53},{6,198},{7,55},{8,200... | collective-permute-start | bytes 3145736 | tf_op jit(solution)/shard_map/ppermute | solution.py:33
  41.0 14.6 %collective-permute-start.8 = (bf16[512,256]{1,0:T(8,128)(2,1)S(1)}, bf16[512,256]{1,0:T(8,128)(2,1)S(1)}, u32[]{:S(2)}, u32[]{:S(2)}) collective-permute-start(bf16[512,256]{1,0:T(8,128)(2,1)S(1)} %copy-done.9), channel_id=1, source_target_pairs={{0,6},{1,7},{2,0},{3,1},{4,2},{5,3},{6,4},{7,5},{8,14},{9,15},{10,... | collective-permute-start | bytes 786440 | tf_op jit(solution)/shard_map/ppermute | solution.py:33
  42.0 15.0 %collective-permute-start.7 = (bf16[512,256]{1,0:T(8,128)(2,1)S(1)}, bf16[512,256]{1,0:T(8,128)(2,1)S(1)}, u32[]{:S(2)}, u32[]{:S(2)}) collective-permute-start(bf16[512,256]{1,0:T(8,128)(2,1)S(1)} %collective-permute-done.4), channel_id=1, source_target_pairs={{0,2},{1,3},{2,4},{3,5},{4,6},{5,7},{6,0},{7,1},{8,10},{9,11},{10,... | collective-permute-start | bytes 786440 | tf_op jit(solution)/shard_map/ppermute | solution.py:33
  57.1 84.1 %copy-start.5 = (bf16[4,512,256]{2,1,0:T(8,128)(2,1)}, bf16[4,512,256]{2,1,0:T(8,128)(2,1)S(1)}, u32[]{:S(2)}) copy-start(bf16[4,512,256]{2,1,0:T(8,128)(2,1)S(1)} %pad_maximum_fusion.cot_mine) | copy-start | bytes 3145732
  57.1 15.9 %collective-permute-start.12 = (bf16[4,512,256]{2,1,0:T(8,128)(2,1)S(1)}, bf16[4,512,256]{2,1,0:T(8,128)(2,1)S(1)}, u32[]{:S(2)}, u32[]{:S(2)}) collective-permute-start(bf16[4,512,256]{2,1,0:T(8,128)(2,1)S(1)} %pad_maximum_fusion.cot_mine), channel_id=1, source_target_pairs={{0,1},{1,0},{2,3},{3,2},{4,5},{5,4},{6,7},{7,6},{8,9},{9,8},{10,11... | collective-permute-start | bytes 3145736 | tf_op jit(solution)/shard_map/ppermute | solution.py:33
  57.2 9.2 %collective-permute-start.9 = (bf16[2,256,256]{2,1,0:T(8,128)(2,1)S(1)}, bf16[2,256,256]{2,1,0:T(8,128)(2,1)S(1)}, u32[]{:S(2)}, u32[]{:S(2)}) collective-permute-start(bf16[2,256,256]{2,1,0:T(8,128)(2,1)S(1)} %get-tuple-element.48), channel_id=1, source_target_pairs={{0,16},{1,65},{2,18},{3,67},{4,20},{5,69},{6,22},{7,71},{8,24},{9,... | collective-permute-start | bytes 786440 | tf_op jit(solution)/shard_map/ppermute | solution.py:33
  57.3 10.1 %collective-permute-start.10 = (bf16[2,256,256]{2,1,0:T(8,128)(2,1)S(1)}, bf16[2,256,256]{2,1,0:T(8,128)(2,1)S(1)}, u32[]{:S(2)}, u32[]{:S(2)}) collective-permute-start(bf16[2,256,256]{2,1,0:T(8,128)(2,1)S(1)} %get-tuple-element.49), channel_id=1, source_target_pairs={{0,48},{1,193},{2,50},{3,195},{4,52},{5,197},{6,54},{7,199},{8,56}... | collective-permute-start | bytes 786440 | tf_op jit(solution)/shard_map/ppermute | solution.py:33
  61.5 11.3 %collective-permute-start.11 = (bf16[2,256,256]{2,1,0:T(8,128)(2,1)S(1)}, bf16[2,256,256]{2,1,0:T(8,128)(2,1)S(1)}, u32[]{:S(2)}, u32[]{:S(2)}) collective-permute-start(bf16[2,256,256]{2,1,0:T(8,128)(2,1)S(1)} %get-tuple-element.50), channel_id=1, source_target_pairs={{0,32},{1,129},{2,34},{3,131},{4,36},{5,133},{6,38},{7,135},{8,40}... | collective-permute-start | bytes 786440 | tf_op jit(solution)/shard_map/ppermute | solution.py:33
  73.0 69.2 %copy-start.6 = (bf16[4,512,256]{2,1,0:T(8,128)(2,1)}, bf16[4,512,256]{2,1,0:T(8,128)(2,1)S(1)}, u32[]{:S(2)}) copy-start(bf16[4,512,256]{2,1,0:T(8,128)(2,1)S(1)} %collective-permute-done.12.cot_theirs) | copy-start | bytes 3145732
  73.0 14.8 %collective-permute-start.13 = (bf16[256,256]{1,0:T(8,128)(2,1)S(1)}, bf16[256,256]{1,0:T(8,128)(2,1)S(1)}, u32[]{:S(2)}, u32[]{:S(2)}) collective-permute-start(bf16[256,256]{1,0:T(8,128)(2,1)S(1)} %get-tuple-element.53), channel_id=1, source_target_pairs={{0,8},{1,9},{2,10},{3,11},{4,12},{5,13},{6,14},{7,15},{8,0},{9,1},... | collective-permute-start | bytes 393224 | tf_op jit(solution)/shard_map/ppermute | solution.py:33
  88.2 54.9 %copy-start.3 = (s32[5]{0:T(128)S(1)}, s32[5]{0:T(128)}, u32[]{:S(2)}) copy-start(s32[5]{0:T(128)} %stack.87.here) | copy-start | bytes 64
  88.2 9.0 %collective-permute-start.14 = (bf16[512,128]{1,0:T(8,128)(2,1)S(1)}, bf16[512,128]{1,0:T(8,128)(2,1)S(1)}, u32[]{:S(2)}, u32[]{:S(2)}) collective-permute-start(bf16[512,128]{1,0:T(8,128)(2,1)S(1)} %get-tuple-element.54), channel_id=1, source_target_pairs={{0,8},{1,9},{2,10},{3,11},{4,12},{5,13},{6,14},{7,15},{8,0},{9,1},... | collective-permute-start | bytes 393224 | tf_op jit(solution)/shard_map/ppermute | solution.py:33
  97.2 8.9 %collective-permute-start.17 = (bf16[2,512,128]{2,1,0:T(8,128)(2,1)S(1)}, bf16[2,512,128]{2,1,0:T(8,128)(2,1)S(1)}, u32[]{:S(2)}, u32[]{:S(2)}) collective-permute-start(bf16[2,512,128]{2,1,0:T(8,128)(2,1)S(1)} %maximum_select_fusion.1), channel_id=1, source_target_pairs={{0,16},{1,65},{2,18},{3,67},{4,20},{5,69},{6,22},{7,71},{8,24},{9,... | collective-permute-start | bytes 786440 | tf_op jit(solution)/shard_map/ppermute | solution.py:33
  98.6 10.6 %collective-permute-start.16 = (bf16[2,512,128]{2,1,0:T(8,128)(2,1)S(1)}, bf16[2,512,128]{2,1,0:T(8,128)(2,1)S(1)}, u32[]{:S(2)}, u32[]{:S(2)}) collective-permute-start(bf16[2,512,128]{2,1,0:T(8,128)(2,1)S(1)} %maximum_select_fusion.1), channel_id=1, source_target_pairs={{0,32},{1,129},{2,34},{3,131},{4,36},{5,133},{6,38},{7,135},{8,40}... | collective-permute-start | bytes 786440 | tf_op jit(solution)/shard_map/ppermute | solution.py:33
  101.8 7.4 %collective-permute-start.15 = (bf16[2,512,128]{2,1,0:T(8,128)(2,1)S(1)}, bf16[2,512,128]{2,1,0:T(8,128)(2,1)S(1)}, u32[]{:S(2)}, u32[]{:S(2)}) collective-permute-start(bf16[2,512,128]{2,1,0:T(8,128)(2,1)S(1)} %maximum_select_fusion.1), channel_id=1, source_target_pairs={{0,48},{1,193},{2,50},{3,195},{4,52},{5,197},{6,54},{7,199},{8,56}... | collective-permute-start | bytes 786440 | tf_op jit(solution)/shard_map/ppermute | solution.py:33
  109.3 16.1 %collective-permute-start.19 = (bf16[4,2,512,128]{3,2,1,0:T(8,128)(2,1)S(1)}, bf16[4,2,512,128]{3,2,1,0:T(8,128)(2,1)S(1)}, u32[]{:S(2)}, u32[]{:S(2)}) collective-permute-start(bf16[4,2,512,128]{3,2,1,0:T(8,128)(2,1)S(1)} %pad_maximum_fusion.1.refs_0_), channel_id=1, source_target_pairs={{0,64},{1,17},{2,66},{3,19},{4,68},{5,21},{6,70},{7,23},{8,72},{9,... | collective-permute-start | bytes 3145736 | tf_op jit(solution)/shard_map/ppermute | solution.py:33
  110.9 15.4 %collective-permute-start.18 = (bf16[4,2,512,128]{3,2,1,0:T(8,128)(2,1)S(1)}, bf16[4,2,512,128]{3,2,1,0:T(8,128)(2,1)S(1)}, u32[]{:S(2)}, u32[]{:S(2)}) collective-permute-start(bf16[4,2,512,128]{3,2,1,0:T(8,128)(2,1)S(1)} %pad_maximum_fusion.1.refs_0_), channel_id=1, source_target_pairs={{0,192},{1,49},{2,194},{3,51},{4,196},{5,53},{6,198},{7,55},{8,200... | collective-permute-start | bytes 3145736 | tf_op jit(solution)/shard_map/ppermute | solution.py:33
  112.6 23.3 %collective-permute-start.20 = (f32[512,128]{1,0:T(8,128)S(1)}, f32[512,128]{1,0:T(8,128)S(1)}, u32[]{:S(2)}, u32[]{:S(2)}) collective-permute-start(f32[512,128]{1,0:T(8,128)S(1)} %get-tuple-element.63), channel_id=1, source_target_pairs={{0,248},{1,249},{2,250},{3,251},{4,252},{5,253},{6,254},{7,255},{8... | collective-permute-start | bytes 786440 | tf_op jit(solution)/shard_map/ppermute | solution.py:33
  121.9 19.2 %collective-permute-start.21 = (bf16[2,2,256,128]{3,2,1,0:T(8,128)(2,1)S(1)}, bf16[2,2,256,128]{3,2,1,0:T(8,128)(2,1)S(1)}, u32[]{:S(2)}, u32[]{:S(2)}) collective-permute-start(bf16[2,2,256,128]{3,2,1,0:T(8,128)(2,1)S(1)} %get-tuple-element.65), channel_id=1, source_target_pairs={{0,248},{1,249},{2,250},{3,251},{4,252},{5,253},{6,254},{7,255},{8... | collective-permute-start | bytes 786440 | tf_op jit(solution)/shard_map/ppermute | solution.py:33
  135.9 16.6 %collective-permute-start.22 = (bf16[2,2,512,128]{3,2,1,0:T(8,128)(2,1)}, bf16[2,2,512,128]{3,2,1,0:T(8,128)(2,1)S(1)}, u32[]{:S(2)}, u32[]{:S(2)}) collective-permute-start(bf16[2,2,512,128]{3,2,1,0:T(8,128)(2,1)} %slice.120), channel_id=1, source_target_pairs={{0,64},{1,17},{2,66},{3,19},{4,68},{5,21},{6,70},{7,23},{8,72},{9,... | collective-permute-start | bytes 1572872 | tf_op jit(solution)/shard_map/ppermute | solution.py:33
  137.3 15.3 %collective-permute-start.23 = (bf16[2,2,512,128]{3,2,1,0:T(8,128)(2,1)}, bf16[2,2,512,128]{3,2,1,0:T(8,128)(2,1)S(1)}, u32[]{:S(2)}, u32[]{:S(2)}) collective-permute-start(bf16[2,2,512,128]{3,2,1,0:T(8,128)(2,1)} %slice.121), channel_id=1, source_target_pairs={{0,192},{1,49},{2,194},{3,51},{4,196},{5,53},{6,198},{7,55},{8,200... | collective-permute-start | bytes 1572872 | tf_op jit(solution)/shard_map/ppermute | solution.py:33
  145.5 7.0 %copy-start.4 = (s32[5]{0:T(128)S(1)}, s32[5]{0:T(128)}, u32[]{:S(2)}) copy-start(s32[5]{0:T(128)} %stack.87.here) | copy-start | bytes 64
Sparse Core Ops, SparseCore 0:
  37.8 70.3 all-gather.1

commit v2 on v1

--- a/solution.py
+++ b/solution.py
@@ -214,7 +214,7 @@
     )(here, cot_t, activations, up_one, down_one)
 
 
-def adam_kernel(mine, theirs, master_in, first_in, second_in, new_master, moments, layer):
+def adam_kernel(mine, theirs, master_in, first_in, second_in, new_master, new_first, new_second, layer):
     grad = (mine[...].astype(jnp.float32) + theirs[...].astype(jnp.float32)).T
     rows = grad.shape[0]
     width = grad.shape[1] // 2
@@ -229,8 +229,8 @@
         new_master[at, :] = master - learn_rate * (
             first_hat / (jnp.sqrt(second_hat) + epsilon) + decay_rate * master
         )
-        moments[0, j] = first.astype(jnp.bfloat16)
-        moments[1, j] = second.astype(jnp.bfloat16)
+        new_first[j] = first.astype(jnp.bfloat16)
+        new_second[j] = second.astype(jnp.bfloat16)
     layer[...] = new_master[...].astype(jnp.bfloat16)
 
 
@@ -240,7 +240,7 @@
         adam_kernel,
         out_shape=(
             jax.ShapeDtypeStruct((rows, width), jnp.float32),
-            jax.ShapeDtypeStruct((2, 2, rows // 2, width), jnp.bfloat16),
+            *[jax.ShapeDtypeStruct((2, rows // 2, width), jnp.bfloat16)] * 2,
             jax.ShapeDtypeStruct((rows, width), jnp.bfloat16),
         ),
         compiler_params=WIDE,
@@ -250,37 +250,68 @@
     )(mine, theirs, master, first, second)
 
 
-def place_kernel(groups, here, *refs):
-    sources, out, sems = refs[: len(groups)], refs[-2], refs[-1]
+def copies_of(groups, here, sources, out, sems):
     copies = []
     for source, (first, second) in zip(sources, groups):
         for i in range(source.shape[0]):
             for s in range(2):
                 at = block_at(here, first, second + i, s, out.shape[0])
                 copies.append(pltpu.make_async_copy(source.at[i, s], out.at[at], sems.at[len(copies)]))
+    return copies
+
+
+def place_kernel(groups, here, *refs):
+    copies = copies_of(groups, here, refs[: len(groups)], refs[-2], refs[-1])
     for copy in copies:
         copy.start()
     for copy in copies:
         copy.wait()
 
 
-def place(here, groups, sources, total, into=None):
+def place(here, groups, sources, total):
     block = sources[0].shape[2:]
-    held = [] if into is None else [into]
     count = 2 * sum(source.shape[0] for source in sources)
-    any_space = pl.BlockSpec(memory_space=pl.ANY)
     return pl.pallas_call(
         functools.partial(place_kernel, groups),
         out_shape=jax.ShapeDtypeStruct((total,) + block, sources[0].dtype),
         in_specs=[pl.BlockSpec(memory_space=pltpu.SMEM)]
-        + [pl.BlockSpec(memory_space=pltpu.VMEM)] * len(sources)
-        + [any_space] * len(held),
-        out_specs=any_space,
+        + [pl.BlockSpec(memory_space=pltpu.VMEM)] * len(sources),
+        out_specs=pl.BlockSpec(memory_space=pl.ANY),
         scratch_shapes=[pltpu.SemaphoreType.DMA((count,))],
-        input_output_aliases={} if into is None else {1 + len(sources): 0},
         compiler_params=WIDE,
         cost_estimate=pl.CostEstimate(flops=0, bytes_accessed=0, transcendentals=0),
-    )(here, *sources, *held)
+    )(here, *sources)
+
+
+def finish_kernel(groups, here, low, high, master_in, first_in, second_in, held, *refs):
+    layer, master, first, second, sems = refs
+    copies = copies_of(groups, here, (low, high), layer, sems)
+    for copy in copies:
+        copy.start()
+    rows = first_in.shape[1]
+    master[...] = master_in[...]
+    for j in range(2):
+        at = pl.ds(j, rows, stride=2)
+        first[at, :] = first_in[j].astype(jnp.float32)
+        second[at, :] = second_in[j].astype(jnp.float32)
+    for copy in copies:
+        copy.wait()
+
+
+def finish(here, groups, low, high, master, first, second, layer):
+    any_space = pl.BlockSpec(memory_space=pl.ANY)
+    in_vmem = pl.BlockSpec(memory_space=pltpu.VMEM)
+    state = jax.ShapeDtypeStruct(master.shape, jnp.float32)
+    return pl.pallas_call(
+        functools.partial(finish_kernel, groups),
+        out_shape=[jax.ShapeDtypeStruct(layer.shape, layer.dtype), state, state, state],
+        in_specs=[pl.BlockSpec(memory_space=pltpu.SMEM)] + [in_vmem] * 5 + [any_space],
+        out_specs=[any_space] + [in_vmem] * 3,
+        scratch_shapes=[pltpu.SemaphoreType.DMA((2 * (low.shape[0] + high.shape[0]),))],
+        input_output_aliases={6: 0},
+        compiler_params=WIDE,
+        cost_estimate=pl.CostEstimate(flops=0, bytes_accessed=0, transcendentals=0),
+    )(here, low, high, master, first, second, layer)
 
 
 def input_kernel(here, cot_mine, cot_theirs, params, out, total):
@@ -323,7 +354,11 @@
             scratch_shapes=[pltpu.VMEM((tokens, 4 * rows), jnp.float32)],
         ),
         compiler_params=MOST,
-        cost_estimate=pl.CostEstimate(flops=0, bytes_accessed=0, transcendentals=0),
+        cost_estimate=pl.CostEstimate(
+            flops=16 * chips * tokens * columns * rows,
+            bytes_accessed=4 * chips * columns * (tokens + 2 * rows) + 8 * tokens * rows,
+            transcendentals=0,
+        ),
     )(here, cot_mine, cot_theirs, params)
 
 
@@ -379,33 +414,35 @@
     near = add(sums[0][0], *(g[0] for g in got))
     far, cot_theirs = tie(far, cot_theirs)
     state = [v.reshape(2 * rows, width) for v in (master_store, first_store, second_store)]
-    new_master, moments, layer = adam(near, move(far, other_half), *state)
+    new_master, new_first, new_second, layer = adam(near, move(far, other_half), *state)
 
     layer_other = move(layer, other_half)
-    layer_other, moments = tie(layer_other, moments)
-    moments = move(moments, previous_block)
+    layer_other, new_first = tie(layer_other, new_first)
+    new_first = move(new_first, previous_block)
     pair = jnp.where(h == 0, jnp.stack([layer, layer_other]), jnp.stack([layer_other, layer]))
     from_up = move(pair, along_second(-1))
     from_down = move(pair, along_second(1))
     from_far = move(pair, along_second(2))
     four = jnp.stack([pair, from_up, from_far, from_down])
-    four, new_master = tie(four, new_master)
+    four, new_master, new_first = tie(four, new_master, new_first)
     four_down, four_up = move(four, along_first(1)), move(four, along_first(-1))
     new_master = move(new_master, previous_block)
-    low, high, new_master = tie(four_down[:2], four_up[2:], new_master)
-    low_far, high_far = move(low, along_first(1)), move(high, along_first(-1))
     input_grad = input_matmul(here, cot_mine, cot_theirs, params)
+    four_down, four_up, input_grad, new_master, new_second = tie(
+        four_down, four_up, input_grad, new_master, new_second
+    )
+    new_second = move(new_second, previous_block)
+    low_far, high_far = move(four_down[:2], along_first(1)), move(four_up[2:], along_first(-1))
     new_layer = place(here, ((0, 0), (1, 0), (-1, 0)), [four, four_up, four_down], 32)
-    new_layer, input_grad = tie(new_layer, input_grad)
-    new_layer = place(here, ((2, 0), (2, 2)), [low_far, high_far], 32, new_layer)
-
-    shape = (rows, 2, width)
-    moments = moments.astype(jnp.float32).transpose(0, 2, 1, 3)
+    new_layer, *state = finish(
+        here, ((2, 0), (2, 2)), low_far, high_far, new_master, new_first, new_second, new_layer
+    )
+    new_master, new_first, new_second = (v.reshape(rows, 2, width) for v in state)
     return (
         input_grad,
-        new_master.reshape(shape),
-        moments[0],
-        moments[1],
+        new_master,
+        new_first,
+        new_second,
         new_layer.reshape(32 * rows, 2, width),
     )
 

time: 162 us -> 168 us (1.037)
  starting transfers between devices: 61.9 us -> 87.8 us
  waiting for transfers between devices: 53.1 us -> 35.9 us
  local copies, waits for them, and re-layouts: 5.89 us -> 1.68 us
  Pallas kernels: 23.7 us -> 25.4 us
    ppermute x24 -> x25, starting transfers between devices: 61.8 us -> 87.8 us  [move(): return lax.ppermute(value, AXES, pairs)]
    ppermute x24 -> x25, waiting for transfers between devices: 53.1 us -> 35.9 us  [move(): return lax.ppermute(value, AXES, pairs)]
    unnamed x23 -> x22, local copies, waits for them, and re-layouts: 3.52 us -> 1 us
    pallas_call x0 -> x1, Pallas kernels: none -> 2.47 us  [finish(): pl.pallas_call(functools.partial(finish_kernel, groups), out_shape=[jax.S...]
    pallas_call x2 -> x1, Pallas kernels: 4 us -> 2.41 us  [place(): pl.pallas_call(functools.partial(place_kernel, groups), out_shape=jax.Sha...]
  transfers between devices with their start and end apart: 25 -> 26, of which waited for: 13 -> 10; matrix products, arithmetic and copies ran while one was open for 3% -> 1% of each run, Pallas kernels for 11% -> 11%
where the time goes in v2:
time: 168 us
  starting transfers between devices  87.8 us (52%)
  waiting for transfers between devices  35.9 us (21%)
  Pallas kernels  25.4 us (15%)
  between operations  14.3 us (9%)
  other arithmetic  2.8 us (2%)
  local copies, waits for them, and re-layouts  1.68 us (1%)
    ppermute x25, starting transfers between devices, move(): return lax.ppermute(value, AXES, pairs)  87.8 us
    ppermute x25, waiting for transfers between devices, move(): return lax.ppermute(value, AXES, pairs)  35.9 us
    pallas_call x1, Pallas kernels, other_terms(): pl.pallas_call(functools.partial(other_kernel, groups), out_shape=[jax.Sh...  7.77 us
    pallas_call x1, Pallas kernels, input_matmul(): pl.pallas_call(input_kernel, out_shape=jax.ShapeDtypeStruct((tokens, 4 *...  7.09 us
    pallas_call x1, Pallas kernels, first_terms(): pl.pallas_call(functools.partial(first_kernel, groups), out_shape=[jax.Sh...  4.59 us
  transfers between devices with their start and end apart: 26, of which 10 were waited for; matrix products, arithmetic and copies ran while one was open for 1% of the time, Pallas kernels for 11%

profile of v2, /device:TPU:32, one launch (start us, length us, event | category | flops | bytes accessed | tf_op | source)
XLA Modules:
  0.0 167.9 jit_solution(4827774442749926879)
XLA Ops:
  7.2 0.0 all-gather.2.cloned.1.call-start
  7.2 0.6 stack.87.here
  7.8 4.6 %shard_map.101 = (bf16[512,256]{1,0:T(8,128)(2,1)}, bf16[256,512]{1,0:T(8,128)(2,1)}, bf16[256,256]{1,0:T(8,128)(2,1)}, bf16[2,2,256,256]{3,2,1,0:T(8,128)(2,1)}, bf16[2,2,256,256]{3,2,1,0:T(8,128)(2,1)}) custom-call(s32[5]{0:T(128)} %stack.87.here, bf16[1024,128]{1,0:T(8,128)(2,1)} %bitcast.55, bf16[512,128]{1,0:T(8,128)(2,1)} %bitcast.63, ...), custom_call_target="tpu_custom_call" | custom-call | flops 536870912 | bytes 3932160 | tf_op jit(solution)/shard_map/pallas_call | solution.py:161
  12.4 1.6 collective-permute-start
  14.0 1.7 %collective-permute-start.1 = (bf16[2,2,256,256]{3,2,1,0:T(8,128)(2,1)}, bf16[2,2,256,256]{3,2,1,0:T(8,128)(2,1)S(1)}, u32[]{:S(2)}, u32[]{:S(2)}) collective-permute-start(bf16[2,2,256,256]{3,2,1,0:T(8,128)(2,1)} %get-tuple-element.45), channel_id=1, source_target_pairs={{0,192},{1,49},{2,194},{3,51},{4,196},{5,53},{6,198},{7,55},{8,200... | collective-permute-start | bytes 1572872 | tf_op jit(solution)/shard_map/ppermute | solution.py:33
  15.7 1.9 %collective-permute-start.4 = (bf16[512,256]{1,0:T(8,128)(2,1)}, bf16[512,256]{1,0:T(8,128)(2,1)S(1)}, u32[]{:S(2)}, u32[]{:S(2)}) collective-permute-start(bf16[512,256]{1,0:T(8,128)(2,1)} %get-tuple-element.50), channel_id=1, source_target_pairs={{0,2},{1,3},{2,4},{3,5},{4,6},{5,7},{6,0},{7,1},{8,10},{9,11},{10,... | collective-permute-start | bytes 786440 | tf_op jit(solution)/shard_map/ppermute | solution.py:33
  17.7 4.7 %collective-permute-start.3 = (bf16[256,256]{1,0:T(8,128)(2,1)}, bf16[256,256]{1,0:T(8,128)(2,1)S(1)}, u32[]{:S(2)}, u32[]{:S(2)}) collective-permute-start(bf16[256,256]{1,0:T(8,128)(2,1)} %get-tuple-element.49), channel_id=1, source_target_pairs={{0,8},{1,40},{2,72},{3,104},{4,136},{5,168},{6,200},{7,232},{8,0},... | collective-permute-start | bytes 393224 | tf_op jit(solution)/shard_map/ppermute | solution.py:33
  22.3 4.1 %collective-permute-start.2 = (bf16[256,256]{1,0:T(8,128)(2,1)}, bf16[256,256]{1,0:T(8,128)(2,1)S(1)}, u32[]{:S(2)}, u32[]{:S(2)}) collective-permute-start(bf16[256,256]{1,0:T(8,128)(2,1)} %get-tuple-element.49), channel_id=1, source_target_pairs={{0,0},{1,32},{2,64},{3,96},{4,128},{5,160},{6,192},{7,224},{8,8},{... | collective-permute-start | bytes 393224 | tf_op jit(solution)/shard_map/ppermute | solution.py:33
  26.4 0.0 collective-permute-done.up_one
  26.4 0.0 collective-permute-done.1.down_one
  26.5 0.8 copy-done.7
  27.2 0.2 copy-done.8
  27.4 7.8 %shard_map.102 = (bf16[4,2,256,256]{3,2,1,0:T(8,128)(2,1)}, bf16[4,2,256,256]{3,2,1,0:T(8,128)(2,1)}, bf16[4,2,256,256]{3,2,1,0:T(8,128)(2,1)}) custom-call(s32[5]{0:T(128)} %stack.87.here, bf16[256,512]{1,0:T(8,128)(2,1)} %get-tuple-element.43.cot, bf16[512,8192]{1,0:T(8,128)(2,1)} %activations.3, bf16[2,2,256,256]{3,2,1,0:T(8,128)(2,1)} %copy-done.7, ...), custom_call_target="tpu_custom_call" | custom-call | flops 1610612736 | bytes 9699328 | tf_op jit(solution)/shard_map/pallas_call | solution.py:192
  35.2 0.0 collective-permute-done.3
  35.2 1.7 %collective-permute-done.2 = bf16[256,256]{1,0:T(8,128)(2,1)S(1)} collective-permute-done((bf16[256,256]{1,0:T(8,128)(2,1)}, bf16[256,256]{1,0:T(8,128)(2,1)S(1)}, u32[]{:S(2)}, u32[]{:S(2)}) %collective-permute-start.2) | collective-permute-done | bytes 131104 | tf_op jit(solution)/shard_map/ppermute | solution.py:33
  36.9 0.0 collective-permute-done.4
  36.9 0.7 maximum_select_fusion.2
  37.6 0.0 all-gather.2.cloned.1.call-update
  37.7 0.1 collective-permute-start.5
  37.8 3.2 %collective-permute-start.6 = (bf16[4,2,256,256]{3,2,1,0:T(8,128)(2,1)}, bf16[4,2,256,256]{3,2,1,0:T(8,128)(2,1)S(1)}, u32[]{:S(2)}, u32[]{:S(2)}) collective-permute-start(bf16[4,2,256,256]{3,2,1,0:T(8,128)(2,1)} %get-tuple-element.52), channel_id=1, source_target_pairs={{0,192},{1,49},{2,194},{3,51},{4,196},{5,53},{6,198},{7,55},{8,200... | collective-permute-start | bytes 3145736 | tf_op jit(solution)/shard_map/ppermute | solution.py:33
  41.0 1.0 collective-permute-start.8
  41.9 2.2 %collective-permute-start.7 = (bf16[512,256]{1,0:T(8,128)(2,1)S(1)}, bf16[512,256]{1,0:T(8,128)(2,1)S(1)}, u32[]{:S(2)}, u32[]{:S(2)}) collective-permute-start(bf16[512,256]{1,0:T(8,128)(2,1)S(1)} %collective-permute-done.4), channel_id=1, source_target_pairs={{0,2},{1,3},{2,4},{3,5},{4,6},{5,7},{6,0},{7,1},{8,10},{9,11},{10,... | collective-permute-start | bytes 786440 | tf_op jit(solution)/shard_map/ppermute | solution.py:33
  44.1 9.8 %collective-permute-done.5 = bf16[4,2,256,256]{3,2,1,0:T(8,128)(2,1)S(1)} collective-permute-done((bf16[4,2,256,256]{3,2,1,0:T(8,128)(2,1)}, bf16[4,2,256,256]{3,2,1,0:T(8,128)(2,1)S(1)}, u32[]{:S(2)}, u32[]{:S(2)}) %collective-permute-start.5) | collective-permute-done | bytes 1048608 | tf_op jit(solution)/shard_map/ppermute | solution.py:33
  54.0 0.0 collective-permute-done.6
  54.0 1.6 add_convert_fusion.3
  55.6 0.0 collective-permute-done.8
  55.6 1.3 collective-permute-done.7
  56.9 0.1 pad_maximum_fusion.cot_mine
  57.1 0.0 copy-start.6
  57.1 0.1 collective-permute-start.12
  57.2 0.1 collective-permute-start.9
  57.3 4.2 %collective-permute-start.10 = (bf16[2,256,256]{2,1,0:T(8,128)(2,1)S(1)}, bf16[2,256,256]{2,1,0:T(8,128)(2,1)S(1)}, u32[]{:S(2)}, u32[]{:S(2)}) collective-permute-start(bf16[2,256,256]{2,1,0:T(8,128)(2,1)S(1)} %get-tuple-element.55), channel_id=1, source_target_pairs={{0,48},{1,193},{2,50},{3,195},{4,52},{5,197},{6,54},{7,199},{8,56}... | collective-permute-start | bytes 786440 | tf_op jit(solution)/shard_map/ppermute | solution.py:33
  61.4 2.0 %collective-permute-start.11 = (bf16[2,256,256]{2,1,0:T(8,128)(2,1)S(1)}, bf16[2,256,256]{2,1,0:T(8,128)(2,1)S(1)}, u32[]{:S(2)}, u32[]{:S(2)}) collective-permute-start(bf16[2,256,256]{2,1,0:T(8,128)(2,1)S(1)} %get-tuple-element.56), channel_id=1, source_target_pairs={{0,32},{1,129},{2,34},{3,131},{4,36},{5,133},{6,38},{7,135},{8,40}... | collective-permute-start | bytes 786440 | tf_op jit(solution)/shard_map/ppermute | solution.py:33
  63.5 2.8 %collective-permute-done.9 = bf16[2,256,256]{2,1,0:T(8,128)(2,1)S(1)} collective-permute-done((bf16[2,256,256]{2,1,0:T(8,128)(2,1)S(1)}, bf16[2,256,256]{2,1,0:T(8,128)(2,1)S(1)}, u32[]{:S(2)}, u32[]{:S(2)}) %collective-permute-start.9) | collective-permute-done | bytes 262176 | tf_op jit(solution)/shard_map/ppermute | solution.py:33
  66.3 1.0 collective-permute-done.10
  67.3 5.4 %collective-permute-done.11 = bf16[2,256,256]{2,1,0:T(8,128)(2,1)S(1)} collective-permute-done((bf16[2,256,256]{2,1,0:T(8,128)(2,1)S(1)}, bf16[2,256,256]{2,1,0:T(8,128)(2,1)S(1)}, u32[]{:S(2)}, u32[]{:S(2)}) %collective-permute-start.11) | collective-permute-done | bytes 262176 | tf_op jit(solution)/shard_map/ppermute | solution.py:33
  72.8 0.1 fusion.10
  72.9 0.0 collective-permute-done.12.cot_theirs
  72.9 10.0 %collective-permute-start.13 = (bf16[256,256]{1,0:T(8,128)(2,1)S(1)}, bf16[256,256]{1,0:T(8,128)(2,1)S(1)}, u32[]{:S(2)}, u32[]{:S(2)}) collective-permute-start(bf16[256,256]{1,0:T(8,128)(2,1)S(1)} %get-tuple-element.59), channel_id=1, source_target_pairs={{0,8},{1,9},{2,10},{3,11},{4,12},{5,13},{6,14},{7,15},{8,0},{9,1},... | collective-permute-start | bytes 393224 | tf_op jit(solution)/shard_map/ppermute | solution.py:33
  82.9 4.3 %collective-permute-done.13.theirs = bf16[256,256]{1,0:T(8,128)(2,1)S(1)} collective-permute-done((bf16[256,256]{1,0:T(8,128)(2,1)S(1)}, bf16[256,256]{1,0:T(8,128)(2,1)S(1)}, u32[]{:S(2)}, u32[]{:S(2)}) %collective-permute-start.13) | collective-permute-done | bytes 131104 | tf_op jit(solution)/shard_map/ppermute | solution.py:33
  87.2 1.0 shard_map.103
  88.2 4.7 %collective-permute-start.14 = (bf16[512,128]{1,0:T(8,128)(2,1)S(1)}, bf16[512,128]{1,0:T(8,128)(2,1)S(1)}, u32[]{:S(2)}, u32[]{:S(2)}) collective-permute-start(bf16[512,128]{1,0:T(8,128)(2,1)S(1)} %get-tuple-element.60), channel_id=1, source_target_pairs={{0,8},{1,9},{2,10},{3,11},{4,12},{5,13},{6,14},{7,15},{8,0},{9,1},... | collective-permute-start | bytes 393224 | tf_op jit(solution)/shard_map/ppermute | solution.py:33
  92.9 4.2 %collective-permute-done.14 = bf16[512,128]{1,0:T(8,128)(2,1)S(1)} collective-permute-done((bf16[512,128]{1,0:T(8,128)(2,1)S(1)}, bf16[512,128]{1,0:T(8,128)(2,1)S(1)}, u32[]{:S(2)}, u32[]{:S(2)}) %collective-permute-start.14) | collective-permute-done | bytes 131104 | tf_op jit(solution)/shard_map/ppermute | solution.py:33
  97.1 1.3 collective-permute-start.17
  98.5 3.2 %collective-permute-start.16 = (bf16[2,512,128]{2,1,0:T(8,128)(2,1)S(1)}, bf16[2,512,128]{2,1,0:T(8,128)(2,1)S(1)}, u32[]{:S(2)}, u32[]{:S(2)}) collective-permute-start(bf16[2,512,128]{2,1,0:T(8,128)(2,1)S(1)} %maximum_select_fusion.1), channel_id=1, source_target_pairs={{0,32},{1,129},{2,34},{3,131},{4,36},{5,133},{6,38},{7,135},{8,40}... | collective-permute-start | bytes 786440 | tf_op jit(solution)/shard_map/ppermute | solution.py:33
  101.7 0.6 collective-permute-start.15
  102.3 14.9 %collective-permute-start.18 = (bf16[2,256,128]{2,1,0:T(8,128)(2,1)S(1)}, bf16[2,256,128]{2,1,0:T(8,128)(2,1)S(1)}, u32[]{:S(2)}, u32[]{:S(2)}) collective-permute-start(bf16[2,256,128]{2,1,0:T(8,128)(2,1)S(1)} %get-tuple-element.64), channel_id=1, source_target_pairs={{0,248},{1,249},{2,250},{3,251},{4,252},{5,253},{6,254},{7,255},{8... | collective-permute-start | bytes 393224 | tf_op jit(solution)/shard_map/ppermute | solution.py:33
  117.2 0.0 collective-permute-done.17
  117.3 0.0 collective-permute-done.16
  117.3 0.0 collective-permute-done.15
  117.3 0.1 pad_maximum_fusion.1.refs_0_
  117.4 5.1 %collective-permute-done.18.first_in = bf16[2,256,128]{2,1,0:T(8,128)(2,1)S(1)} collective-permute-done((bf16[2,256,128]{2,1,0:T(8,128)(2,1)S(1)}, bf16[2,256,128]{2,1,0:T(8,128)(2,1)S(1)}, u32[]{:S(2)}, u32[]{:S(2)}) %collective-permute-start.18) | collective-permute-done | bytes 131104 | tf_op jit(solution)/shard_map/ppermute | solution.py:33
  122.6 2.0 %collective-permute-start.19 = (bf16[4,2,512,128]{3,2,1,0:T(8,128)(2,1)S(1)}, bf16[4,2,512,128]{3,2,1,0:T(8,128)(2,1)S(1)}, u32[]{:S(2)}, u32[]{:S(2)}) collective-permute-start(bf16[4,2,512,128]{3,2,1,0:T(8,128)(2,1)S(1)} %pad_maximum_fusion.1.refs_0_), channel_id=1, source_target_pairs={{0,64},{1,17},{2,66},{3,19},{4,68},{5,21},{6,70},{7,23},{8,72},{9,... | collective-permute-start | bytes 3145736 | tf_op jit(solution)/shard_map/ppermute | solution.py:33
  124.6 11.9 %collective-permute-start.21 = (f32[512,128]{1,0:T(8,128)}, f32[512,128]{1,0:T(8,128)S(1)}, u32[]{:S(2)}, u32[]{:S(2)}) collective-permute-start(f32[512,128]{1,0:T(8,128)} %get-tuple-element.69), channel_id=1, source_target_pairs={{0,248},{1,249},{2,250},{3,251},{4,252},{5,253},{6,254},{7,255},{8... | collective-permute-start | bytes 786440 | tf_op jit(solution)/shard_map/ppermute | solution.py:33
  136.5 7.1 %shard_map.104 = bf16[512,1024]{1,0:T(8,128)(2,1)} custom-call(s32[5]{0:T(128)} %stack.87.here, bf16[4,512,256]{2,1,0:T(8,128)(2,1)} %copy-done.6, bf16[4,512,256]{2,1,0:T(8,128)(2,1)} %copy-done.10, bf16[16,2,256,256]{3,2,1,0:T(8,128)(2,1)} %all-gather.2.cloned.1.call-done.params), custom_call_target="tpu_custom_call" | custom-call | flops 2147483648 | bytes 5242880 | tf_op jit(solution)/shard_map/pallas_call | solution.py:342
  143.6 0.0 collective-permute-done.19.refs_2_
  143.7 0.1 collective-permute-start.23
  143.8 2.0 %collective-permute-start.22 = (bf16[2,2,512,128]{3,2,1,0:T(8,128)(2,1)S(1)}, bf16[2,2,512,128]{3,2,1,0:T(8,128)(2,1)S(1)}, u32[]{:S(2)}, u32[]{:S(2)}) collective-permute-start(bf16[2,2,512,128]{3,2,1,0:T(8,128)(2,1)S(1)} %slice.94), channel_id=1, source_target_pairs={{0,64},{1,17},{2,66},{3,19},{4,68},{5,21},{6,70},{7,23},{8,72},{9,... | collective-permute-start | bytes 1572872 | tf_op jit(solution)/shard_map/ppermute | solution.py:33
  145.8 10.2 %collective-permute-start.24 = (bf16[2,256,128]{2,1,0:T(8,128)(2,1)S(1)}, bf16[2,256,128]{2,1,0:T(8,128)(2,1)S(1)}, u32[]{:S(2)}, u32[]{:S(2)}) collective-permute-start(bf16[2,256,128]{2,1,0:T(8,128)(2,1)S(1)} %copy-done.5), channel_id=1, source_target_pairs={{0,248},{1,249},{2,250},{3,251},{4,252},{5,253},{6,254},{7,255},{8... | collective-permute-start | bytes 393224 | tf_op jit(solution)/shard_map/ppermute | solution.py:33
  156.0 2.4 %shard_map.105.held = bf16[32,512,128]{2,1,0:T(8,128)(2,1)} custom-call(s32[5]{0:T(128)S(1)} %copy-done.3, bf16[4,2,512,128]{3,2,1,0:T(8,128)(2,1)S(1)} %pad_maximum_fusion.1.refs_0_, bf16[4,2,512,128]{3,2,1,0:T(8,128)(2,1)S(1)} %collective-permute-done.20.refs_1_, bf16[4,2,512,128]{3,2,1,0:T(8,128)(2,1)S(1)} %collective-permute-done.19.refs_2_), custom_call_target="tpu_custom_call" | custom-call | tf_op jit(solution)/shard_map/pallas_call | solution.py:274
  158.4 0.1 collective-permute-done.24.second_in
  158.5 0.0 collective-permute-done.23.high
  158.5 0.0 collective-permute-done.22.low
  158.5 2.5 %shard_map.106 = (bf16[32,512,128]{2,1,0:T(8,128)(2,1)}, f32[512,128]{1,0:T(8,128)}, f32[512,128]{1,0:T(8,128)}, f32[512,128]{1,0:T(8,128)}) custom-call(s32[5]{0:T(128)S(1)} %copy-done.3, bf16[2,2,512,128]{3,2,1,0:T(8,128)(2,1)S(1)} %collective-permute-done.22.low, ...), custom_call_target="tpu_custom_call", output_to_operand_aliasing={{0}: (6, {})} | custom-call | tf_op jit(solution)/shard_map/pallas_call | solution.py:305
  (27 shorter events, 0.2 us)
Async XLA Ops:
  7.2 129.3 %all-gather.2.cloned.1.call-start = ((), (), s32[]{:S(2)}) async-start(), calls=%async_computation | async-start | bytes 4456448 | tf_op jit(solution)/shard_map/all_gather | solution.py:401
  12.4 14.0 %collective-permute-start = (bf16[2,2,256,256]{3,2,1,0:T(8,128)(2,1)}, bf16[2,2,256,256]{3,2,1,0:T(8,128)(2,1)S(1)}, u32[]{:S(2)}, u32[]{:S(2)}) collective-permute-start(bf16[2,2,256,256]{3,2,1,0:T(8,128)(2,1)} %get-tuple-element.44), channel_id=1, source_target_pairs={{0,64},{1,17},{2,66},{3,19},{4,68},{5,21},{6,70},{7,23},{8,72},{9,... | collective-permute-start | bytes 1572872 | tf_op jit(solution)/shard_map/ppermute | solution.py:33
  14.0 12.4 %collective-permute-start.1 = (bf16[2,2,256,256]{3,2,1,0:T(8,128)(2,1)}, bf16[2,2,256,256]{3,2,1,0:T(8,128)(2,1)S(1)}, u32[]{:S(2)}, u32[]{:S(2)}) collective-permute-start(bf16[2,2,256,256]{3,2,1,0:T(8,128)(2,1)} %get-tuple-element.45), channel_id=1, source_target_pairs={{0,192},{1,49},{2,194},{3,51},{4,196},{5,53},{6,198},{7,55},{8,200... | collective-permute-start | bytes 1572872 | tf_op jit(solution)/shard_map/ppermute | solution.py:33
  15.7 21.2 %collective-permute-start.4 = (bf16[512,256]{1,0:T(8,128)(2,1)}, bf16[512,256]{1,0:T(8,128)(2,1)S(1)}, u32[]{:S(2)}, u32[]{:S(2)}) collective-permute-start(bf16[512,256]{1,0:T(8,128)(2,1)} %get-tuple-element.50), channel_id=1, source_target_pairs={{0,2},{1,3},{2,4},{3,5},{4,6},{5,7},{6,0},{7,1},{8,10},{9,11},{10,... | collective-permute-start | bytes 786440 | tf_op jit(solution)/shard_map/ppermute | solution.py:33
  17.7 17.5 %collective-permute-start.3 = (bf16[256,256]{1,0:T(8,128)(2,1)}, bf16[256,256]{1,0:T(8,128)(2,1)S(1)}, u32[]{:S(2)}, u32[]{:S(2)}) collective-permute-start(bf16[256,256]{1,0:T(8,128)(2,1)} %get-tuple-element.49), channel_id=1, source_target_pairs={{0,8},{1,40},{2,72},{3,104},{4,136},{5,168},{6,200},{7,232},{8,0},... | collective-permute-start | bytes 393224 | tf_op jit(solution)/shard_map/ppermute | solution.py:33
  22.3 14.6 %collective-permute-start.2 = (bf16[256,256]{1,0:T(8,128)(2,1)}, bf16[256,256]{1,0:T(8,128)(2,1)S(1)}, u32[]{:S(2)}, u32[]{:S(2)}) collective-permute-start(bf16[256,256]{1,0:T(8,128)(2,1)} %get-tuple-element.49), channel_id=1, source_target_pairs={{0,0},{1,32},{2,64},{3,96},{4,128},{5,160},{6,192},{7,224},{8,8},{... | collective-permute-start | bytes 393224 | tf_op jit(solution)/shard_map/ppermute | solution.py:33
  26.4 0.8 copy-start.7
  26.4 1.0 copy-start.8
  27.4 13.6 %copy-start.9 = (bf16[512,256]{1,0:T(8,128)(2,1)S(1)}, bf16[512,256]{1,0:T(8,128)(2,1)}, u32[]{:S(2)}) copy-start(bf16[512,256]{1,0:T(8,128)(2,1)} %get-tuple-element.50) | copy-start | bytes 786436
  36.9 50.3 %copy-start = (f32[256,2,128]{2,1,0:T(2,128)S(1)}, f32[256,2,128]{2,1,0:T(2,128)}, u32[]{:S(2)}) copy-start(f32[256,2,128]{2,1,0:T(2,128)} %param.9) | copy-start | bytes 786436
  36.9 50.3 %copy-start.1 = (f32[256,2,128]{2,1,0:T(2,128)S(1)}, f32[256,2,128]{2,1,0:T(2,128)}, u32[]{:S(2)}) copy-start(f32[256,2,128]{2,1,0:T(2,128)} %param.10) | copy-start | bytes 786436
  36.9 50.3 %copy-start.2 = (f32[256,2,128]{2,1,0:T(2,128)S(1)}, f32[256,2,128]{2,1,0:T(2,128)}, u32[]{:S(2)}) copy-start(f32[256,2,128]{2,1,0:T(2,128)} %param.11) | copy-start | bytes 786436
  37.7 16.3 %collective-permute-start.5 = (bf16[4,2,256,256]{3,2,1,0:T(8,128)(2,1)}, bf16[4,2,256,256]{3,2,1,0:T(8,128)(2,1)S(1)}, u32[]{:S(2)}, u32[]{:S(2)}) collective-permute-start(bf16[4,2,256,256]{3,2,1,0:T(8,128)(2,1)} %get-tuple-element.51), channel_id=1, source_target_pairs={{0,64},{1,17},{2,66},{3,19},{4,68},{5,21},{6,70},{7,23},{8,72},{9,... | collective-permute-start | bytes 3145736 | tf_op jit(solution)/shard_map/ppermute | solution.py:33
  37.8 16.2 %collective-permute-start.6 = (bf16[4,2,256,256]{3,2,1,0:T(8,128)(2,1)}, bf16[4,2,256,256]{3,2,1,0:T(8,128)(2,1)S(1)}, u32[]{:S(2)}, u32[]{:S(2)}) collective-permute-start(bf16[4,2,256,256]{3,2,1,0:T(8,128)(2,1)} %get-tuple-element.52), channel_id=1, source_target_pairs={{0,192},{1,49},{2,194},{3,51},{4,196},{5,53},{6,198},{7,55},{8,200... | collective-permute-start | bytes 3145736 | tf_op jit(solution)/shard_map/ppermute | solution.py:33
  41.0 14.6 %collective-permute-start.8 = (bf16[512,256]{1,0:T(8,128)(2,1)S(1)}, bf16[512,256]{1,0:T(8,128)(2,1)S(1)}, u32[]{:S(2)}, u32[]{:S(2)}) collective-permute-start(bf16[512,256]{1,0:T(8,128)(2,1)S(1)} %copy-done.9), channel_id=1, source_target_pairs={{0,6},{1,7},{2,0},{3,1},{4,2},{5,3},{6,4},{7,5},{8,14},{9,15},{10,... | collective-permute-start | bytes 786440 | tf_op jit(solution)/shard_map/ppermute | solution.py:33
  41.9 15.0 %collective-permute-start.7 = (bf16[512,256]{1,0:T(8,128)(2,1)S(1)}, bf16[512,256]{1,0:T(8,128)(2,1)S(1)}, u32[]{:S(2)}, u32[]{:S(2)}) collective-permute-start(bf16[512,256]{1,0:T(8,128)(2,1)S(1)} %collective-permute-done.4), channel_id=1, source_target_pairs={{0,2},{1,3},{2,4},{3,5},{4,6},{5,7},{6,0},{7,1},{8,10},{9,11},{10,... | collective-permute-start | bytes 786440 | tf_op jit(solution)/shard_map/ppermute | solution.py:33
  57.1 30.1 %copy-start.6 = (bf16[4,512,256]{2,1,0:T(8,128)(2,1)}, bf16[4,512,256]{2,1,0:T(8,128)(2,1)S(1)}, u32[]{:S(2)}) copy-start(bf16[4,512,256]{2,1,0:T(8,128)(2,1)S(1)} %pad_maximum_fusion.cot_mine) | copy-start | bytes 3145732
  57.1 15.8 %collective-permute-start.12 = (bf16[4,512,256]{2,1,0:T(8,128)(2,1)S(1)}, bf16[4,512,256]{2,1,0:T(8,128)(2,1)S(1)}, u32[]{:S(2)}, u32[]{:S(2)}) collective-permute-start(bf16[4,512,256]{2,1,0:T(8,128)(2,1)S(1)} %pad_maximum_fusion.cot_mine), channel_id=1, source_target_pairs={{0,1},{1,0},{2,3},{3,2},{4,5},{5,4},{6,7},{7,6},{8,9},{9,8},{10,11... | collective-permute-start | bytes 3145736 | tf_op jit(solution)/shard_map/ppermute | solution.py:33
  57.2 9.1 %collective-permute-start.9 = (bf16[2,256,256]{2,1,0:T(8,128)(2,1)S(1)}, bf16[2,256,256]{2,1,0:T(8,128)(2,1)S(1)}, u32[]{:S(2)}, u32[]{:S(2)}) collective-permute-start(bf16[2,256,256]{2,1,0:T(8,128)(2,1)S(1)} %get-tuple-element.54), channel_id=1, source_target_pairs={{0,16},{1,65},{2,18},{3,67},{4,20},{5,69},{6,22},{7,71},{8,24},{9,... | collective-permute-start | bytes 786440 | tf_op jit(solution)/shard_map/ppermute | solution.py:33
  57.3 10.1 %collective-permute-start.10 = (bf16[2,256,256]{2,1,0:T(8,128)(2,1)S(1)}, bf16[2,256,256]{2,1,0:T(8,128)(2,1)S(1)}, u32[]{:S(2)}, u32[]{:S(2)}) collective-permute-start(bf16[2,256,256]{2,1,0:T(8,128)(2,1)S(1)} %get-tuple-element.55), channel_id=1, source_target_pairs={{0,48},{1,193},{2,50},{3,195},{4,52},{5,197},{6,54},{7,199},{8,56}... | collective-permute-start | bytes 786440 | tf_op jit(solution)/shard_map/ppermute | solution.py:33
  61.4 11.3 %collective-permute-start.11 = (bf16[2,256,256]{2,1,0:T(8,128)(2,1)S(1)}, bf16[2,256,256]{2,1,0:T(8,128)(2,1)S(1)}, u32[]{:S(2)}, u32[]{:S(2)}) collective-permute-start(bf16[2,256,256]{2,1,0:T(8,128)(2,1)S(1)} %get-tuple-element.56), channel_id=1, source_target_pairs={{0,32},{1,129},{2,34},{3,131},{4,36},{5,133},{6,38},{7,135},{8,40}... | collective-permute-start | bytes 786440 | tf_op jit(solution)/shard_map/ppermute | solution.py:33
  72.9 14.3 %copy-start.10 = (bf16[4,512,256]{2,1,0:T(8,128)(2,1)}, bf16[4,512,256]{2,1,0:T(8,128)(2,1)S(1)}, u32[]{:S(2)}) copy-start(bf16[4,512,256]{2,1,0:T(8,128)(2,1)S(1)} %collective-permute-done.12.cot_theirs) | copy-start | bytes 3145732
  72.9 14.2 %collective-permute-start.13 = (bf16[256,256]{1,0:T(8,128)(2,1)S(1)}, bf16[256,256]{1,0:T(8,128)(2,1)S(1)}, u32[]{:S(2)}, u32[]{:S(2)}) collective-permute-start(bf16[256,256]{1,0:T(8,128)(2,1)S(1)} %get-tuple-element.59), channel_id=1, source_target_pairs={{0,8},{1,9},{2,10},{3,11},{4,12},{5,13},{6,14},{7,15},{8,0},{9,1},... | collective-permute-start | bytes 393224 | tf_op jit(solution)/shard_map/ppermute | solution.py:33
  88.2 34.3 %copy-start.4 = (bf16[2,256,128]{2,1,0:T(8,128)(2,1)}, bf16[2,256,128]{2,1,0:T(8,128)(2,1)S(1)}, u32[]{:S(2)}) copy-start(bf16[2,256,128]{2,1,0:T(8,128)(2,1)S(1)} %get-tuple-element.76) | copy-start | bytes 393220
  88.2 8.9 %collective-permute-start.14 = (bf16[512,128]{1,0:T(8,128)(2,1)S(1)}, bf16[512,128]{1,0:T(8,128)(2,1)S(1)}, u32[]{:S(2)}, u32[]{:S(2)}) collective-permute-start(bf16[512,128]{1,0:T(8,128)(2,1)S(1)} %get-tuple-element.60), channel_id=1, source_target_pairs={{0,8},{1,9},{2,10},{3,11},{4,12},{5,13},{6,14},{7,15},{8,0},{9,1},... | collective-permute-start | bytes 393224 | tf_op jit(solution)/shard_map/ppermute | solution.py:33
  97.1 20.1 %collective-permute-start.17 = (bf16[2,512,128]{2,1,0:T(8,128)(2,1)S(1)}, bf16[2,512,128]{2,1,0:T(8,128)(2,1)S(1)}, u32[]{:S(2)}, u32[]{:S(2)}) collective-permute-start(bf16[2,512,128]{2,1,0:T(8,128)(2,1)S(1)} %maximum_select_fusion.1), channel_id=1, source_target_pairs={{0,16},{1,65},{2,18},{3,67},{4,20},{5,69},{6,22},{7,71},{8,24},{9,... | collective-permute-start | bytes 786440 | tf_op jit(solution)/shard_map/ppermute | solution.py:33
  98.5 18.8 %collective-permute-start.16 = (bf16[2,512,128]{2,1,0:T(8,128)(2,1)S(1)}, bf16[2,512,128]{2,1,0:T(8,128)(2,1)S(1)}, u32[]{:S(2)}, u32[]{:S(2)}) collective-permute-start(bf16[2,512,128]{2,1,0:T(8,128)(2,1)S(1)} %maximum_select_fusion.1), channel_id=1, source_target_pairs={{0,32},{1,129},{2,34},{3,131},{4,36},{5,133},{6,38},{7,135},{8,40}... | collective-permute-start | bytes 786440 | tf_op jit(solution)/shard_map/ppermute | solution.py:33
  101.7 15.6 %collective-permute-start.15 = (bf16[2,512,128]{2,1,0:T(8,128)(2,1)S(1)}, bf16[2,512,128]{2,1,0:T(8,128)(2,1)S(1)}, u32[]{:S(2)}, u32[]{:S(2)}) collective-permute-start(bf16[2,512,128]{2,1,0:T(8,128)(2,1)S(1)} %maximum_select_fusion.1), channel_id=1, source_target_pairs={{0,48},{1,193},{2,50},{3,195},{4,52},{5,197},{6,54},{7,199},{8,56}... | collective-permute-start | bytes 786440 | tf_op jit(solution)/shard_map/ppermute | solution.py:33
  102.3 20.2 %collective-permute-start.18 = (bf16[2,256,128]{2,1,0:T(8,128)(2,1)S(1)}, bf16[2,256,128]{2,1,0:T(8,128)(2,1)S(1)}, u32[]{:S(2)}, u32[]{:S(2)}) collective-permute-start(bf16[2,256,128]{2,1,0:T(8,128)(2,1)S(1)} %get-tuple-element.64), channel_id=1, source_target_pairs={{0,248},{1,249},{2,250},{3,251},{4,252},{5,253},{6,254},{7,255},{8... | collective-permute-start | bytes 393224 | tf_op jit(solution)/shard_map/ppermute | solution.py:33
  122.5 33.4 %copy-start.3 = (s32[5]{0:T(128)S(1)}, s32[5]{0:T(128)}, u32[]{:S(2)}) copy-start(s32[5]{0:T(128)} %stack.87.here) | copy-start | bytes 64
  122.6 21.0 %collective-permute-start.20 = (bf16[4,2,512,128]{3,2,1,0:T(8,128)(2,1)S(1)}, bf16[4,2,512,128]{3,2,1,0:T(8,128)(2,1)S(1)}, u32[]{:S(2)}, u32[]{:S(2)}) collective-permute-start(bf16[4,2,512,128]{3,2,1,0:T(8,128)(2,1)S(1)} %pad_maximum_fusion.1.refs_0_), channel_id=1, source_target_pairs={{0,192},{1,49},{2,194},{3,51},{4,196},{5,53},{6,198},{7,55},{8,200... | collective-permute-start | bytes 3145736 | tf_op jit(solution)/shard_map/ppermute | solution.py:33
  122.6 21.0 %collective-permute-start.19 = (bf16[4,2,512,128]{3,2,1,0:T(8,128)(2,1)S(1)}, bf16[4,2,512,128]{3,2,1,0:T(8,128)(2,1)S(1)}, u32[]{:S(2)}, u32[]{:S(2)}) collective-permute-start(bf16[4,2,512,128]{3,2,1,0:T(8,128)(2,1)S(1)} %pad_maximum_fusion.1.refs_0_), channel_id=1, source_target_pairs={{0,64},{1,17},{2,66},{3,19},{4,68},{5,21},{6,70},{7,23},{8,72},{9,... | collective-permute-start | bytes 3145736 | tf_op jit(solution)/shard_map/ppermute | solution.py:33
  124.6 19.0 %collective-permute-start.21 = (f32[512,128]{1,0:T(8,128)}, f32[512,128]{1,0:T(8,128)S(1)}, u32[]{:S(2)}, u32[]{:S(2)}) collective-permute-start(f32[512,128]{1,0:T(8,128)} %get-tuple-element.69), channel_id=1, source_target_pairs={{0,248},{1,249},{2,250},{3,251},{4,252},{5,253},{6,254},{7,255},{8... | collective-permute-start | bytes 786440 | tf_op jit(solution)/shard_map/ppermute | solution.py:33
  136.5 9.3 %copy-start.5 = (bf16[2,256,128]{2,1,0:T(8,128)(2,1)S(1)}, bf16[2,256,128]{2,1,0:T(8,128)(2,1)}, u32[]{:S(2)}) copy-start(bf16[2,256,128]{2,1,0:T(8,128)(2,1)} %copy-done.4) | copy-start | bytes 393220
  143.7 14.8 %collective-permute-start.23 = (bf16[2,2,512,128]{3,2,1,0:T(8,128)(2,1)S(1)}, bf16[2,2,512,128]{3,2,1,0:T(8,128)(2,1)S(1)}, u32[]{:S(2)}, u32[]{:S(2)}) collective-permute-start(bf16[2,2,512,128]{3,2,1,0:T(8,128)(2,1)S(1)} %slice.95), channel_id=1, source_target_pairs={{0,192},{1,49},{2,194},{3,51},{4,196},{5,53},{6,198},{7,55},{8,200... | collective-permute-start | bytes 1572872 | tf_op jit(solution)/shard_map/ppermute | solution.py:33
  143.8 14.8 %collective-permute-start.22 = (bf16[2,2,512,128]{3,2,1,0:T(8,128)(2,1)S(1)}, bf16[2,2,512,128]{3,2,1,0:T(8,128)(2,1)S(1)}, u32[]{:S(2)}, u32[]{:S(2)}) collective-permute-start(bf16[2,2,512,128]{3,2,1,0:T(8,128)(2,1)S(1)} %slice.94), channel_id=1, source_target_pairs={{0,64},{1,17},{2,66},{3,19},{4,68},{5,21},{6,70},{7,23},{8,72},{9,... | collective-permute-start | bytes 1572872 | tf_op jit(solution)/shard_map/ppermute | solution.py:33
  145.8 12.7 %collective-permute-start.24 = (bf16[2,256,128]{2,1,0:T(8,128)(2,1)S(1)}, bf16[2,256,128]{2,1,0:T(8,128)(2,1)S(1)}, u32[]{:S(2)}, u32[]{:S(2)}) collective-permute-start(bf16[2,256,128]{2,1,0:T(8,128)(2,1)S(1)} %copy-done.5), channel_id=1, source_target_pairs={{0,248},{1,249},{2,250},{3,251},{4,252},{5,253},{6,254},{7,255},{8... | collective-permute-start | bytes 393224 | tf_op jit(solution)/shard_map/ppermute | solution.py:33
Sparse Core Ops, SparseCore 0:
  37.8 69.9 all-gather.1

commit v3 on v1

--- a/solution.py
+++ b/solution.py
@@ -214,7 +214,7 @@
     )(here, cot_t, activations, up_one, down_one)
 
 
-def adam_kernel(mine, theirs, master_in, first_in, second_in, new_master, moments, layer):
+def adam_kernel(mine, theirs, master_in, first_in, second_in, sent, layer, new_master):
     grad = (mine[...].astype(jnp.float32) + theirs[...].astype(jnp.float32)).T
     rows = grad.shape[0]
     width = grad.shape[1] // 2
@@ -226,11 +226,13 @@
         second = beta_two * second_in[at, :] + (1.0 - beta_two) * weight_grad * weight_grad
         first_hat = first / (1.0 - beta_one**step_number)
         second_hat = second / (1.0 - beta_two**step_number)
-        new_master[at, :] = master - learn_rate * (
+        new_master[at, :] = master = master - learn_rate * (
             first_hat / (jnp.sqrt(second_hat) + epsilon) + decay_rate * master
         )
-        moments[0, j] = first.astype(jnp.bfloat16)
-        moments[1, j] = second.astype(jnp.bfloat16)
+        sent[0, j] = first.astype(jnp.bfloat16)
+        sent[1, j] = second.astype(jnp.bfloat16)
+        sent[2, j] = master.astype(jnp.bfloat16)
+        sent[3, j] = (master - sent[2, j].astype(jnp.float32)).astype(jnp.bfloat16)
     layer[...] = new_master[...].astype(jnp.bfloat16)
 
 
@@ -239,10 +241,10 @@
     return pl.pallas_call(
         adam_kernel,
         out_shape=(
-            jax.ShapeDtypeStruct((rows, width), jnp.float32),
-            jax.ShapeDtypeStruct((2, 2, rows // 2, width), jnp.bfloat16),
+            jax.ShapeDtypeStruct((4, 2, rows // 2, width), jnp.bfloat16),
             jax.ShapeDtypeStruct((rows, width), jnp.bfloat16),
         ),
+        scratch_shapes=[pltpu.VMEM((rows, width), jnp.float32)],
         compiler_params=WIDE,
         cost_estimate=pl.CostEstimate(
             flops=20 * rows * width, bytes_accessed=30 * rows * width, transcendentals=2 * rows * width
@@ -283,6 +285,25 @@
     )(here, *sources, *held)
 
 
+def unpack_kernel(sent, master, first, second):
+    rows = sent.shape[2]
+    for j in range(2):
+        at = pl.ds(j, rows, stride=2)
+        first[at, :] = sent[0, j].astype(jnp.float32)
+        second[at, :] = sent[1, j].astype(jnp.float32)
+        master[at, :] = sent[2, j].astype(jnp.float32) + sent[3, j].astype(jnp.float32)
+
+
+def unpack(sent):
+    _, _, rows, width = sent.shape
+    return pl.pallas_call(
+        unpack_kernel,
+        out_shape=[jax.ShapeDtypeStruct((2 * rows, width), jnp.float32)] * 3,
+        compiler_params=WIDE,
+        cost_estimate=pl.CostEstimate(flops=0, bytes_accessed=10 * sent.size, transcendentals=0),
+    )(sent)
+
+
 def input_kernel(here, cot_mine, cot_theirs, params, out, total):
     step = pl.program_id(0)
     rows = params.shape[3]
@@ -323,7 +344,11 @@
             scratch_shapes=[pltpu.VMEM((tokens, 4 * rows), jnp.float32)],
         ),
         compiler_params=MOST,
-        cost_estimate=pl.CostEstimate(flops=0, bytes_accessed=0, transcendentals=0),
+        cost_estimate=pl.CostEstimate(
+            flops=16 * chips * tokens * columns * rows,
+            bytes_accessed=4 * chips * columns * (tokens + 2 * rows) + 8 * tokens * rows,
+            transcendentals=0,
+        ),
     )(here, cot_mine, cot_theirs, params)
 
 
@@ -379,33 +404,30 @@
     near = add(sums[0][0], *(g[0] for g in got))
     far, cot_theirs = tie(far, cot_theirs)
     state = [v.reshape(2 * rows, width) for v in (master_store, first_store, second_store)]
-    new_master, moments, layer = adam(near, move(far, other_half), *state)
+    sent, layer = adam(near, move(far, other_half), *state)
 
     layer_other = move(layer, other_half)
-    layer_other, moments = tie(layer_other, moments)
-    moments = move(moments, previous_block)
     pair = jnp.where(h == 0, jnp.stack([layer, layer_other]), jnp.stack([layer_other, layer]))
     from_up = move(pair, along_second(-1))
     from_down = move(pair, along_second(1))
     from_far = move(pair, along_second(2))
     four = jnp.stack([pair, from_up, from_far, from_down])
-    four, new_master = tie(four, new_master)
+    four, sent = tie(four, sent)
     four_down, four_up = move(four, along_first(1)), move(four, along_first(-1))
-    new_master = move(new_master, previous_block)
-    low, high, new_master = tie(four_down[:2], four_up[2:], new_master)
-    low_far, high_far = move(low, along_first(1)), move(high, along_first(-1))
+    sent = move(sent, previous_block)
     input_grad = input_matmul(here, cot_mine, cot_theirs, params)
+    four_down, four_up, input_grad = tie(four_down, four_up, input_grad)
+    low_far, high_far = move(four_down[:2], along_first(1)), move(four_up[2:], along_first(-1))
     new_layer = place(here, ((0, 0), (1, 0), (-1, 0)), [four, four_up, four_down], 32)
-    new_layer, input_grad = tie(new_layer, input_grad)
+    new_layer, sent = tie(new_layer, sent)
+    new_layer, *state = tie(new_layer, *unpack(sent))
     new_layer = place(here, ((2, 0), (2, 2)), [low_far, high_far], 32, new_layer)
-
-    shape = (rows, 2, width)
-    moments = moments.astype(jnp.float32).transpose(0, 2, 1, 3)
+    new_master, new_first, new_second = (v.reshape(rows, 2, width) for v in state)
     return (
         input_grad,
-        new_master.reshape(shape),
-        moments[0],
-        moments[1],
+        new_master,
+        new_first,
+        new_second,
         new_layer.reshape(32 * rows, 2, width),
     )
 

time: 162 us -> 156 us (0.963)
  the two profiles are of different devices: /device:TPU:32 before, /device:TPU:166 now
where the time goes in v3:
time: 156 us
  waiting for transfers between devices  70.4 us (45%)
  starting transfers between devices  40.5 us (26%)
  Pallas kernels  26.4 us (17%)
  between operations  14.3 us (9%)
  other arithmetic  2.85 us (2%)
    ppermute x23, waiting for transfers between devices, move(): return lax.ppermute(value, AXES, pairs)  70.4 us
    ppermute x23, starting transfers between devices, move(): return lax.ppermute(value, AXES, pairs)  40.4 us
    pallas_call x1, Pallas kernels, other_terms(): pl.pallas_call(functools.partial(other_kernel, groups), out_shape=[jax.Sh...  7.79 us
    pallas_call x1, Pallas kernels, input_matmul(): pl.pallas_call(input_kernel, out_shape=jax.ShapeDtypeStruct((tokens, 4 *...  6.96 us
    pallas_call x1, Pallas kernels, first_terms(): pl.pallas_call(functools.partial(first_kernel, groups), out_shape=[jax.Sh...  4.58 us
    pallas_call x2, Pallas kernels, place(): pl.pallas_call(functools.partial(place_kernel, groups), out_shape=jax.Sha...  4 us
  transfers between devices with their start and end apart: 24, of which 16 were waited for; matrix products, arithmetic and copies ran while one was open for 1% of the time, Pallas kernels for 13%

profile of v3, /device:TPU:166, one launch (start us, length us, event | category | flops | bytes accessed | tf_op | source)
XLA Modules:
  0.0 156.0 jit_solution(17724979025209541706)
XLA Ops:
  7.2 0.0 all-gather.2.cloned.1.call-start
  7.2 0.6 stack.87.here
  7.8 4.6 %shard_map.101 = (bf16[512,256]{1,0:T(8,128)(2,1)}, bf16[256,512]{1,0:T(8,128)(2,1)}, bf16[256,256]{1,0:T(8,128)(2,1)}, bf16[2,2,256,256]{3,2,1,0:T(8,128)(2,1)}, bf16[2,2,256,256]{3,2,1,0:T(8,128)(2,1)}) custom-call(s32[5]{0:T(128)} %stack.87.here, bf16[1024,128]{1,0:T(8,128)(2,1)} %bitcast.55, bf16[512,128]{1,0:T(8,128)(2,1)} %bitcast.63, ...), custom_call_target="tpu_custom_call" | custom-call | flops 536870912 | bytes 3932160 | tf_op jit(solution)/shard_map/pallas_call | solution.py:161
  12.4 0.6 collective-permute-start
  13.0 1.5 collective-permute-start.1
  14.5 1.0 collective-permute-start.4
  15.6 0.4 collective-permute-start.3
  15.9 5.0 %collective-permute-start.2 = (bf16[256,256]{1,0:T(8,128)(2,1)}, bf16[256,256]{1,0:T(8,128)(2,1)S(1)}, u32[]{:S(2)}, u32[]{:S(2)}) collective-permute-start(bf16[256,256]{1,0:T(8,128)(2,1)} %get-tuple-element.47), channel_id=1, source_target_pairs={{0,0},{1,32},{2,64},{3,96},{4,128},{5,160},{6,192},{7,224},{8,8},{... | collective-permute-start | bytes 393224 | tf_op jit(solution)/shard_map/ppermute | solution.py:33
  21.0 0.9 collective-permute-done.up_one
  21.9 1.7 %collective-permute-done.1.down_one = bf16[2,2,256,256]{3,2,1,0:T(8,128)(2,1)S(1)} collective-permute-done((bf16[2,2,256,256]{3,2,1,0:T(8,128)(2,1)}, bf16[2,2,256,256]{3,2,1,0:T(8,128)(2,1)S(1)}, u32[]{:S(2)}, u32[]{:S(2)}) %collective-permute-start.1) | collective-permute-done | bytes 524320 | tf_op jit(solution)/shard_map/ppermute | solution.py:33
  23.6 0.0 copy-done.5
  23.6 0.8 copy-done.6
  24.4 7.8 %shard_map.102 = (bf16[4,2,256,256]{3,2,1,0:T(8,128)(2,1)}, bf16[4,2,256,256]{3,2,1,0:T(8,128)(2,1)}, bf16[4,2,256,256]{3,2,1,0:T(8,128)(2,1)}) custom-call(s32[5]{0:T(128)} %stack.87.here, bf16[256,512]{1,0:T(8,128)(2,1)} %get-tuple-element.41.cot, bf16[512,8192]{1,0:T(8,128)(2,1)} %activations.3, bf16[2,2,256,256]{3,2,1,0:T(8,128)(2,1)} %copy-done.5, ...), custom_call_target="tpu_custom_call" | custom-call | flops 1610612736 | bytes 9699328 | tf_op jit(solution)/shard_map/pallas_call | solution.py:192
  32.2 0.0 collective-permute-done.3
  32.2 5.2 %collective-permute-done.2 = bf16[256,256]{1,0:T(8,128)(2,1)S(1)} collective-permute-done((bf16[256,256]{1,0:T(8,128)(2,1)}, bf16[256,256]{1,0:T(8,128)(2,1)S(1)}, u32[]{:S(2)}, u32[]{:S(2)}) %collective-permute-start.2) | collective-permute-done | bytes 131104 | tf_op jit(solution)/shard_map/ppermute | solution.py:33
  37.4 0.0 collective-permute-done.4
  37.5 0.7 maximum_select_fusion.2
  38.2 0.0 all-gather.2.cloned.1.call-update
  38.2 0.1 collective-permute-start.5
  38.3 2.0 %collective-permute-start.6 = (bf16[4,2,256,256]{3,2,1,0:T(8,128)(2,1)}, bf16[4,2,256,256]{3,2,1,0:T(8,128)(2,1)S(1)}, u32[]{:S(2)}, u32[]{:S(2)}) collective-permute-start(bf16[4,2,256,256]{3,2,1,0:T(8,128)(2,1)} %get-tuple-element.50), channel_id=1, source_target_pairs={{0,192},{1,49},{2,194},{3,51},{4,196},{5,53},{6,198},{7,55},{8,200... | collective-permute-start | bytes 3145736 | tf_op jit(solution)/shard_map/ppermute | solution.py:33
  40.3 0.0 collective-permute-start.8
  40.3 2.0 %collective-permute-start.7 = (bf16[512,256]{1,0:T(8,128)(2,1)S(1)}, bf16[512,256]{1,0:T(8,128)(2,1)S(1)}, u32[]{:S(2)}, u32[]{:S(2)}) collective-permute-start(bf16[512,256]{1,0:T(8,128)(2,1)S(1)} %collective-permute-done.4), channel_id=1, source_target_pairs={{0,2},{1,3},{2,4},{3,5},{4,6},{5,7},{6,0},{7,1},{8,10},{9,11},{10,... | collective-permute-start | bytes 786440 | tf_op jit(solution)/shard_map/ppermute | solution.py:33
  42.3 11.0 %collective-permute-done.5 = bf16[4,2,256,256]{3,2,1,0:T(8,128)(2,1)S(1)} collective-permute-done((bf16[4,2,256,256]{3,2,1,0:T(8,128)(2,1)}, bf16[4,2,256,256]{3,2,1,0:T(8,128)(2,1)S(1)}, u32[]{:S(2)}, u32[]{:S(2)}) %collective-permute-start.5) | collective-permute-done | bytes 1048608 | tf_op jit(solution)/shard_map/ppermute | solution.py:33
  53.3 1.3 collective-permute-done.6
  54.6 1.7 %add_convert_fusion.3 = (bf16[1,2,256,256]{3,2,1,0:T(8,128)(2,1)S(1)}, bf16[2,256,256]{2,1,0:T(8,128)(2,1)S(1)}, bf16[2,256,256]{2,1,0:T(8,128)(2,1)S(1)}, bf16[2,256,256]{2,1,0:T(8,128)(2,1)S(1)}) fusion(bf16[4,2,256,256]{3,2,1,0:T(8,128)(2,1)S(1)} %collective-permute-done.6, bf16[4,2,256,256]{3,2,1,0:T(8,128)(2,1)S(1)} %collective-permute-done.5, ...), kind=kLoop, calls=%fused_computation.5 | loop fusion | flops 3145728 | bytes 4194304 | tf_op jit(solution)/shard_map/convert_element_type | solution.py:359
  56.3 0.0 collective-permute-done.8
  56.3 0.0 collective-permute-done.7
  56.3 0.1 pad_maximum_fusion.cot_mine
  56.4 0.0 copy-start.4
  56.4 0.1 collective-permute-start.12
  56.5 1.4 collective-permute-start.9
  57.9 10.6 %collective-permute-start.10 = (bf16[2,256,256]{2,1,0:T(8,128)(2,1)S(1)}, bf16[2,256,256]{2,1,0:T(8,128)(2,1)S(1)}, u32[]{:S(2)}, u32[]{:S(2)}) collective-permute-start(bf16[2,256,256]{2,1,0:T(8,128)(2,1)S(1)} %get-tuple-element.53), channel_id=1, source_target_pairs={{0,48},{1,193},{2,50},{3,195},{4,52},{5,197},{6,54},{7,199},{8,56}... | collective-permute-start | bytes 786440 | tf_op jit(solution)/shard_map/ppermute | solution.py:33
  68.6 2.0 %collective-permute-start.11 = (bf16[2,256,256]{2,1,0:T(8,128)(2,1)S(1)}, bf16[2,256,256]{2,1,0:T(8,128)(2,1)S(1)}, u32[]{:S(2)}, u32[]{:S(2)}) collective-permute-start(bf16[2,256,256]{2,1,0:T(8,128)(2,1)S(1)} %get-tuple-element.54), channel_id=1, source_target_pairs={{0,32},{1,129},{2,34},{3,131},{4,36},{5,133},{6,38},{7,135},{8,40}... | collective-permute-start | bytes 786440 | tf_op jit(solution)/shard_map/ppermute | solution.py:33
  70.5 2.3 %collective-permute-done.9 = bf16[2,256,256]{2,1,0:T(8,128)(2,1)S(1)} collective-permute-done((bf16[2,256,256]{2,1,0:T(8,128)(2,1)S(1)}, bf16[2,256,256]{2,1,0:T(8,128)(2,1)S(1)}, u32[]{:S(2)}, u32[]{:S(2)}) %collective-permute-start.9) | collective-permute-done | bytes 262176 | tf_op jit(solution)/shard_map/ppermute | solution.py:33
  72.8 2.5 %collective-permute-done.10 = bf16[2,256,256]{2,1,0:T(8,128)(2,1)S(1)} collective-permute-done((bf16[2,256,256]{2,1,0:T(8,128)(2,1)S(1)}, bf16[2,256,256]{2,1,0:T(8,128)(2,1)S(1)}, u32[]{:S(2)}, u32[]{:S(2)}) %collective-permute-start.10) | collective-permute-done | bytes 262176 | tf_op jit(solution)/shard_map/ppermute | solution.py:33
  75.3 1.8 %collective-permute-done.11 = bf16[2,256,256]{2,1,0:T(8,128)(2,1)S(1)} collective-permute-done((bf16[2,256,256]{2,1,0:T(8,128)(2,1)S(1)}, bf16[2,256,256]{2,1,0:T(8,128)(2,1)S(1)}, u32[]{:S(2)}, u32[]{:S(2)}) %collective-permute-start.11) | collective-permute-done | bytes 262176 | tf_op jit(solution)/shard_map/ppermute | solution.py:33
  77.1 0.1 fusion.10
  77.2 0.0 collective-permute-done.12.cot_theirs
  77.2 0.3 collective-permute-start.13
  77.5 10.0 %collective-permute-done.13.theirs = bf16[256,256]{1,0:T(8,128)(2,1)S(1)} collective-permute-done((bf16[256,256]{1,0:T(8,128)(2,1)S(1)}, bf16[256,256]{1,0:T(8,128)(2,1)S(1)}, u32[]{:S(2)}, u32[]{:S(2)}) %collective-permute-start.13) | collective-permute-done | bytes 131104 | tf_op jit(solution)/shard_map/ppermute | solution.py:33
  87.6 1.1 shard_map.103
  88.7 0.0 collective-permute-start.14
  88.7 8.9 %collective-permute-done.14 = bf16[512,128]{1,0:T(8,128)(2,1)S(1)} collective-permute-done((bf16[512,128]{1,0:T(8,128)(2,1)S(1)}, bf16[512,128]{1,0:T(8,128)(2,1)S(1)}, u32[]{:S(2)}, u32[]{:S(2)}) %collective-permute-start.14) | collective-permute-done | bytes 131104 | tf_op jit(solution)/shard_map/ppermute | solution.py:33
  97.6 4.1 %collective-permute-start.17 = (bf16[2,512,128]{2,1,0:T(8,128)(2,1)S(1)}, bf16[2,512,128]{2,1,0:T(8,128)(2,1)S(1)}, u32[]{:S(2)}, u32[]{:S(2)}) collective-permute-start(bf16[2,512,128]{2,1,0:T(8,128)(2,1)S(1)} %maximum_select_fusion.1), channel_id=1, source_target_pairs={{0,16},{1,65},{2,18},{3,67},{4,20},{5,69},{6,22},{7,71},{8,24},{9,... | collective-permute-start | bytes 786440 | tf_op jit(solution)/shard_map/ppermute | solution.py:33
  101.8 0.0 collective-permute-start.16
  101.8 2.8 %collective-permute-start.15 = (bf16[2,512,128]{2,1,0:T(8,128)(2,1)S(1)}, bf16[2,512,128]{2,1,0:T(8,128)(2,1)S(1)}, u32[]{:S(2)}, u32[]{:S(2)}) collective-permute-start(bf16[2,512,128]{2,1,0:T(8,128)(2,1)S(1)} %maximum_select_fusion.1), channel_id=1, source_target_pairs={{0,48},{1,193},{2,50},{3,195},{4,52},{5,197},{6,54},{7,199},{8,56}... | collective-permute-start | bytes 786440 | tf_op jit(solution)/shard_map/ppermute | solution.py:33
  104.6 1.1 collective-permute-done.17
  105.7 4.0 %collective-permute-done.16 = bf16[2,512,128]{2,1,0:T(8,128)(2,1)S(1)} collective-permute-done((bf16[2,512,128]{2,1,0:T(8,128)(2,1)S(1)}, bf16[2,512,128]{2,1,0:T(8,128)(2,1)S(1)}, u32[]{:S(2)}, u32[]{:S(2)}) %collective-permute-start.16) | collective-permute-done | bytes 262176 | tf_op jit(solution)/shard_map/ppermute | solution.py:33
  109.7 0.1 collective-permute-done.15
  109.7 0.1 pad_maximum_fusion.1.refs_0_
  109.9 0.1 collective-permute-start.19
  110.0 3.2 %collective-permute-start.18 = (bf16[4,2,512,128]{3,2,1,0:T(8,128)(2,1)S(1)}, bf16[4,2,512,128]{3,2,1,0:T(8,128)(2,1)S(1)}, u32[]{:S(2)}, u32[]{:S(2)}) collective-permute-start(bf16[4,2,512,128]{3,2,1,0:T(8,128)(2,1)S(1)} %pad_maximum_fusion.1.refs_0_), channel_id=1, source_target_pairs={{0,64},{1,17},{2,66},{3,19},{4,68},{5,21},{6,70},{7,23},{8,72},{9,... | collective-permute-start | bytes 3145736 | tf_op jit(solution)/shard_map/ppermute | solution.py:33
  113.2 0.0 collective-permute-start.20
  113.2 7.0 %shard_map.104 = bf16[512,1024]{1,0:T(8,128)(2,1)} custom-call(s32[5]{0:T(128)} %stack.87.here, bf16[4,512,256]{2,1,0:T(8,128)(2,1)} %copy-done.4, bf16[4,512,256]{2,1,0:T(8,128)(2,1)} %copy-done.8, bf16[16,2,256,256]{3,2,1,0:T(8,128)(2,1)} %all-gather.2.cloned.1.call-done.params), custom_call_target="tpu_custom_call" | custom-call | flops 2147483648 | bytes 5242880 | tf_op jit(solution)/shard_map/pallas_call | solution.py:332
  120.2 5.9 %collective-permute-done.19.refs_1_ = bf16[4,2,512,128]{3,2,1,0:T(8,128)(2,1)S(1)} collective-permute-done((bf16[4,2,512,128]{3,2,1,0:T(8,128)(2,1)S(1)}, bf16[4,2,512,128]{3,2,1,0:T(8,128)(2,1)S(1)}, u32[]{:S(2)}, u32[]{:S(2)}) %collective-permute-start.19) | collective-permute-done | bytes 1048608 | tf_op jit(solution)/shard_map/ppermute | solution.py:33
  126.1 0.0 collective-permute-done.18.refs_2_
  126.2 3.2 %collective-permute-start.21 = (bf16[2,2,512,128]{3,2,1,0:T(8,128)(2,1)S(1)}, bf16[2,2,512,128]{3,2,1,0:T(8,128)(2,1)S(1)}, u32[]{:S(2)}, u32[]{:S(2)}) collective-permute-start(bf16[2,2,512,128]{3,2,1,0:T(8,128)(2,1)S(1)} %slice.94), channel_id=1, source_target_pairs={{0,64},{1,17},{2,66},{3,19},{4,68},{5,21},{6,70},{7,23},{8,72},{9,... | collective-permute-start | bytes 1572872 | tf_op jit(solution)/shard_map/ppermute | solution.py:33
  129.4 0.0 collective-permute-start.22
  129.4 2.4 %shard_map.105.refs_2_ = bf16[32,512,128]{2,1,0:T(8,128)(2,1)} custom-call(s32[5]{0:T(128)S(1)} %copy-done.3, bf16[4,2,512,128]{3,2,1,0:T(8,128)(2,1)S(1)} %pad_maximum_fusion.1.refs_0_, bf16[4,2,512,128]{3,2,1,0:T(8,128)(2,1)S(1)} %collective-permute-done.19.refs_1_, bf16[4,2,512,128]{3,2,1,0:T(8,128)(2,1)S(1)} %collective-permute-done.18.refs_2_), custom_call_target="tpu_custom_call" | custom-call | tf_op jit(solution)/shard_map/pallas_call | solution.py:274
  131.8 6.8 %collective-permute-done.20.sent = bf16[4,2,256,128]{3,2,1,0:T(8,128)(2,1)} collective-permute-done((bf16[4,2,256,128]{3,2,1,0:T(8,128)(2,1)}, bf16[4,2,256,128]{3,2,1,0:T(8,128)(2,1)}, u32[]{:S(2)}, u32[]{:S(2)}) %collective-permute-start.20) | collective-permute-done | bytes 524320 | tf_op jit(solution)/shard_map/ppermute | solution.py:33
  138.6 1.9 %shard_map.106 = (f32[512,128]{1,0:T(8,128)}, f32[512,128]{1,0:T(8,128)}, f32[512,128]{1,0:T(8,128)}) custom-call(bf16[4,2,256,128]{3,2,1,0:T(8,128)(2,1)} %collective-permute-done.20.sent), custom_call_target="tpu_custom_call" | custom-call | bytes 2621440 | tf_op jit(solution)/shard_map/pallas_call | solution.py:299
  140.5 0.0 collective-permute-done.21.refs_0_
  140.5 7.0 %collective-permute-done.22.refs_1_ = bf16[2,2,512,128]{3,2,1,0:T(8,128)(2,1)S(1)} collective-permute-done((bf16[2,2,512,128]{3,2,1,0:T(8,128)(2,1)S(1)}, bf16[2,2,512,128]{3,2,1,0:T(8,128)(2,1)S(1)}, u32[]{:S(2)}, u32[]{:S(2)}) %collective-permute-start.22) | collective-permute-done | bytes 524320 | tf_op jit(solution)/shard_map/ppermute | solution.py:33
  147.5 1.6 %shard_map.107 = bf16[32,512,128]{2,1,0:T(8,128)(2,1)} custom-call(s32[5]{0:T(128)S(1)} %copy-done.3, bf16[2,2,512,128]{3,2,1,0:T(8,128)(2,1)S(1)} %collective-permute-done.21.refs_0_, bf16[2,2,512,128]{3,2,1,0:T(8,128)(2,1)S(1)} %collective-permute-done.22.refs_1_, bf16[32,512,128]{2,1,0:T(8,128)(2,1)} %shard_map.105.refs_2_), custom_call_target="tpu_custom_call", output_to_operand_aliasing={{}: (3, {})} | custom-call | tf_op jit(solution)/shard_map/pallas_call | solution.py:274
  (20 shorter events, 0.2 us)
Async XLA Ops:
  7.2 106.0 %all-gather.2.cloned.1.call-start = ((), (), s32[]{:S(2)}) async-start(), calls=%async_computation | async-start | bytes 4456448 | tf_op jit(solution)/shard_map/all_gather | solution.py:391
  12.4 9.5 %collective-permute-start = (bf16[2,2,256,256]{3,2,1,0:T(8,128)(2,1)}, bf16[2,2,256,256]{3,2,1,0:T(8,128)(2,1)S(1)}, u32[]{:S(2)}, u32[]{:S(2)}) collective-permute-start(bf16[2,2,256,256]{3,2,1,0:T(8,128)(2,1)} %get-tuple-element.42), channel_id=1, source_target_pairs={{0,64},{1,17},{2,66},{3,19},{4,68},{5,21},{6,70},{7,23},{8,72},{9,... | collective-permute-start | bytes 1572872 | tf_op jit(solution)/shard_map/ppermute | solution.py:33
  13.0 10.6 %collective-permute-start.1 = (bf16[2,2,256,256]{3,2,1,0:T(8,128)(2,1)}, bf16[2,2,256,256]{3,2,1,0:T(8,128)(2,1)S(1)}, u32[]{:S(2)}, u32[]{:S(2)}) collective-permute-start(bf16[2,2,256,256]{3,2,1,0:T(8,128)(2,1)} %get-tuple-element.43), channel_id=1, source_target_pairs={{0,192},{1,49},{2,194},{3,51},{4,196},{5,53},{6,198},{7,55},{8,200... | collective-permute-start | bytes 1572872 | tf_op jit(solution)/shard_map/ppermute | solution.py:33
  14.5 22.9 %collective-permute-start.4 = (bf16[512,256]{1,0:T(8,128)(2,1)}, bf16[512,256]{1,0:T(8,128)(2,1)S(1)}, u32[]{:S(2)}, u32[]{:S(2)}) collective-permute-start(bf16[512,256]{1,0:T(8,128)(2,1)} %get-tuple-element.48), channel_id=1, source_target_pairs={{0,2},{1,3},{2,4},{3,5},{4,6},{5,7},{6,0},{7,1},{8,10},{9,11},{10,... | collective-permute-start | bytes 786440 | tf_op jit(solution)/shard_map/ppermute | solution.py:33
  15.6 16.6 %collective-permute-start.3 = (bf16[256,256]{1,0:T(8,128)(2,1)}, bf16[256,256]{1,0:T(8,128)(2,1)S(1)}, u32[]{:S(2)}, u32[]{:S(2)}) collective-permute-start(bf16[256,256]{1,0:T(8,128)(2,1)} %get-tuple-element.47), channel_id=1, source_target_pairs={{0,8},{1,40},{2,72},{3,104},{4,136},{5,168},{6,200},{7,232},{8,0},... | collective-permute-start | bytes 393224 | tf_op jit(solution)/shard_map/ppermute | solution.py:33
  15.9 21.5 %collective-permute-start.2 = (bf16[256,256]{1,0:T(8,128)(2,1)}, bf16[256,256]{1,0:T(8,128)(2,1)S(1)}, u32[]{:S(2)}, u32[]{:S(2)}) collective-permute-start(bf16[256,256]{1,0:T(8,128)(2,1)} %get-tuple-element.47), channel_id=1, source_target_pairs={{0,0},{1,32},{2,64},{3,96},{4,128},{5,160},{6,192},{7,224},{8,8},{... | collective-permute-start | bytes 393224 | tf_op jit(solution)/shard_map/ppermute | solution.py:33
  21.9 1.7 %copy-start.5 = (bf16[2,2,256,256]{3,2,1,0:T(8,128)(2,1)}, bf16[2,2,256,256]{3,2,1,0:T(8,128)(2,1)S(1)}, u32[]{:S(2)}) copy-start(bf16[2,2,256,256]{3,2,1,0:T(8,128)(2,1)S(1)} %collective-permute-done.up_one) | copy-start | bytes 1572868
  23.6 0.8 copy-start.6
  24.4 15.9 %copy-start.7 = (bf16[512,256]{1,0:T(8,128)(2,1)S(1)}, bf16[512,256]{1,0:T(8,128)(2,1)}, u32[]{:S(2)}) copy-start(bf16[512,256]{1,0:T(8,128)(2,1)} %get-tuple-element.48) | copy-start | bytes 786436
  37.4 50.1 %copy-start = (f32[256,2,128]{2,1,0:T(2,128)S(1)}, f32[256,2,128]{2,1,0:T(2,128)}, u32[]{:S(2)}) copy-start(f32[256,2,128]{2,1,0:T(2,128)} %param.9) | copy-start | bytes 786436
  37.4 50.1 %copy-start.1 = (f32[256,2,128]{2,1,0:T(2,128)S(1)}, f32[256,2,128]{2,1,0:T(2,128)}, u32[]{:S(2)}) copy-start(f32[256,2,128]{2,1,0:T(2,128)} %param.10) | copy-start | bytes 786436
  37.4 50.1 %copy-start.2 = (f32[256,2,128]{2,1,0:T(2,128)S(1)}, f32[256,2,128]{2,1,0:T(2,128)}, u32[]{:S(2)}) copy-start(f32[256,2,128]{2,1,0:T(2,128)} %param.11) | copy-start | bytes 786436
  38.2 15.1 %collective-permute-start.5 = (bf16[4,2,256,256]{3,2,1,0:T(8,128)(2,1)}, bf16[4,2,256,256]{3,2,1,0:T(8,128)(2,1)S(1)}, u32[]{:S(2)}, u32[]{:S(2)}) collective-permute-start(bf16[4,2,256,256]{3,2,1,0:T(8,128)(2,1)} %get-tuple-element.49), channel_id=1, source_target_pairs={{0,64},{1,17},{2,66},{3,19},{4,68},{5,21},{6,70},{7,23},{8,72},{9,... | collective-permute-start | bytes 3145736 | tf_op jit(solution)/shard_map/ppermute | solution.py:33
  38.3 16.3 %collective-permute-start.6 = (bf16[4,2,256,256]{3,2,1,0:T(8,128)(2,1)}, bf16[4,2,256,256]{3,2,1,0:T(8,128)(2,1)S(1)}, u32[]{:S(2)}, u32[]{:S(2)}) collective-permute-start(bf16[4,2,256,256]{3,2,1,0:T(8,128)(2,1)} %get-tuple-element.50), channel_id=1, source_target_pairs={{0,192},{1,49},{2,194},{3,51},{4,196},{5,53},{6,198},{7,55},{8,200... | collective-permute-start | bytes 3145736 | tf_op jit(solution)/shard_map/ppermute | solution.py:33
  40.3 15.9 %collective-permute-start.8 = (bf16[512,256]{1,0:T(8,128)(2,1)S(1)}, bf16[512,256]{1,0:T(8,128)(2,1)S(1)}, u32[]{:S(2)}, u32[]{:S(2)}) collective-permute-start(bf16[512,256]{1,0:T(8,128)(2,1)S(1)} %copy-done.7), channel_id=1, source_target_pairs={{0,6},{1,7},{2,0},{3,1},{4,2},{5,3},{6,4},{7,5},{8,14},{9,15},{10,... | collective-permute-start | bytes 786440 | tf_op jit(solution)/shard_map/ppermute | solution.py:33
  40.3 16.0 %collective-permute-start.7 = (bf16[512,256]{1,0:T(8,128)(2,1)S(1)}, bf16[512,256]{1,0:T(8,128)(2,1)S(1)}, u32[]{:S(2)}, u32[]{:S(2)}) collective-permute-start(bf16[512,256]{1,0:T(8,128)(2,1)S(1)} %collective-permute-done.4), channel_id=1, source_target_pairs={{0,2},{1,3},{2,4},{3,5},{4,6},{5,7},{6,0},{7,1},{8,10},{9,11},{10,... | collective-permute-start | bytes 786440 | tf_op jit(solution)/shard_map/ppermute | solution.py:33
  56.4 31.1 %copy-start.4 = (bf16[4,512,256]{2,1,0:T(8,128)(2,1)}, bf16[4,512,256]{2,1,0:T(8,128)(2,1)S(1)}, u32[]{:S(2)}) copy-start(bf16[4,512,256]{2,1,0:T(8,128)(2,1)S(1)} %pad_maximum_fusion.cot_mine) | copy-start | bytes 3145732
  56.4 20.8 %collective-permute-start.12 = (bf16[4,512,256]{2,1,0:T(8,128)(2,1)S(1)}, bf16[4,512,256]{2,1,0:T(8,128)(2,1)S(1)}, u32[]{:S(2)}, u32[]{:S(2)}) collective-permute-start(bf16[4,512,256]{2,1,0:T(8,128)(2,1)S(1)} %pad_maximum_fusion.cot_mine), channel_id=1, source_target_pairs={{0,1},{1,0},{2,3},{3,2},{4,5},{5,4},{6,7},{7,6},{8,9},{9,8},{10,11... | collective-permute-start | bytes 3145736 | tf_op jit(solution)/shard_map/ppermute | solution.py:33
  56.5 16.3 %collective-permute-start.9 = (bf16[2,256,256]{2,1,0:T(8,128)(2,1)S(1)}, bf16[2,256,256]{2,1,0:T(8,128)(2,1)S(1)}, u32[]{:S(2)}, u32[]{:S(2)}) collective-permute-start(bf16[2,256,256]{2,1,0:T(8,128)(2,1)S(1)} %get-tuple-element.52), channel_id=1, source_target_pairs={{0,16},{1,65},{2,18},{3,67},{4,20},{5,69},{6,22},{7,71},{8,24},{9,... | collective-permute-start | bytes 786440 | tf_op jit(solution)/shard_map/ppermute | solution.py:33
  57.9 17.4 %collective-permute-start.10 = (bf16[2,256,256]{2,1,0:T(8,128)(2,1)S(1)}, bf16[2,256,256]{2,1,0:T(8,128)(2,1)S(1)}, u32[]{:S(2)}, u32[]{:S(2)}) collective-permute-start(bf16[2,256,256]{2,1,0:T(8,128)(2,1)S(1)} %get-tuple-element.53), channel_id=1, source_target_pairs={{0,48},{1,193},{2,50},{3,195},{4,52},{5,197},{6,54},{7,199},{8,56}... | collective-permute-start | bytes 786440 | tf_op jit(solution)/shard_map/ppermute | solution.py:33
  68.6 8.5 %collective-permute-start.11 = (bf16[2,256,256]{2,1,0:T(8,128)(2,1)S(1)}, bf16[2,256,256]{2,1,0:T(8,128)(2,1)S(1)}, u32[]{:S(2)}, u32[]{:S(2)}) collective-permute-start(bf16[2,256,256]{2,1,0:T(8,128)(2,1)S(1)} %get-tuple-element.54), channel_id=1, source_target_pairs={{0,32},{1,129},{2,34},{3,131},{4,36},{5,133},{6,38},{7,135},{8,40}... | collective-permute-start | bytes 786440 | tf_op jit(solution)/shard_map/ppermute | solution.py:33
  77.2 10.3 %copy-start.8 = (bf16[4,512,256]{2,1,0:T(8,128)(2,1)}, bf16[4,512,256]{2,1,0:T(8,128)(2,1)S(1)}, u32[]{:S(2)}) copy-start(bf16[4,512,256]{2,1,0:T(8,128)(2,1)S(1)} %collective-permute-done.12.cot_theirs) | copy-start | bytes 3145732
  77.2 10.3 %collective-permute-start.13 = (bf16[256,256]{1,0:T(8,128)(2,1)S(1)}, bf16[256,256]{1,0:T(8,128)(2,1)S(1)}, u32[]{:S(2)}, u32[]{:S(2)}) collective-permute-start(bf16[256,256]{1,0:T(8,128)(2,1)S(1)} %get-tuple-element.57), channel_id=1, source_target_pairs={{0,8},{1,9},{2,10},{3,11},{4,12},{5,13},{6,14},{7,15},{8,0},{9,1},... | collective-permute-start | bytes 393224 | tf_op jit(solution)/shard_map/ppermute | solution.py:33
  88.7 8.9 %collective-permute-start.14 = (bf16[512,128]{1,0:T(8,128)(2,1)S(1)}, bf16[512,128]{1,0:T(8,128)(2,1)S(1)}, u32[]{:S(2)}, u32[]{:S(2)}) collective-permute-start(bf16[512,128]{1,0:T(8,128)(2,1)S(1)} %get-tuple-element.58), channel_id=1, source_target_pairs={{0,8},{1,9},{2,10},{3,11},{4,12},{5,13},{6,14},{7,15},{8,0},{9,1},... | collective-permute-start | bytes 393224 | tf_op jit(solution)/shard_map/ppermute | solution.py:33
  97.6 8.0 %collective-permute-start.17 = (bf16[2,512,128]{2,1,0:T(8,128)(2,1)S(1)}, bf16[2,512,128]{2,1,0:T(8,128)(2,1)S(1)}, u32[]{:S(2)}, u32[]{:S(2)}) collective-permute-start(bf16[2,512,128]{2,1,0:T(8,128)(2,1)S(1)} %maximum_select_fusion.1), channel_id=1, source_target_pairs={{0,16},{1,65},{2,18},{3,67},{4,20},{5,69},{6,22},{7,71},{8,24},{9,... | collective-permute-start | bytes 786440 | tf_op jit(solution)/shard_map/ppermute | solution.py:33
  101.8 7.9 %collective-permute-start.16 = (bf16[2,512,128]{2,1,0:T(8,128)(2,1)S(1)}, bf16[2,512,128]{2,1,0:T(8,128)(2,1)S(1)}, u32[]{:S(2)}, u32[]{:S(2)}) collective-permute-start(bf16[2,512,128]{2,1,0:T(8,128)(2,1)S(1)} %maximum_select_fusion.1), channel_id=1, source_target_pairs={{0,32},{1,129},{2,34},{3,131},{4,36},{5,133},{6,38},{7,135},{8,40}... | collective-permute-start | bytes 786440 | tf_op jit(solution)/shard_map/ppermute | solution.py:33
  101.8 8.0 %collective-permute-start.15 = (bf16[2,512,128]{2,1,0:T(8,128)(2,1)S(1)}, bf16[2,512,128]{2,1,0:T(8,128)(2,1)S(1)}, u32[]{:S(2)}, u32[]{:S(2)}) collective-permute-start(bf16[2,512,128]{2,1,0:T(8,128)(2,1)S(1)} %maximum_select_fusion.1), channel_id=1, source_target_pairs={{0,48},{1,193},{2,50},{3,195},{4,52},{5,197},{6,54},{7,199},{8,56}... | collective-permute-start | bytes 786440 | tf_op jit(solution)/shard_map/ppermute | solution.py:33
  109.9 19.5 %copy-start.3 = (s32[5]{0:T(128)S(1)}, s32[5]{0:T(128)}, u32[]{:S(2)}) copy-start(s32[5]{0:T(128)} %stack.87.here) | copy-start | bytes 64
  109.9 16.2 %collective-permute-start.19 = (bf16[4,2,512,128]{3,2,1,0:T(8,128)(2,1)S(1)}, bf16[4,2,512,128]{3,2,1,0:T(8,128)(2,1)S(1)}, u32[]{:S(2)}, u32[]{:S(2)}) collective-permute-start(bf16[4,2,512,128]{3,2,1,0:T(8,128)(2,1)S(1)} %pad_maximum_fusion.1.refs_0_), channel_id=1, source_target_pairs={{0,192},{1,49},{2,194},{3,51},{4,196},{5,53},{6,198},{7,55},{8,200... | collective-permute-start | bytes 3145736 | tf_op jit(solution)/shard_map/ppermute | solution.py:33
  110.0 16.1 %collective-permute-start.18 = (bf16[4,2,512,128]{3,2,1,0:T(8,128)(2,1)S(1)}, bf16[4,2,512,128]{3,2,1,0:T(8,128)(2,1)S(1)}, u32[]{:S(2)}, u32[]{:S(2)}) collective-permute-start(bf16[4,2,512,128]{3,2,1,0:T(8,128)(2,1)S(1)} %pad_maximum_fusion.1.refs_0_), channel_id=1, source_target_pairs={{0,64},{1,17},{2,66},{3,19},{4,68},{5,21},{6,70},{7,23},{8,72},{9,... | collective-permute-start | bytes 3145736 | tf_op jit(solution)/shard_map/ppermute | solution.py:33
  113.2 25.4 %collective-permute-start.20 = (bf16[4,2,256,128]{3,2,1,0:T(8,128)(2,1)}, bf16[4,2,256,128]{3,2,1,0:T(8,128)(2,1)}, u32[]{:S(2)}, u32[]{:S(2)}) collective-permute-start(bf16[4,2,256,128]{3,2,1,0:T(8,128)(2,1)} %get-tuple-element.67), channel_id=1, source_target_pairs={{0,248},{1,249},{2,250},{3,251},{4,252},{5,253},{6,254},{7,255},{8... | collective-permute-start | bytes 1572872 | tf_op jit(solution)/shard_map/ppermute | solution.py:33
  126.2 14.4 %collective-permute-start.21 = (bf16[2,2,512,128]{3,2,1,0:T(8,128)(2,1)S(1)}, bf16[2,2,512,128]{3,2,1,0:T(8,128)(2,1)S(1)}, u32[]{:S(2)}, u32[]{:S(2)}) collective-permute-start(bf16[2,2,512,128]{3,2,1,0:T(8,128)(2,1)S(1)} %slice.94), channel_id=1, source_target_pairs={{0,64},{1,17},{2,66},{3,19},{4,68},{5,21},{6,70},{7,23},{8,72},{9,... | collective-permute-start | bytes 1572872 | tf_op jit(solution)/shard_map/ppermute | solution.py:33
  129.4 18.2 %collective-permute-start.22 = (bf16[2,2,512,128]{3,2,1,0:T(8,128)(2,1)S(1)}, bf16[2,2,512,128]{3,2,1,0:T(8,128)(2,1)S(1)}, u32[]{:S(2)}, u32[]{:S(2)}) collective-permute-start(bf16[2,2,512,128]{3,2,1,0:T(8,128)(2,1)S(1)} %slice.95), channel_id=1, source_target_pairs={{0,192},{1,49},{2,194},{3,51},{4,196},{5,53},{6,198},{7,55},{8,200... | collective-permute-start | bytes 1572872 | tf_op jit(solution)/shard_map/ppermute | solution.py:33
Sparse Core Ops, SparseCore 0:
  38.3 67.2 all-gather.1

commit v4 on v3

--- a/solution.py
+++ b/solution.py
@@ -411,14 +411,21 @@
     from_up = move(pair, along_second(-1))
     from_down = move(pair, along_second(1))
     from_far = move(pair, along_second(2))
-    four = jnp.stack([pair, from_up, from_far, from_down])
-    four, sent = tie(four, sent)
-    four_down, four_up = move(four, along_first(1)), move(four, along_first(-1))
+    low, high = jnp.stack([pair, from_up]), jnp.stack([from_far, from_down])
+    low, high, sent = tie(low, high, sent)
+    low_down, high_up = move(low, along_first(1)), move(high, along_first(-1))
+    high_down, low_up = move(high, along_first(1)), move(low, along_first(-1))
     sent = move(sent, previous_block)
+    low_down, high_up = tie(low_down, high_up)
+    low_far, high_far = move(low_down, along_first(1)), move(high_up, along_first(-1))
     input_grad = input_matmul(here, cot_mine, cot_theirs, params)
-    four_down, four_up, input_grad = tie(four_down, four_up, input_grad)
-    low_far, high_far = move(four_down[:2], along_first(1)), move(four_up[2:], along_first(-1))
-    new_layer = place(here, ((0, 0), (1, 0), (-1, 0)), [four, four_up, four_down], 32)
+    low_up, high_down, input_grad = tie(low_up, high_down, input_grad)
+    new_layer = place(
+        here,
+        ((0, 0), (0, 2), (1, 0), (1, 2), (-1, 0), (-1, 2)),
+        [low, high, low_up, high_up, low_down, high_down],
+        32,
+    )
     new_layer, sent = tie(new_layer, sent)
     new_layer, *state = tie(new_layer, *unpack(sent))
     new_layer = place(here, ((2, 0), (2, 2)), [low_far, high_far], 32, new_layer)

time: 156 us -> 154 us (0.987)
  the two profiles are of different devices: /device:TPU:166 before, /device:TPU:32 now
where the time goes in v4:
time: 154 us; the launch traced here: 153 us
  starting transfers between devices  65.3 us (42%)
  waiting for transfers between devices  42.6 us (28%)
  Pallas kernels  26.2 us (17%)
  between operations  14.3 us (9%)
  other arithmetic  2.77 us (2%)
  local copies, waits for them, and re-layouts  1.66 us (1%)
    ppermute x25, starting transfers between devices, move(): return lax.ppermute(value, AXES, pairs)  65.3 us
    ppermute x25, waiting for transfers between devices, move(): return lax.ppermute(value, AXES, pairs)  42.6 us
    pallas_call x1, Pallas kernels, other_terms(): pl.pallas_call(functools.partial(other_kernel, groups), out_shape=[jax.Sh...  7.79 us
    pallas_call x1, Pallas kernels, input_matmul(): pl.pallas_call(input_kernel, out_shape=jax.ShapeDtypeStruct((tokens, 4 *...  6.96 us
    pallas_call x2, Pallas kernels, place(): pl.pallas_call(functools.partial(place_kernel, groups), out_shape=jax.Sha...  4.83 us
    pallas_call x1, Pallas kernels, first_terms(): pl.pallas_call(functools.partial(first_kernel, groups), out_shape=[jax.Sh...  4.59 us
  transfers between devices with their start and end apart: 26, of which 11 were waited for; matrix products, arithmetic and copies ran while one was open for 1% of the time, Pallas kernels for 13%

profile of v4, /device:TPU:32, one launch (start us, length us, event | category | flops | bytes accessed | tf_op | source)
XLA Modules:
  0.0 152.9 jit_solution(18248046394736985350)
XLA Ops:
  7.2 0.0 all-gather.2.cloned.1.call-start
  7.2 0.7 stack.90.here
  7.9 4.6 %shard_map.101 = (bf16[512,256]{1,0:T(8,128)(2,1)}, bf16[256,512]{1,0:T(8,128)(2,1)}, bf16[256,256]{1,0:T(8,128)(2,1)}, bf16[2,2,256,256]{3,2,1,0:T(8,128)(2,1)}, bf16[2,2,256,256]{3,2,1,0:T(8,128)(2,1)}) custom-call(s32[5]{0:T(128)} %stack.90.here, bf16[1024,128]{1,0:T(8,128)(2,1)} %bitcast.55, bf16[512,128]{1,0:T(8,128)(2,1)} %bitcast.63, ...), custom_call_target="tpu_custom_call" | custom-call | flops 536870912 | bytes 3932160 | tf_op jit(solution)/shard_map/pallas_call | solution.py:161
  12.5 1.6 %collective-permute-start = (bf16[2,2,256,256]{3,2,1,0:T(8,128)(2,1)}, bf16[2,2,256,256]{3,2,1,0:T(8,128)(2,1)S(1)}, u32[]{:S(2)}, u32[]{:S(2)}) collective-permute-start(bf16[2,2,256,256]{3,2,1,0:T(8,128)(2,1)} %get-tuple-element.45), channel_id=1, source_target_pairs={{0,64},{1,17},{2,66},{3,19},{4,68},{5,21},{6,70},{7,23},{8,72},{9,... | collective-permute-start | bytes 1572872 | tf_op jit(solution)/shard_map/ppermute | solution.py:33
  14.0 1.7 %collective-permute-start.1 = (bf16[2,2,256,256]{3,2,1,0:T(8,128)(2,1)}, bf16[2,2,256,256]{3,2,1,0:T(8,128)(2,1)S(1)}, u32[]{:S(2)}, u32[]{:S(2)}) collective-permute-start(bf16[2,2,256,256]{3,2,1,0:T(8,128)(2,1)} %get-tuple-element.46), channel_id=1, source_target_pairs={{0,192},{1,49},{2,194},{3,51},{4,196},{5,53},{6,198},{7,55},{8,200... | collective-permute-start | bytes 1572872 | tf_op jit(solution)/shard_map/ppermute | solution.py:33
  15.8 1.9 %collective-permute-start.4 = (bf16[512,256]{1,0:T(8,128)(2,1)}, bf16[512,256]{1,0:T(8,128)(2,1)S(1)}, u32[]{:S(2)}, u32[]{:S(2)}) collective-permute-start(bf16[512,256]{1,0:T(8,128)(2,1)} %get-tuple-element.51), channel_id=1, source_target_pairs={{0,2},{1,3},{2,4},{3,5},{4,6},{5,7},{6,0},{7,1},{8,10},{9,11},{10,... | collective-permute-start | bytes 786440 | tf_op jit(solution)/shard_map/ppermute | solution.py:33
  17.7 4.7 %collective-permute-start.3 = (bf16[256,256]{1,0:T(8,128)(2,1)}, bf16[256,256]{1,0:T(8,128)(2,1)S(1)}, u32[]{:S(2)}, u32[]{:S(2)}) collective-permute-start(bf16[256,256]{1,0:T(8,128)(2,1)} %get-tuple-element.50), channel_id=1, source_target_pairs={{0,8},{1,40},{2,72},{3,104},{4,136},{5,168},{6,200},{7,232},{8,0},... | collective-permute-start | bytes 393224 | tf_op jit(solution)/shard_map/ppermute | solution.py:33
  22.4 4.1 %collective-permute-start.2 = (bf16[256,256]{1,0:T(8,128)(2,1)}, bf16[256,256]{1,0:T(8,128)(2,1)S(1)}, u32[]{:S(2)}, u32[]{:S(2)}) collective-permute-start(bf16[256,256]{1,0:T(8,128)(2,1)} %get-tuple-element.50), channel_id=1, source_target_pairs={{0,0},{1,32},{2,64},{3,96},{4,128},{5,160},{6,192},{7,224},{8,8},{... | collective-permute-start | bytes 393224 | tf_op jit(solution)/shard_map/ppermute | solution.py:33
  26.5 0.0 collective-permute-done.up_one
  26.5 0.0 collective-permute-done.1.down_one
  26.5 0.8 copy-done.5
  27.3 0.2 copy-done.6
  27.5 7.8 %shard_map.102 = (bf16[4,2,256,256]{3,2,1,0:T(8,128)(2,1)}, bf16[4,2,256,256]{3,2,1,0:T(8,128)(2,1)}, bf16[4,2,256,256]{3,2,1,0:T(8,128)(2,1)}) custom-call(s32[5]{0:T(128)} %stack.90.here, bf16[256,512]{1,0:T(8,128)(2,1)} %get-tuple-element.44.cot, bf16[512,8192]{1,0:T(8,128)(2,1)} %activations.3, bf16[2,2,256,256]{3,2,1,0:T(8,128)(2,1)} %copy-done.5, ...), custom_call_target="tpu_custom_call" | custom-call | flops 1610612736 | bytes 9699328 | tf_op jit(solution)/shard_map/pallas_call | solution.py:192
  35.3 0.0 collective-permute-done.3
  35.3 1.7 %collective-permute-done.2 = bf16[256,256]{1,0:T(8,128)(2,1)S(1)} collective-permute-done((bf16[256,256]{1,0:T(8,128)(2,1)}, bf16[256,256]{1,0:T(8,128)(2,1)S(1)}, u32[]{:S(2)}, u32[]{:S(2)}) %collective-permute-start.2) | collective-permute-done | bytes 131104 | tf_op jit(solution)/shard_map/ppermute | solution.py:33
  37.0 0.7 maximum_select_fusion.2
  37.7 0.0 all-gather.2.cloned.1.call-update
  37.7 0.1 collective-permute-start.5
  37.8 3.2 %collective-permute-start.6 = (bf16[4,2,256,256]{3,2,1,0:T(8,128)(2,1)}, bf16[4,2,256,256]{3,2,1,0:T(8,128)(2,1)S(1)}, u32[]{:S(2)}, u32[]{:S(2)}) collective-permute-start(bf16[4,2,256,256]{3,2,1,0:T(8,128)(2,1)} %get-tuple-element.53), channel_id=1, source_target_pairs={{0,192},{1,49},{2,194},{3,51},{4,196},{5,53},{6,198},{7,55},{8,200... | collective-permute-start | bytes 3145736 | tf_op jit(solution)/shard_map/ppermute | solution.py:33
  41.0 1.0 collective-permute-start.8
  42.0 2.2 %collective-permute-start.7 = (bf16[512,256]{1,0:T(8,128)(2,1)S(1)}, bf16[512,256]{1,0:T(8,128)(2,1)S(1)}, u32[]{:S(2)}, u32[]{:S(2)}) collective-permute-start(bf16[512,256]{1,0:T(8,128)(2,1)S(1)} %collective-permute-done.4), channel_id=1, source_target_pairs={{0,2},{1,3},{2,4},{3,5},{4,6},{5,7},{6,0},{7,1},{8,10},{9,11},{10,... | collective-permute-start | bytes 786440 | tf_op jit(solution)/shard_map/ppermute | solution.py:33
  44.2 9.8 %collective-permute-done.5 = bf16[4,2,256,256]{3,2,1,0:T(8,128)(2,1)S(1)} collective-permute-done((bf16[4,2,256,256]{3,2,1,0:T(8,128)(2,1)}, bf16[4,2,256,256]{3,2,1,0:T(8,128)(2,1)S(1)}, u32[]{:S(2)}, u32[]{:S(2)}) %collective-permute-start.5) | collective-permute-done | bytes 1048608 | tf_op jit(solution)/shard_map/ppermute | solution.py:33
  54.0 1.6 %add_convert_fusion.3 = (bf16[1,2,256,256]{3,2,1,0:T(8,128)(2,1)S(1)}, bf16[2,256,256]{2,1,0:T(8,128)(2,1)S(1)}, bf16[2,256,256]{2,1,0:T(8,128)(2,1)S(1)}, bf16[2,256,256]{2,1,0:T(8,128)(2,1)S(1)}) fusion(bf16[4,2,256,256]{3,2,1,0:T(8,128)(2,1)S(1)} %collective-permute-done.6, bf16[4,2,256,256]{3,2,1,0:T(8,128)(2,1)S(1)} %collective-permute-done.5, ...), kind=kLoop, calls=%fused_computation.6 | loop fusion | flops 3145728 | bytes 4194304 | tf_op jit(solution)/shard_map/convert_element_type | solution.py:359
  55.6 1.4 collective-permute-done.7
  57.0 0.1 pad_maximum_fusion.cot_mine
  57.1 0.0 copy-start.4
  57.1 0.1 collective-permute-start.12
  57.2 0.1 collective-permute-start.9
  57.3 4.2 %collective-permute-start.10 = (bf16[2,256,256]{2,1,0:T(8,128)(2,1)S(1)}, bf16[2,256,256]{2,1,0:T(8,128)(2,1)S(1)}, u32[]{:S(2)}, u32[]{:S(2)}) collective-permute-start(bf16[2,256,256]{2,1,0:T(8,128)(2,1)S(1)} %get-tuple-element.56), channel_id=1, source_target_pairs={{0,48},{1,193},{2,50},{3,195},{4,52},{5,197},{6,54},{7,199},{8,56}... | collective-permute-start | bytes 786440 | tf_op jit(solution)/shard_map/ppermute | solution.py:33
  61.5 2.0 %collective-permute-start.11 = (bf16[2,256,256]{2,1,0:T(8,128)(2,1)S(1)}, bf16[2,256,256]{2,1,0:T(8,128)(2,1)S(1)}, u32[]{:S(2)}, u32[]{:S(2)}) collective-permute-start(bf16[2,256,256]{2,1,0:T(8,128)(2,1)S(1)} %get-tuple-element.57), channel_id=1, source_target_pairs={{0,32},{1,129},{2,34},{3,131},{4,36},{5,133},{6,38},{7,135},{8,40}... | collective-permute-start | bytes 786440 | tf_op jit(solution)/shard_map/ppermute | solution.py:33
  63.6 2.9 %collective-permute-done.9 = bf16[2,256,256]{2,1,0:T(8,128)(2,1)S(1)} collective-permute-done((bf16[2,256,256]{2,1,0:T(8,128)(2,1)S(1)}, bf16[2,256,256]{2,1,0:T(8,128)(2,1)S(1)}, u32[]{:S(2)}, u32[]{:S(2)}) %collective-permute-start.9) | collective-permute-done | bytes 262176 | tf_op jit(solution)/shard_map/ppermute | solution.py:33
  66.4 1.0 collective-permute-done.10
  67.4 5.4 %collective-permute-done.11 = bf16[2,256,256]{2,1,0:T(8,128)(2,1)S(1)} collective-permute-done((bf16[2,256,256]{2,1,0:T(8,128)(2,1)S(1)}, bf16[2,256,256]{2,1,0:T(8,128)(2,1)S(1)}, u32[]{:S(2)}, u32[]{:S(2)}) %collective-permute-start.11) | collective-permute-done | bytes 262176 | tf_op jit(solution)/shard_map/ppermute | solution.py:33
  72.9 0.1 fusion.10
  73.0 10.0 %collective-permute-start.13 = (bf16[256,256]{1,0:T(8,128)(2,1)S(1)}, bf16[256,256]{1,0:T(8,128)(2,1)S(1)}, u32[]{:S(2)}, u32[]{:S(2)}) collective-permute-start(bf16[256,256]{1,0:T(8,128)(2,1)S(1)} %get-tuple-element.60), channel_id=1, source_target_pairs={{0,8},{1,9},{2,10},{3,11},{4,12},{5,13},{6,14},{7,15},{8,0},{9,1},... | collective-permute-start | bytes 393224 | tf_op jit(solution)/shard_map/ppermute | solution.py:33
  83.0 4.1 %collective-permute-done.13.theirs = bf16[256,256]{1,0:T(8,128)(2,1)S(1)} collective-permute-done((bf16[256,256]{1,0:T(8,128)(2,1)S(1)}, bf16[256,256]{1,0:T(8,128)(2,1)S(1)}, u32[]{:S(2)}, u32[]{:S(2)}) %collective-permute-start.13) | collective-permute-done | bytes 131104 | tf_op jit(solution)/shard_map/ppermute | solution.py:33
  87.1 1.2 shard_map.103
  88.3 4.9 %collective-permute-start.14 = (bf16[512,128]{1,0:T(8,128)(2,1)S(1)}, bf16[512,128]{1,0:T(8,128)(2,1)S(1)}, u32[]{:S(2)}, u32[]{:S(2)}) collective-permute-start(bf16[512,128]{1,0:T(8,128)(2,1)S(1)} %get-tuple-element.61), channel_id=1, source_target_pairs={{0,8},{1,9},{2,10},{3,11},{4,12},{5,13},{6,14},{7,15},{8,0},{9,1},... | collective-permute-start | bytes 393224 | tf_op jit(solution)/shard_map/ppermute | solution.py:33
  93.2 4.0 %collective-permute-done.14 = bf16[512,128]{1,0:T(8,128)(2,1)S(1)} collective-permute-done((bf16[512,128]{1,0:T(8,128)(2,1)S(1)}, bf16[512,128]{1,0:T(8,128)(2,1)S(1)}, u32[]{:S(2)}, u32[]{:S(2)}) %collective-permute-start.14) | collective-permute-done | bytes 131104 | tf_op jit(solution)/shard_map/ppermute | solution.py:33
  97.3 1.3 collective-permute-start.17
  98.6 3.2 %collective-permute-start.16 = (bf16[2,512,128]{2,1,0:T(8,128)(2,1)S(1)}, bf16[2,512,128]{2,1,0:T(8,128)(2,1)S(1)}, u32[]{:S(2)}, u32[]{:S(2)}) collective-permute-start(bf16[2,512,128]{2,1,0:T(8,128)(2,1)S(1)} %maximum_select_fusion.1), channel_id=1, source_target_pairs={{0,32},{1,129},{2,34},{3,131},{4,36},{5,133},{6,38},{7,135},{8,40}... | collective-permute-start | bytes 786440 | tf_op jit(solution)/shard_map/ppermute | solution.py:33
  101.8 0.6 collective-permute-start.15
  102.5 3.6 %collective-permute-done.17 = bf16[2,512,128]{2,1,0:T(8,128)(2,1)S(1)} collective-permute-done((bf16[2,512,128]{2,1,0:T(8,128)(2,1)S(1)}, bf16[2,512,128]{2,1,0:T(8,128)(2,1)S(1)}, u32[]{:S(2)}, u32[]{:S(2)}) %collective-permute-start.17) | collective-permute-done | bytes 262176 | tf_op jit(solution)/shard_map/ppermute | solution.py:33
  106.1 3.1 %collective-permute-done.16 = bf16[2,512,128]{2,1,0:T(8,128)(2,1)S(1)} collective-permute-done((bf16[2,512,128]{2,1,0:T(8,128)(2,1)S(1)}, bf16[2,512,128]{2,1,0:T(8,128)(2,1)S(1)}, u32[]{:S(2)}, u32[]{:S(2)}) %collective-permute-start.16) | collective-permute-done | bytes 262176 | tf_op jit(solution)/shard_map/ppermute | solution.py:33
  109.2 0.1 pad_maximum_fusion.2.refs_1_
  109.2 0.0 collective-permute-done.15
  109.2 0.1 pad_maximum_fusion.1.refs_0_
  109.3 1.5 %collective-permute-start.20 = (bf16[2,2,512,128]{3,2,1,0:T(8,128)(2,1)S(1)}, bf16[2,2,512,128]{3,2,1,0:T(8,128)(2,1)S(1)}, u32[]{:S(2)}, u32[]{:S(2)}) collective-permute-start(bf16[2,2,512,128]{3,2,1,0:T(8,128)(2,1)S(1)} %pad_maximum_fusion.1.refs_0_), channel_id=1, source_target_pairs={{0,64},{1,17},{2,66},{3,19},{4,68},{5,21},{6,70},{7,23},{8,72},{9,... | collective-permute-start | bytes 1572872 | tf_op jit(solution)/shard_map/ppermute | solution.py:33
  110.9 2.3 %collective-permute-start.21 = (bf16[2,2,512,128]{3,2,1,0:T(8,128)(2,1)S(1)}, bf16[2,2,512,128]{3,2,1,0:T(8,128)(2,1)}, u32[]{:S(2)}, u32[]{:S(2)}) collective-permute-start(bf16[2,2,512,128]{3,2,1,0:T(8,128)(2,1)S(1)} %pad_maximum_fusion.2.refs_1_), channel_id=1, source_target_pairs={{0,192},{1,49},{2,194},{3,51},{4,196},{5,53},{6,198},{7,55},{8,200... | collective-permute-start | bytes 1572872 | tf_op jit(solution)/shard_map/ppermute | solution.py:33
  113.2 1.9 %collective-permute-start.18 = (bf16[2,2,512,128]{3,2,1,0:T(8,128)(2,1)S(1)}, bf16[2,2,512,128]{3,2,1,0:T(8,128)(2,1)}, u32[]{:S(2)}, u32[]{:S(2)}) collective-permute-start(bf16[2,2,512,128]{3,2,1,0:T(8,128)(2,1)S(1)} %pad_maximum_fusion.1.refs_0_), channel_id=1, source_target_pairs={{0,192},{1,49},{2,194},{3,51},{4,196},{5,53},{6,198},{7,55},{8,200... | collective-permute-start | bytes 1572872 | tf_op jit(solution)/shard_map/ppermute | solution.py:33
  115.2 0.1 collective-permute-start.19
  115.2 10.4 %collective-permute-start.22 = (bf16[4,2,256,128]{3,2,1,0:T(8,128)(2,1)}, bf16[4,2,256,128]{3,2,1,0:T(8,128)(2,1)S(1)}, u32[]{:S(2)}, u32[]{:S(2)}) collective-permute-start(bf16[4,2,256,128]{3,2,1,0:T(8,128)(2,1)} %get-tuple-element.73), channel_id=1, source_target_pairs={{0,248},{1,249},{2,250},{3,251},{4,252},{5,253},{6,254},{7,255},{8... | collective-permute-start | bytes 1572872 | tf_op jit(solution)/shard_map/ppermute | solution.py:33
  125.7 0.0 collective-permute-done.20.refs_4_
  125.7 0.0 collective-permute-done.21.refs_3_
  125.7 0.0 collective-permute-start.24
  125.7 2.0 %collective-permute-start.23 = (bf16[2,2,512,128]{3,2,1,0:T(8,128)(2,1)S(1)}, bf16[2,2,512,128]{3,2,1,0:T(8,128)(2,1)S(1)}, u32[]{:S(2)}, u32[]{:S(2)}) collective-permute-start(bf16[2,2,512,128]{3,2,1,0:T(8,128)(2,1)S(1)} %collective-permute-done.20.refs_4_), channel_id=1, source_target_pairs={{0,64},{1,17},{2,66},{3,19},{4,68},{5,21},{6,70},{7,23},{8,72},{9,... | collective-permute-start | bytes 1572872 | tf_op jit(solution)/shard_map/ppermute | solution.py:33
  127.7 7.0 %shard_map.104 = bf16[512,1024]{1,0:T(8,128)(2,1)} custom-call(s32[5]{0:T(128)} %stack.90.here, bf16[4,512,256]{2,1,0:T(8,128)(2,1)} %copy-done.4, bf16[4,512,256]{2,1,0:T(8,128)(2,1)} %copy-done.8, bf16[16,2,256,256]{3,2,1,0:T(8,128)(2,1)} %all-gather.2.cloned.1.call-done.params), custom_call_target="tpu_custom_call" | custom-call | flops 2147483648 | bytes 5242880 | tf_op jit(solution)/shard_map/pallas_call | solution.py:332
  134.7 0.0 collective-permute-done.18.refs_2_
  134.7 3.2 %shard_map.105.refs_2_ = bf16[32,512,128]{2,1,0:T(8,128)(2,1)} custom-call(s32[5]{0:T(128)S(1)} %copy-done.3, bf16[2,2,512,128]{3,2,1,0:T(8,128)(2,1)S(1)} %pad_maximum_fusion.1.refs_0_, bf16[2,2,512,128]{3,2,1,0:T(8,128)(2,1)S(1)} %pad_maximum_fusion.2.refs_1_, bf16[2,2,512,128]{3,2,1,0:T(8,128)(2,1)} %collective-permute-done.18.refs_2_, ...), custom_call_target="tpu_custom_call" | custom-call | tf_op jit(solution)/shard_map/pallas_call | solution.py:274
  137.9 5.6 %collective-permute-done.22.sent = bf16[4,2,256,128]{3,2,1,0:T(8,128)(2,1)S(1)} collective-permute-done((bf16[4,2,256,128]{3,2,1,0:T(8,128)(2,1)}, bf16[4,2,256,128]{3,2,1,0:T(8,128)(2,1)S(1)}, u32[]{:S(2)}, u32[]{:S(2)}) %collective-permute-start.22) | collective-permute-done | bytes 524320 | tf_op jit(solution)/shard_map/ppermute | solution.py:33
  143.5 0.9 shard_map.106
  144.5 0.0 collective-permute-done.24.refs_1_
  144.5 0.0 collective-permute-done.23.refs_0_
  144.5 1.6 %shard_map.107 = bf16[32,512,128]{2,1,0:T(8,128)(2,1)} custom-call(s32[5]{0:T(128)S(1)} %copy-done.3, bf16[2,2,512,128]{3,2,1,0:T(8,128)(2,1)S(1)} %collective-permute-done.23.refs_0_, bf16[2,2,512,128]{3,2,1,0:T(8,128)(2,1)S(1)} %collective-permute-done.24.refs_1_, bf16[32,512,128]{2,1,0:T(8,128)(2,1)} %shard_map.105.refs_2_), custom_call_target="tpu_custom_call", output_to_operand_aliasing={{}: (3, {})} | custom-call | tf_op jit(solution)/shard_map/pallas_call | solution.py:274
  (23 shorter events, 0.1 us)
Async XLA Ops:
  7.2 120.5 %all-gather.2.cloned.1.call-start = ((), (), s32[]{:S(2)}) async-start(), calls=%async_computation | async-start | bytes 4456448 | tf_op jit(solution)/shard_map/all_gather | solution.py:391
  12.5 14.0 %collective-permute-start = (bf16[2,2,256,256]{3,2,1,0:T(8,128)(2,1)}, bf16[2,2,256,256]{3,2,1,0:T(8,128)(2,1)S(1)}, u32[]{:S(2)}, u32[]{:S(2)}) collective-permute-start(bf16[2,2,256,256]{3,2,1,0:T(8,128)(2,1)} %get-tuple-element.45), channel_id=1, source_target_pairs={{0,64},{1,17},{2,66},{3,19},{4,68},{5,21},{6,70},{7,23},{8,72},{9,... | collective-permute-start | bytes 1572872 | tf_op jit(solution)/shard_map/ppermute | solution.py:33
  14.0 12.4 %collective-permute-start.1 = (bf16[2,2,256,256]{3,2,1,0:T(8,128)(2,1)}, bf16[2,2,256,256]{3,2,1,0:T(8,128)(2,1)S(1)}, u32[]{:S(2)}, u32[]{:S(2)}) collective-permute-start(bf16[2,2,256,256]{3,2,1,0:T(8,128)(2,1)} %get-tuple-element.46), channel_id=1, source_target_pairs={{0,192},{1,49},{2,194},{3,51},{4,196},{5,53},{6,198},{7,55},{8,200... | collective-permute-start | bytes 1572872 | tf_op jit(solution)/shard_map/ppermute | solution.py:33
  15.8 21.2 %collective-permute-start.4 = (bf16[512,256]{1,0:T(8,128)(2,1)}, bf16[512,256]{1,0:T(8,128)(2,1)S(1)}, u32[]{:S(2)}, u32[]{:S(2)}) collective-permute-start(bf16[512,256]{1,0:T(8,128)(2,1)} %get-tuple-element.51), channel_id=1, source_target_pairs={{0,2},{1,3},{2,4},{3,5},{4,6},{5,7},{6,0},{7,1},{8,10},{9,11},{10,... | collective-permute-start | bytes 786440 | tf_op jit(solution)/shard_map/ppermute | solution.py:33
  17.7 17.6 %collective-permute-start.3 = (bf16[256,256]{1,0:T(8,128)(2,1)}, bf16[256,256]{1,0:T(8,128)(2,1)S(1)}, u32[]{:S(2)}, u32[]{:S(2)}) collective-permute-start(bf16[256,256]{1,0:T(8,128)(2,1)} %get-tuple-element.50), channel_id=1, source_target_pairs={{0,8},{1,40},{2,72},{3,104},{4,136},{5,168},{6,200},{7,232},{8,0},... | collective-permute-start | bytes 393224 | tf_op jit(solution)/shard_map/ppermute | solution.py:33
  22.4 14.6 %collective-permute-start.2 = (bf16[256,256]{1,0:T(8,128)(2,1)}, bf16[256,256]{1,0:T(8,128)(2,1)S(1)}, u32[]{:S(2)}, u32[]{:S(2)}) collective-permute-start(bf16[256,256]{1,0:T(8,128)(2,1)} %get-tuple-element.50), channel_id=1, source_target_pairs={{0,0},{1,32},{2,64},{3,96},{4,128},{5,160},{6,192},{7,224},{8,8},{... | collective-permute-start | bytes 393224 | tf_op jit(solution)/shard_map/ppermute | solution.py:33
  26.5 0.8 copy-start.5
  26.5 1.0 copy-start.6
  27.5 13.5 %copy-start.7 = (bf16[512,256]{1,0:T(8,128)(2,1)S(1)}, bf16[512,256]{1,0:T(8,128)(2,1)}, u32[]{:S(2)}) copy-start(bf16[512,256]{1,0:T(8,128)(2,1)} %get-tuple-element.51) | copy-start | bytes 786436
  36.9 50.2 %copy-start = (f32[256,2,128]{2,1,0:T(2,128)S(1)}, f32[256,2,128]{2,1,0:T(2,128)}, u32[]{:S(2)}) copy-start(f32[256,2,128]{2,1,0:T(2,128)} %param.9) | copy-start | bytes 786436
  37.0 50.2 %copy-start.1 = (f32[256,2,128]{2,1,0:T(2,128)S(1)}, f32[256,2,128]{2,1,0:T(2,128)}, u32[]{:S(2)}) copy-start(f32[256,2,128]{2,1,0:T(2,128)} %param.10) | copy-start | bytes 786436
  37.0 50.2 %copy-start.2 = (f32[256,2,128]{2,1,0:T(2,128)S(1)}, f32[256,2,128]{2,1,0:T(2,128)}, u32[]{:S(2)}) copy-start(f32[256,2,128]{2,1,0:T(2,128)} %param.11) | copy-start | bytes 786436
  37.7 16.3 %collective-permute-start.5 = (bf16[4,2,256,256]{3,2,1,0:T(8,128)(2,1)}, bf16[4,2,256,256]{3,2,1,0:T(8,128)(2,1)S(1)}, u32[]{:S(2)}, u32[]{:S(2)}) collective-permute-start(bf16[4,2,256,256]{3,2,1,0:T(8,128)(2,1)} %get-tuple-element.52), channel_id=1, source_target_pairs={{0,64},{1,17},{2,66},{3,19},{4,68},{5,21},{6,70},{7,23},{8,72},{9,... | collective-permute-start | bytes 3145736 | tf_op jit(solution)/shard_map/ppermute | solution.py:33
  37.8 16.2 %collective-permute-start.6 = (bf16[4,2,256,256]{3,2,1,0:T(8,128)(2,1)}, bf16[4,2,256,256]{3,2,1,0:T(8,128)(2,1)S(1)}, u32[]{:S(2)}, u32[]{:S(2)}) collective-permute-start(bf16[4,2,256,256]{3,2,1,0:T(8,128)(2,1)} %get-tuple-element.53), channel_id=1, source_target_pairs={{0,192},{1,49},{2,194},{3,51},{4,196},{5,53},{6,198},{7,55},{8,200... | collective-permute-start | bytes 3145736 | tf_op jit(solution)/shard_map/ppermute | solution.py:33
  41.0 14.6 %collective-permute-start.8 = (bf16[512,256]{1,0:T(8,128)(2,1)S(1)}, bf16[512,256]{1,0:T(8,128)(2,1)S(1)}, u32[]{:S(2)}, u32[]{:S(2)}) collective-permute-start(bf16[512,256]{1,0:T(8,128)(2,1)S(1)} %copy-done.7), channel_id=1, source_target_pairs={{0,6},{1,7},{2,0},{3,1},{4,2},{5,3},{6,4},{7,5},{8,14},{9,15},{10,... | collective-permute-start | bytes 786440 | tf_op jit(solution)/shard_map/ppermute | solution.py:33
  42.0 15.0 %collective-permute-start.7 = (bf16[512,256]{1,0:T(8,128)(2,1)S(1)}, bf16[512,256]{1,0:T(8,128)(2,1)S(1)}, u32[]{:S(2)}, u32[]{:S(2)}) collective-permute-start(bf16[512,256]{1,0:T(8,128)(2,1)S(1)} %collective-permute-done.4), channel_id=1, source_target_pairs={{0,2},{1,3},{2,4},{3,5},{4,6},{5,7},{6,0},{7,1},{8,10},{9,11},{10,... | collective-permute-start | bytes 786440 | tf_op jit(solution)/shard_map/ppermute | solution.py:33
  57.1 30.0 %copy-start.4 = (bf16[4,512,256]{2,1,0:T(8,128)(2,1)}, bf16[4,512,256]{2,1,0:T(8,128)(2,1)S(1)}, u32[]{:S(2)}) copy-start(bf16[4,512,256]{2,1,0:T(8,128)(2,1)S(1)} %pad_maximum_fusion.cot_mine) | copy-start | bytes 3145732
  57.1 15.8 %collective-permute-start.12 = (bf16[4,512,256]{2,1,0:T(8,128)(2,1)S(1)}, bf16[4,512,256]{2,1,0:T(8,128)(2,1)S(1)}, u32[]{:S(2)}, u32[]{:S(2)}) collective-permute-start(bf16[4,512,256]{2,1,0:T(8,128)(2,1)S(1)} %pad_maximum_fusion.cot_mine), channel_id=1, source_target_pairs={{0,1},{1,0},{2,3},{3,2},{4,5},{5,4},{6,7},{7,6},{8,9},{9,8},{10,11... | collective-permute-start | bytes 3145736 | tf_op jit(solution)/shard_map/ppermute | solution.py:33
  57.2 9.2 %collective-permute-start.9 = (bf16[2,256,256]{2,1,0:T(8,128)(2,1)S(1)}, bf16[2,256,256]{2,1,0:T(8,128)(2,1)S(1)}, u32[]{:S(2)}, u32[]{:S(2)}) collective-permute-start(bf16[2,256,256]{2,1,0:T(8,128)(2,1)S(1)} %get-tuple-element.55), channel_id=1, source_target_pairs={{0,16},{1,65},{2,18},{3,67},{4,20},{5,69},{6,22},{7,71},{8,24},{9,... | collective-permute-start | bytes 786440 | tf_op jit(solution)/shard_map/ppermute | solution.py:33
  57.3 10.1 %collective-permute-start.10 = (bf16[2,256,256]{2,1,0:T(8,128)(2,1)S(1)}, bf16[2,256,256]{2,1,0:T(8,128)(2,1)S(1)}, u32[]{:S(2)}, u32[]{:S(2)}) collective-permute-start(bf16[2,256,256]{2,1,0:T(8,128)(2,1)S(1)} %get-tuple-element.56), channel_id=1, source_target_pairs={{0,48},{1,193},{2,50},{3,195},{4,52},{5,197},{6,54},{7,199},{8,56}... | collective-permute-start | bytes 786440 | tf_op jit(solution)/shard_map/ppermute | solution.py:33
  61.5 11.3 %collective-permute-start.11 = (bf16[2,256,256]{2,1,0:T(8,128)(2,1)S(1)}, bf16[2,256,256]{2,1,0:T(8,128)(2,1)S(1)}, u32[]{:S(2)}, u32[]{:S(2)}) collective-permute-start(bf16[2,256,256]{2,1,0:T(8,128)(2,1)S(1)} %get-tuple-element.57), channel_id=1, source_target_pairs={{0,32},{1,129},{2,34},{3,131},{4,36},{5,133},{6,38},{7,135},{8,40}... | collective-permute-start | bytes 786440 | tf_op jit(solution)/shard_map/ppermute | solution.py:33
  73.0 14.1 %copy-start.8 = (bf16[4,512,256]{2,1,0:T(8,128)(2,1)}, bf16[4,512,256]{2,1,0:T(8,128)(2,1)S(1)}, u32[]{:S(2)}) copy-start(bf16[4,512,256]{2,1,0:T(8,128)(2,1)S(1)} %collective-permute-done.12.cot_theirs) | copy-start | bytes 3145732
  73.0 14.1 %collective-permute-start.13 = (bf16[256,256]{1,0:T(8,128)(2,1)S(1)}, bf16[256,256]{1,0:T(8,128)(2,1)S(1)}, u32[]{:S(2)}, u32[]{:S(2)}) collective-permute-start(bf16[256,256]{1,0:T(8,128)(2,1)S(1)} %get-tuple-element.60), channel_id=1, source_target_pairs={{0,8},{1,9},{2,10},{3,11},{4,12},{5,13},{6,14},{7,15},{8,0},{9,1},... | collective-permute-start | bytes 393224 | tf_op jit(solution)/shard_map/ppermute | solution.py:33
  88.3 8.9 %collective-permute-start.14 = (bf16[512,128]{1,0:T(8,128)(2,1)S(1)}, bf16[512,128]{1,0:T(8,128)(2,1)S(1)}, u32[]{:S(2)}, u32[]{:S(2)}) collective-permute-start(bf16[512,128]{1,0:T(8,128)(2,1)S(1)} %get-tuple-element.61), channel_id=1, source_target_pairs={{0,8},{1,9},{2,10},{3,11},{4,12},{5,13},{6,14},{7,15},{8,0},{9,1},... | collective-permute-start | bytes 393224 | tf_op jit(solution)/shard_map/ppermute | solution.py:33
  97.3 8.8 %collective-permute-start.17 = (bf16[2,512,128]{2,1,0:T(8,128)(2,1)S(1)}, bf16[2,512,128]{2,1,0:T(8,128)(2,1)S(1)}, u32[]{:S(2)}, u32[]{:S(2)}) collective-permute-start(bf16[2,512,128]{2,1,0:T(8,128)(2,1)S(1)} %maximum_select_fusion.1), channel_id=1, source_target_pairs={{0,16},{1,65},{2,18},{3,67},{4,20},{5,69},{6,22},{7,71},{8,24},{9,... | collective-permute-start | bytes 786440 | tf_op jit(solution)/shard_map/ppermute | solution.py:33
  98.6 10.6 %collective-permute-start.16 = (bf16[2,512,128]{2,1,0:T(8,128)(2,1)S(1)}, bf16[2,512,128]{2,1,0:T(8,128)(2,1)S(1)}, u32[]{:S(2)}, u32[]{:S(2)}) collective-permute-start(bf16[2,512,128]{2,1,0:T(8,128)(2,1)S(1)} %maximum_select_fusion.1), channel_id=1, source_target_pairs={{0,32},{1,129},{2,34},{3,131},{4,36},{5,133},{6,38},{7,135},{8,40}... | collective-permute-start | bytes 786440 | tf_op jit(solution)/shard_map/ppermute | solution.py:33
  101.8 7.4 %collective-permute-start.15 = (bf16[2,512,128]{2,1,0:T(8,128)(2,1)S(1)}, bf16[2,512,128]{2,1,0:T(8,128)(2,1)S(1)}, u32[]{:S(2)}, u32[]{:S(2)}) collective-permute-start(bf16[2,512,128]{2,1,0:T(8,128)(2,1)S(1)} %maximum_select_fusion.1), channel_id=1, source_target_pairs={{0,48},{1,193},{2,50},{3,195},{4,52},{5,197},{6,54},{7,199},{8,56}... | collective-permute-start | bytes 786440 | tf_op jit(solution)/shard_map/ppermute | solution.py:33
  109.3 25.4 %copy-start.3 = (s32[5]{0:T(128)S(1)}, s32[5]{0:T(128)}, u32[]{:S(2)}) copy-start(s32[5]{0:T(128)} %stack.90.here) | copy-start | bytes 64
  109.3 16.3 %collective-permute-start.20 = (bf16[2,2,512,128]{3,2,1,0:T(8,128)(2,1)S(1)}, bf16[2,2,512,128]{3,2,1,0:T(8,128)(2,1)S(1)}, u32[]{:S(2)}, u32[]{:S(2)}) collective-permute-start(bf16[2,2,512,128]{3,2,1,0:T(8,128)(2,1)S(1)} %pad_maximum_fusion.1.refs_0_), channel_id=1, source_target_pairs={{0,64},{1,17},{2,66},{3,19},{4,68},{5,21},{6,70},{7,23},{8,72},{9,... | collective-permute-start | bytes 1572872 | tf_op jit(solution)/shard_map/ppermute | solution.py:33
  110.9 14.8 %collective-permute-start.21 = (bf16[2,2,512,128]{3,2,1,0:T(8,128)(2,1)S(1)}, bf16[2,2,512,128]{3,2,1,0:T(8,128)(2,1)}, u32[]{:S(2)}, u32[]{:S(2)}) collective-permute-start(bf16[2,2,512,128]{3,2,1,0:T(8,128)(2,1)S(1)} %pad_maximum_fusion.2.refs_1_), channel_id=1, source_target_pairs={{0,192},{1,49},{2,194},{3,51},{4,196},{5,53},{6,198},{7,55},{8,200... | collective-permute-start | bytes 1572872 | tf_op jit(solution)/shard_map/ppermute | solution.py:33
  113.2 21.4 %collective-permute-start.18 = (bf16[2,2,512,128]{3,2,1,0:T(8,128)(2,1)S(1)}, bf16[2,2,512,128]{3,2,1,0:T(8,128)(2,1)}, u32[]{:S(2)}, u32[]{:S(2)}) collective-permute-start(bf16[2,2,512,128]{3,2,1,0:T(8,128)(2,1)S(1)} %pad_maximum_fusion.1.refs_0_), channel_id=1, source_target_pairs={{0,192},{1,49},{2,194},{3,51},{4,196},{5,53},{6,198},{7,55},{8,200... | collective-permute-start | bytes 1572872 | tf_op jit(solution)/shard_map/ppermute | solution.py:33
  115.2 19.5 %collective-permute-start.19 = (bf16[2,2,512,128]{3,2,1,0:T(8,128)(2,1)S(1)}, bf16[2,2,512,128]{3,2,1,0:T(8,128)(2,1)}, u32[]{:S(2)}, u32[]{:S(2)}) collective-permute-start(bf16[2,2,512,128]{3,2,1,0:T(8,128)(2,1)S(1)} %pad_maximum_fusion.2.refs_1_), channel_id=1, source_target_pairs={{0,64},{1,17},{2,66},{3,19},{4,68},{5,21},{6,70},{7,23},{8,72},{9,... | collective-permute-start | bytes 1572872 | tf_op jit(solution)/shard_map/ppermute | solution.py:33
  115.2 28.3 %collective-permute-start.22 = (bf16[4,2,256,128]{3,2,1,0:T(8,128)(2,1)}, bf16[4,2,256,128]{3,2,1,0:T(8,128)(2,1)S(1)}, u32[]{:S(2)}, u32[]{:S(2)}) collective-permute-start(bf16[4,2,256,128]{3,2,1,0:T(8,128)(2,1)} %get-tuple-element.73), channel_id=1, source_target_pairs={{0,248},{1,249},{2,250},{3,251},{4,252},{5,253},{6,254},{7,255},{8... | collective-permute-start | bytes 1572872 | tf_op jit(solution)/shard_map/ppermute | solution.py:33
  125.7 18.8 %collective-permute-start.24 = (bf16[2,2,512,128]{3,2,1,0:T(8,128)(2,1)}, bf16[2,2,512,128]{3,2,1,0:T(8,128)(2,1)S(1)}, u32[]{:S(2)}, u32[]{:S(2)}) collective-permute-start(bf16[2,2,512,128]{3,2,1,0:T(8,128)(2,1)} %collective-permute-done.21.refs_3_), channel_id=1, source_target_pairs={{0,192},{1,49},{2,194},{3,51},{4,196},{5,53},{6,198},{7,55},{8,200... | collective-permute-start | bytes 1572872 | tf_op jit(solution)/shard_map/ppermute | solution.py:33
  125.7 18.8 %collective-permute-start.23 = (bf16[2,2,512,128]{3,2,1,0:T(8,128)(2,1)S(1)}, bf16[2,2,512,128]{3,2,1,0:T(8,128)(2,1)S(1)}, u32[]{:S(2)}, u32[]{:S(2)}) collective-permute-start(bf16[2,2,512,128]{3,2,1,0:T(8,128)(2,1)S(1)} %collective-permute-done.20.refs_4_), channel_id=1, source_target_pairs={{0,64},{1,17},{2,66},{3,19},{4,68},{5,21},{6,70},{7,23},{8,72},{9,... | collective-permute-start | bytes 1572872 | tf_op jit(solution)/shard_map/ppermute | solution.py:33
Sparse Core Ops, SparseCore 0:
  37.8 70.6 all-gather.1

commit v5 on v4

--- a/solution.py
+++ b/solution.py
@@ -406,17 +406,17 @@
     state = [v.reshape(2 * rows, width) for v in (master_store, first_store, second_store)]
     sent, layer = adam(near, move(far, other_half), *state)
 
-    layer_other = move(layer, other_half)
+    layer_other, sent = tie(move(layer, other_half), sent)
+    sent = move(sent, previous_block)
     pair = jnp.where(h == 0, jnp.stack([layer, layer_other]), jnp.stack([layer_other, layer]))
     from_up = move(pair, along_second(-1))
     from_down = move(pair, along_second(1))
     from_far = move(pair, along_second(2))
     low, high = jnp.stack([pair, from_up]), jnp.stack([from_far, from_down])
-    low, high, sent = tie(low, high, sent)
+    low, high = tie(low, high)
     low_down, high_up = move(low, along_first(1)), move(high, along_first(-1))
     high_down, low_up = move(high, along_first(1)), move(low, along_first(-1))
-    sent = move(sent, previous_block)
-    low_down, high_up = tie(low_down, high_up)
+    low_down, high_up, sent = tie(low_down, high_up, sent)
     low_far, high_far = move(low_down, along_first(1)), move(high_up, along_first(-1))
     input_grad = input_matmul(here, cot_mine, cot_theirs, params)
     low_up, high_down, input_grad = tie(low_up, high_down, input_grad)
@@ -426,7 +426,6 @@
         [low, high, low_up, high_up, low_down, high_down],
         32,
     )
-    new_layer, sent = tie(new_layer, sent)
     new_layer, *state = tie(new_layer, *unpack(sent))
     new_layer = place(here, ((2, 0), (2, 2)), [low_far, high_far], 32, new_layer)
     new_master, new_first, new_second = (v.reshape(rows, 2, width) for v in state)

time: 154 us -> 165 us (1.071)
  the two profiles are of different devices: /device:TPU:32 before, /device:TPU:210 now
where the time goes in v5:
time: 165 us; the launch traced here: 164 us
  starting transfers between devices  61.2 us (37%)
  waiting for transfers between devices  59.4 us (36%)
  Pallas kernels  25.3 us (15%)
  between operations  14.3 us (9%)
  other arithmetic  2.77 us (2%)
    ppermute x25, starting transfers between devices, move(): return lax.ppermute(value, AXES, pairs)  61.2 us
    ppermute x25, waiting for transfers between devices, move(): return lax.ppermute(value, AXES, pairs)  59.4 us
    pallas_call x1, Pallas kernels, other_terms(): pl.pallas_call(functools.partial(other_kernel, groups), out_shape=[jax.Sh...  7.79 us
    pallas_call x1, Pallas kernels, input_matmul(): pl.pallas_call(input_kernel, out_shape=jax.ShapeDtypeStruct((tokens, 4 *...  6.96 us
    pallas_call x2, Pallas kernels, place(): pl.pallas_call(functools.partial(place_kernel, groups), out_shape=jax.Sha...  4.67 us
    pallas_call x1, Pallas kernels, first_terms(): pl.pallas_call(functools.partial(first_kernel, groups), out_shape=[jax.Sh...  4.58 us
  transfers between devices with their start and end apart: 26, of which 13 were waited for; matrix products, arithmetic and copies ran while one was open for 1% of the time, Pallas kernels for 12%

profile of v5, /device:TPU:210, one launch (start us, length us, event | category | flops | bytes accessed | tf_op | source)
XLA Modules:
  0.0 164.4 jit_solution(4040220822133701223)
XLA Ops:
  7.2 0.0 all-gather.2.cloned.1.call-start
  7.2 0.6 stack.90.here
  7.8 4.6 %shard_map.101 = (bf16[512,256]{1,0:T(8,128)(2,1)}, bf16[256,512]{1,0:T(8,128)(2,1)}, bf16[256,256]{1,0:T(8,128)(2,1)}, bf16[2,2,256,256]{3,2,1,0:T(8,128)(2,1)}, bf16[2,2,256,256]{3,2,1,0:T(8,128)(2,1)}) custom-call(s32[5]{0:T(128)} %stack.90.here, bf16[1024,128]{1,0:T(8,128)(2,1)} %bitcast.55, bf16[512,128]{1,0:T(8,128)(2,1)} %bitcast.63, ...), custom_call_target="tpu_custom_call" | custom-call | flops 536870912 | bytes 3932160 | tf_op jit(solution)/shard_map/pallas_call | solution.py:161
  12.4 1.6 collective-permute-start
  14.0 0.5 collective-permute-start.1
  14.5 1.0 collective-permute-start.4
  15.5 0.7 collective-permute-start.3
  16.3 6.2 %collective-permute-start.2 = (bf16[256,256]{1,0:T(8,128)(2,1)}, bf16[256,256]{1,0:T(8,128)(2,1)S(1)}, u32[]{:S(2)}, u32[]{:S(2)}) collective-permute-start(bf16[256,256]{1,0:T(8,128)(2,1)} %get-tuple-element.50), channel_id=1, source_target_pairs={{0,0},{1,32},{2,64},{3,96},{4,128},{5,160},{6,192},{7,224},{8,8},{... | collective-permute-start | bytes 393224 | tf_op jit(solution)/shard_map/ppermute | solution.py:33
  22.5 0.0 collective-permute-done.up_one
  22.5 4.0 %collective-permute-done.1.down_one = bf16[2,2,256,256]{3,2,1,0:T(8,128)(2,1)S(1)} collective-permute-done((bf16[2,2,256,256]{3,2,1,0:T(8,128)(2,1)}, bf16[2,2,256,256]{3,2,1,0:T(8,128)(2,1)S(1)}, u32[]{:S(2)}, u32[]{:S(2)}) %collective-permute-start.1) | collective-permute-done | bytes 524320 | tf_op jit(solution)/shard_map/ppermute | solution.py:33
  26.5 0.8 copy-done.6
  27.4 7.8 %shard_map.102 = (bf16[4,2,256,256]{3,2,1,0:T(8,128)(2,1)}, bf16[4,2,256,256]{3,2,1,0:T(8,128)(2,1)}, bf16[4,2,256,256]{3,2,1,0:T(8,128)(2,1)}) custom-call(s32[5]{0:T(128)} %stack.90.here, bf16[256,512]{1,0:T(8,128)(2,1)} %get-tuple-element.44.cot, bf16[512,8192]{1,0:T(8,128)(2,1)} %activations.3, bf16[2,2,256,256]{3,2,1,0:T(8,128)(2,1)} %copy-done.5, ...), custom_call_target="tpu_custom_call" | custom-call | flops 1610612736 | bytes 9699328 | tf_op jit(solution)/shard_map/pallas_call | solution.py:192
  35.2 0.0 collective-permute-done.3
  35.2 0.0 copy-start
  35.2 0.0 copy-start.1
  35.2 0.0 copy-start.2
  35.2 0.7 maximum_select_fusion.2
  36.0 0.0 all-gather.2.cloned.1.call-update
  36.0 7.2 %collective-permute-start.5 = (bf16[4,2,256,256]{3,2,1,0:T(8,128)(2,1)}, bf16[4,2,256,256]{3,2,1,0:T(8,128)(2,1)S(1)}, u32[]{:S(2)}, u32[]{:S(2)}) collective-permute-start(bf16[4,2,256,256]{3,2,1,0:T(8,128)(2,1)} %get-tuple-element.52), channel_id=1, source_target_pairs={{0,64},{1,17},{2,66},{3,19},{4,68},{5,21},{6,70},{7,23},{8,72},{9,... | collective-permute-start | bytes 3145736 | tf_op jit(solution)/shard_map/ppermute | solution.py:33
  43.2 0.0 collective-permute-start.6
  43.2 2.6 %collective-permute-start.8 = (bf16[512,256]{1,0:T(8,128)(2,1)S(1)}, bf16[512,256]{1,0:T(8,128)(2,1)S(1)}, u32[]{:S(2)}, u32[]{:S(2)}) collective-permute-start(bf16[512,256]{1,0:T(8,128)(2,1)S(1)} %copy-done.7), channel_id=1, source_target_pairs={{0,6},{1,7},{2,0},{3,1},{4,2},{5,3},{6,4},{7,5},{8,14},{9,15},{10,... | collective-permute-start | bytes 786440 | tf_op jit(solution)/shard_map/ppermute | solution.py:33
  45.8 0.0 collective-permute-start.7
  45.8 10.1 %collective-permute-done.5 = bf16[4,2,256,256]{3,2,1,0:T(8,128)(2,1)S(1)} collective-permute-done((bf16[4,2,256,256]{3,2,1,0:T(8,128)(2,1)}, bf16[4,2,256,256]{3,2,1,0:T(8,128)(2,1)S(1)}, u32[]{:S(2)}, u32[]{:S(2)}) %collective-permute-start.5) | collective-permute-done | bytes 1048608 | tf_op jit(solution)/shard_map/ppermute | solution.py:33
  55.9 4.0 %collective-permute-done.6 = bf16[4,2,256,256]{3,2,1,0:T(8,128)(2,1)S(1)} collective-permute-done((bf16[4,2,256,256]{3,2,1,0:T(8,128)(2,1)}, bf16[4,2,256,256]{3,2,1,0:T(8,128)(2,1)S(1)}, u32[]{:S(2)}, u32[]{:S(2)}) %collective-permute-start.6) | collective-permute-done | bytes 1048608 | tf_op jit(solution)/shard_map/ppermute | solution.py:33
  59.9 1.6 add_convert_fusion.3
  61.5 0.0 collective-permute-done.8
  61.5 0.1 pad_maximum_fusion.cot_mine
  61.7 0.0 copy-start.4
  61.7 0.1 collective-permute-start.12
  61.8 1.4 collective-permute-start.9
  63.2 0.7 collective-permute-start.10
  63.9 1.4 collective-permute-start.11
  65.3 3.1 %collective-permute-done.9 = bf16[2,256,256]{2,1,0:T(8,128)(2,1)S(1)} collective-permute-done((bf16[2,256,256]{2,1,0:T(8,128)(2,1)S(1)}, bf16[2,256,256]{2,1,0:T(8,128)(2,1)S(1)}, u32[]{:S(2)}, u32[]{:S(2)}) %collective-permute-start.9) | collective-permute-done | bytes 262176 | tf_op jit(solution)/shard_map/ppermute | solution.py:33
  68.4 1.1 collective-permute-done.10
  69.5 2.2 %collective-permute-done.11 = bf16[2,256,256]{2,1,0:T(8,128)(2,1)S(1)} collective-permute-done((bf16[2,256,256]{2,1,0:T(8,128)(2,1)S(1)}, bf16[2,256,256]{2,1,0:T(8,128)(2,1)S(1)}, u32[]{:S(2)}, u32[]{:S(2)}) %collective-permute-start.11) | collective-permute-done | bytes 262176 | tf_op jit(solution)/shard_map/ppermute | solution.py:33
  71.8 0.1 fusion.10
  71.9 0.0 collective-permute-done.12.cot_theirs
  71.9 0.3 collective-permute-start.13
  72.2 10.2 %collective-permute-done.13.theirs = bf16[256,256]{1,0:T(8,128)(2,1)S(1)} collective-permute-done((bf16[256,256]{1,0:T(8,128)(2,1)S(1)}, bf16[256,256]{1,0:T(8,128)(2,1)S(1)}, u32[]{:S(2)}, u32[]{:S(2)}) %collective-permute-start.13) | collective-permute-done | bytes 131104 | tf_op jit(solution)/shard_map/ppermute | solution.py:33
  82.4 0.4 shard_map.103
  82.8 0.7 collective-permute-start.14
  83.5 8.8 %collective-permute-done.14 = bf16[512,128]{1,0:T(8,128)(2,1)S(1)} collective-permute-done((bf16[512,128]{1,0:T(8,128)(2,1)S(1)}, bf16[512,128]{1,0:T(8,128)(2,1)S(1)}, u32[]{:S(2)}, u32[]{:S(2)}) %collective-permute-start.14) | collective-permute-done | bytes 131104 | tf_op jit(solution)/shard_map/ppermute | solution.py:33
  92.3 1.3 collective-permute-start.17
  93.6 1.1 collective-permute-start.16
  94.7 0.9 collective-permute-start.15
  95.5 1.1 collective-permute-start.22
  96.7 5.1 %collective-permute-done.17 = bf16[2,512,128]{2,1,0:T(8,128)(2,1)S(1)} collective-permute-done((bf16[2,512,128]{2,1,0:T(8,128)(2,1)S(1)}, bf16[2,512,128]{2,1,0:T(8,128)(2,1)S(1)}, u32[]{:S(2)}, u32[]{:S(2)}) %collective-permute-start.17) | collective-permute-done | bytes 262176 | tf_op jit(solution)/shard_map/ppermute | solution.py:33
  101.8 2.8 %collective-permute-done.16 = bf16[2,512,128]{2,1,0:T(8,128)(2,1)S(1)} collective-permute-done((bf16[2,512,128]{2,1,0:T(8,128)(2,1)S(1)}, bf16[2,512,128]{2,1,0:T(8,128)(2,1)S(1)}, u32[]{:S(2)}, u32[]{:S(2)}) %collective-permute-start.16) | collective-permute-done | bytes 262176 | tf_op jit(solution)/shard_map/ppermute | solution.py:33
  104.6 0.1 pad_maximum_fusion.2.refs_1_
  104.7 0.7 collective-permute-done.15
  105.4 0.1 pad_maximum_fusion.1.refs_0_
  105.5 28.3 %collective-permute-start.20 = (bf16[2,2,512,128]{3,2,1,0:T(8,128)(2,1)S(1)}, bf16[2,2,512,128]{3,2,1,0:T(8,128)(2,1)S(1)}, u32[]{:S(2)}, u32[]{:S(2)}) collective-permute-start(bf16[2,2,512,128]{3,2,1,0:T(8,128)(2,1)S(1)} %pad_maximum_fusion.1.refs_0_), channel_id=1, source_target_pairs={{0,64},{1,17},{2,66},{3,19},{4,68},{5,21},{6,70},{7,23},{8,72},{9,... | collective-permute-start | bytes 1572872 | tf_op jit(solution)/shard_map/ppermute | solution.py:33
  133.8 0.0 collective-permute-start.21
  133.8 0.0 collective-permute-start.18
  133.8 2.1 %collective-permute-start.19 = (bf16[2,2,512,128]{3,2,1,0:T(8,128)(2,1)S(1)}, bf16[2,2,512,128]{3,2,1,0:T(8,128)(2,1)}, u32[]{:S(2)}, u32[]{:S(2)}) collective-permute-start(bf16[2,2,512,128]{3,2,1,0:T(8,128)(2,1)S(1)} %pad_maximum_fusion.2.refs_1_), channel_id=1, source_target_pairs={{0,64},{1,17},{2,66},{3,19},{4,68},{5,21},{6,70},{7,23},{8,72},{9,... | collective-permute-start | bytes 1572872 | tf_op jit(solution)/shard_map/ppermute | solution.py:33
  135.8 4.6 %collective-permute-done.20.refs_4_ = bf16[2,2,512,128]{3,2,1,0:T(8,128)(2,1)S(1)} collective-permute-done((bf16[2,2,512,128]{3,2,1,0:T(8,128)(2,1)S(1)}, bf16[2,2,512,128]{3,2,1,0:T(8,128)(2,1)S(1)}, u32[]{:S(2)}, u32[]{:S(2)}) %collective-permute-start.20) | collective-permute-done | bytes 524320 | tf_op jit(solution)/shard_map/ppermute | solution.py:33
  140.5 2.5 %collective-permute-done.21.refs_3_ = bf16[2,2,512,128]{3,2,1,0:T(8,128)(2,1)S(1)} collective-permute-done((bf16[2,2,512,128]{3,2,1,0:T(8,128)(2,1)S(1)}, bf16[2,2,512,128]{3,2,1,0:T(8,128)(2,1)S(1)}, u32[]{:S(2)}, u32[]{:S(2)}) %collective-permute-start.21) | collective-permute-done | bytes 524320 | tf_op jit(solution)/shard_map/ppermute | solution.py:33
  143.0 0.0 collective-permute-start.24
  143.0 2.0 %collective-permute-start.23 = (bf16[2,2,512,128]{3,2,1,0:T(8,128)(2,1)S(1)}, bf16[2,2,512,128]{3,2,1,0:T(8,128)(2,1)S(1)}, u32[]{:S(2)}, u32[]{:S(2)}) collective-permute-start(bf16[2,2,512,128]{3,2,1,0:T(8,128)(2,1)S(1)} %collective-permute-done.20.refs_4_), channel_id=1, source_target_pairs={{0,64},{1,17},{2,66},{3,19},{4,68},{5,21},{6,70},{7,23},{8,72},{9,... | collective-permute-start | bytes 1572872 | tf_op jit(solution)/shard_map/ppermute | solution.py:33
  145.0 0.9 shard_map.106
  145.9 7.0 %shard_map.104 = bf16[512,1024]{1,0:T(8,128)(2,1)} custom-call(s32[5]{0:T(128)} %stack.90.here, bf16[4,512,256]{2,1,0:T(8,128)(2,1)} %copy-done.4, bf16[4,512,256]{2,1,0:T(8,128)(2,1)} %copy-done.8, bf16[16,2,256,256]{3,2,1,0:T(8,128)(2,1)} %all-gather.2.cloned.1.call-done.params), custom_call_target="tpu_custom_call" | custom-call | flops 2147483648 | bytes 5242880 | tf_op jit(solution)/shard_map/pallas_call | solution.py:332
  152.9 0.0 collective-permute-done.19.refs_5_
  152.9 3.1 %shard_map.105.refs_2_ = bf16[32,512,128]{2,1,0:T(8,128)(2,1)} custom-call(s32[5]{0:T(128)S(1)} %copy-done.3, bf16[2,2,512,128]{3,2,1,0:T(8,128)(2,1)S(1)} %pad_maximum_fusion.1.refs_0_, bf16[2,2,512,128]{3,2,1,0:T(8,128)(2,1)S(1)} %pad_maximum_fusion.2.refs_1_, bf16[2,2,512,128]{3,2,1,0:T(8,128)(2,1)} %collective-permute-done.18.refs_2_, ...), custom_call_target="tpu_custom_call" | custom-call | tf_op jit(solution)/shard_map/pallas_call | solution.py:274
  156.0 1.6 shard_map.107
  (23 shorter events, 0.1 us)
Async XLA Ops:
  7.2 138.7 %all-gather.2.cloned.1.call-start = ((), (), s32[]{:S(2)}) async-start(), calls=%async_computation | async-start | bytes 4456448 | tf_op jit(solution)/shard_map/all_gather | solution.py:391
  12.4 10.1 %collective-permute-start = (bf16[2,2,256,256]{3,2,1,0:T(8,128)(2,1)}, bf16[2,2,256,256]{3,2,1,0:T(8,128)(2,1)S(1)}, u32[]{:S(2)}, u32[]{:S(2)}) collective-permute-start(bf16[2,2,256,256]{3,2,1,0:T(8,128)(2,1)} %get-tuple-element.45), channel_id=1, source_target_pairs={{0,64},{1,17},{2,66},{3,19},{4,68},{5,21},{6,70},{7,23},{8,72},{9,... | collective-permute-start | bytes 1572872 | tf_op jit(solution)/shard_map/ppermute | solution.py:33
  14.0 12.5 %collective-permute-start.1 = (bf16[2,2,256,256]{3,2,1,0:T(8,128)(2,1)}, bf16[2,2,256,256]{3,2,1,0:T(8,128)(2,1)S(1)}, u32[]{:S(2)}, u32[]{:S(2)}) collective-permute-start(bf16[2,2,256,256]{3,2,1,0:T(8,128)(2,1)} %get-tuple-element.46), channel_id=1, source_target_pairs={{0,192},{1,49},{2,194},{3,51},{4,196},{5,53},{6,198},{7,55},{8,200... | collective-permute-start | bytes 1572872 | tf_op jit(solution)/shard_map/ppermute | solution.py:33
  14.5 20.7 %collective-permute-start.4 = (bf16[512,256]{1,0:T(8,128)(2,1)}, bf16[512,256]{1,0:T(8,128)(2,1)S(1)}, u32[]{:S(2)}, u32[]{:S(2)}) collective-permute-start(bf16[512,256]{1,0:T(8,128)(2,1)} %get-tuple-element.51), channel_id=1, source_target_pairs={{0,2},{1,3},{2,4},{3,5},{4,6},{5,7},{6,0},{7,1},{8,10},{9,11},{10,... | collective-permute-start | bytes 786440 | tf_op jit(solution)/shard_map/ppermute | solution.py:33
  15.5 19.6 %collective-permute-start.3 = (bf16[256,256]{1,0:T(8,128)(2,1)}, bf16[256,256]{1,0:T(8,128)(2,1)S(1)}, u32[]{:S(2)}, u32[]{:S(2)}) collective-permute-start(bf16[256,256]{1,0:T(8,128)(2,1)} %get-tuple-element.50), channel_id=1, source_target_pairs={{0,8},{1,40},{2,72},{3,104},{4,136},{5,168},{6,200},{7,232},{8,0},... | collective-permute-start | bytes 393224 | tf_op jit(solution)/shard_map/ppermute | solution.py:33
  16.3 18.9 %collective-permute-start.2 = (bf16[256,256]{1,0:T(8,128)(2,1)}, bf16[256,256]{1,0:T(8,128)(2,1)S(1)}, u32[]{:S(2)}, u32[]{:S(2)}) collective-permute-start(bf16[256,256]{1,0:T(8,128)(2,1)} %get-tuple-element.50), channel_id=1, source_target_pairs={{0,0},{1,32},{2,64},{3,96},{4,128},{5,160},{6,192},{7,224},{8,8},{... | collective-permute-start | bytes 393224 | tf_op jit(solution)/shard_map/ppermute | solution.py:33
  22.5 4.0 %copy-start.5 = (bf16[2,2,256,256]{3,2,1,0:T(8,128)(2,1)}, bf16[2,2,256,256]{3,2,1,0:T(8,128)(2,1)S(1)}, u32[]{:S(2)}) copy-start(bf16[2,2,256,256]{3,2,1,0:T(8,128)(2,1)S(1)} %collective-permute-done.up_one) | copy-start | bytes 1572868
  26.5 0.8 copy-start.6
  27.4 15.8 %copy-start.7 = (bf16[512,256]{1,0:T(8,128)(2,1)S(1)}, bf16[512,256]{1,0:T(8,128)(2,1)}, u32[]{:S(2)}) copy-start(bf16[512,256]{1,0:T(8,128)(2,1)} %get-tuple-element.51) | copy-start | bytes 786436
  35.2 47.2 %copy-start = (f32[256,2,128]{2,1,0:T(2,128)S(1)}, f32[256,2,128]{2,1,0:T(2,128)}, u32[]{:S(2)}) copy-start(f32[256,2,128]{2,1,0:T(2,128)} %param.9) | copy-start | bytes 786436
  35.2 47.2 %copy-start.1 = (f32[256,2,128]{2,1,0:T(2,128)S(1)}, f32[256,2,128]{2,1,0:T(2,128)}, u32[]{:S(2)}) copy-start(f32[256,2,128]{2,1,0:T(2,128)} %param.10) | copy-start | bytes 786436
  35.2 47.2 %copy-start.2 = (f32[256,2,128]{2,1,0:T(2,128)S(1)}, f32[256,2,128]{2,1,0:T(2,128)}, u32[]{:S(2)}) copy-start(f32[256,2,128]{2,1,0:T(2,128)} %param.11) | copy-start | bytes 786436
  36.0 19.9 %collective-permute-start.5 = (bf16[4,2,256,256]{3,2,1,0:T(8,128)(2,1)}, bf16[4,2,256,256]{3,2,1,0:T(8,128)(2,1)S(1)}, u32[]{:S(2)}, u32[]{:S(2)}) collective-permute-start(bf16[4,2,256,256]{3,2,1,0:T(8,128)(2,1)} %get-tuple-element.52), channel_id=1, source_target_pairs={{0,64},{1,17},{2,66},{3,19},{4,68},{5,21},{6,70},{7,23},{8,72},{9,... | collective-permute-start | bytes 3145736 | tf_op jit(solution)/shard_map/ppermute | solution.py:33
  43.2 16.7 %collective-permute-start.6 = (bf16[4,2,256,256]{3,2,1,0:T(8,128)(2,1)}, bf16[4,2,256,256]{3,2,1,0:T(8,128)(2,1)S(1)}, u32[]{:S(2)}, u32[]{:S(2)}) collective-permute-start(bf16[4,2,256,256]{3,2,1,0:T(8,128)(2,1)} %get-tuple-element.53), channel_id=1, source_target_pairs={{0,192},{1,49},{2,194},{3,51},{4,196},{5,53},{6,198},{7,55},{8,200... | collective-permute-start | bytes 3145736 | tf_op jit(solution)/shard_map/ppermute | solution.py:33
  43.2 18.4 %collective-permute-start.8 = (bf16[512,256]{1,0:T(8,128)(2,1)S(1)}, bf16[512,256]{1,0:T(8,128)(2,1)S(1)}, u32[]{:S(2)}, u32[]{:S(2)}) collective-permute-start(bf16[512,256]{1,0:T(8,128)(2,1)S(1)} %copy-done.7), channel_id=1, source_target_pairs={{0,6},{1,7},{2,0},{3,1},{4,2},{5,3},{6,4},{7,5},{8,14},{9,15},{10,... | collective-permute-start | bytes 786440 | tf_op jit(solution)/shard_map/ppermute | solution.py:33
  45.8 15.8 %collective-permute-start.7 = (bf16[512,256]{1,0:T(8,128)(2,1)S(1)}, bf16[512,256]{1,0:T(8,128)(2,1)S(1)}, u32[]{:S(2)}, u32[]{:S(2)}) collective-permute-start(bf16[512,256]{1,0:T(8,128)(2,1)S(1)} %collective-permute-done.4), channel_id=1, source_target_pairs={{0,2},{1,3},{2,4},{3,5},{4,6},{5,7},{6,0},{7,1},{8,10},{9,11},{10,... | collective-permute-start | bytes 786440 | tf_op jit(solution)/shard_map/ppermute | solution.py:33
  61.7 20.7 %copy-start.4 = (bf16[4,512,256]{2,1,0:T(8,128)(2,1)}, bf16[4,512,256]{2,1,0:T(8,128)(2,1)S(1)}, u32[]{:S(2)}) copy-start(bf16[4,512,256]{2,1,0:T(8,128)(2,1)S(1)} %pad_maximum_fusion.cot_mine) | copy-start | bytes 3145732
  61.7 10.2 %collective-permute-start.12 = (bf16[4,512,256]{2,1,0:T(8,128)(2,1)S(1)}, bf16[4,512,256]{2,1,0:T(8,128)(2,1)S(1)}, u32[]{:S(2)}, u32[]{:S(2)}) collective-permute-start(bf16[4,512,256]{2,1,0:T(8,128)(2,1)S(1)} %pad_maximum_fusion.cot_mine), channel_id=1, source_target_pairs={{0,1},{1,0},{2,3},{3,2},{4,5},{5,4},{6,7},{7,6},{8,9},{9,8},{10,11... | collective-permute-start | bytes 3145736 | tf_op jit(solution)/shard_map/ppermute | solution.py:33
  61.8 6.6 %collective-permute-start.9 = (bf16[2,256,256]{2,1,0:T(8,128)(2,1)S(1)}, bf16[2,256,256]{2,1,0:T(8,128)(2,1)S(1)}, u32[]{:S(2)}, u32[]{:S(2)}) collective-permute-start(bf16[2,256,256]{2,1,0:T(8,128)(2,1)S(1)} %get-tuple-element.55), channel_id=1, source_target_pairs={{0,16},{1,65},{2,18},{3,67},{4,20},{5,69},{6,22},{7,71},{8,24},{9,... | collective-permute-start | bytes 786440 | tf_op jit(solution)/shard_map/ppermute | solution.py:33
  63.2 6.4 %collective-permute-start.10 = (bf16[2,256,256]{2,1,0:T(8,128)(2,1)S(1)}, bf16[2,256,256]{2,1,0:T(8,128)(2,1)S(1)}, u32[]{:S(2)}, u32[]{:S(2)}) collective-permute-start(bf16[2,256,256]{2,1,0:T(8,128)(2,1)S(1)} %get-tuple-element.56), channel_id=1, source_target_pairs={{0,48},{1,193},{2,50},{3,195},{4,52},{5,197},{6,54},{7,199},{8,56}... | collective-permute-start | bytes 786440 | tf_op jit(solution)/shard_map/ppermute | solution.py:33
  63.9 7.9 %collective-permute-start.11 = (bf16[2,256,256]{2,1,0:T(8,128)(2,1)S(1)}, bf16[2,256,256]{2,1,0:T(8,128)(2,1)S(1)}, u32[]{:S(2)}, u32[]{:S(2)}) collective-permute-start(bf16[2,256,256]{2,1,0:T(8,128)(2,1)S(1)} %get-tuple-element.57), channel_id=1, source_target_pairs={{0,32},{1,129},{2,34},{3,131},{4,36},{5,133},{6,38},{7,135},{8,40}... | collective-permute-start | bytes 786440 | tf_op jit(solution)/shard_map/ppermute | solution.py:33
  71.9 10.5 %copy-start.8 = (bf16[4,512,256]{2,1,0:T(8,128)(2,1)}, bf16[4,512,256]{2,1,0:T(8,128)(2,1)S(1)}, u32[]{:S(2)}) copy-start(bf16[4,512,256]{2,1,0:T(8,128)(2,1)S(1)} %collective-permute-done.12.cot_theirs) | copy-start | bytes 3145732
  71.9 10.4 %collective-permute-start.13 = (bf16[256,256]{1,0:T(8,128)(2,1)S(1)}, bf16[256,256]{1,0:T(8,128)(2,1)S(1)}, u32[]{:S(2)}, u32[]{:S(2)}) collective-permute-start(bf16[256,256]{1,0:T(8,128)(2,1)S(1)} %get-tuple-element.60), channel_id=1, source_target_pairs={{0,8},{1,9},{2,10},{3,11},{4,12},{5,13},{6,14},{7,15},{8,0},{9,1},... | collective-permute-start | bytes 393224 | tf_op jit(solution)/shard_map/ppermute | solution.py:33
  82.8 9.5 %collective-permute-start.14 = (bf16[512,128]{1,0:T(8,128)(2,1)S(1)}, bf16[512,128]{1,0:T(8,128)(2,1)S(1)}, u32[]{:S(2)}, u32[]{:S(2)}) collective-permute-start(bf16[512,128]{1,0:T(8,128)(2,1)S(1)} %get-tuple-element.61), channel_id=1, source_target_pairs={{0,8},{1,9},{2,10},{3,11},{4,12},{5,13},{6,14},{7,15},{8,0},{9,1},... | collective-permute-start | bytes 393224 | tf_op jit(solution)/shard_map/ppermute | solution.py:33
  92.3 9.6 %collective-permute-start.17 = (bf16[2,512,128]{2,1,0:T(8,128)(2,1)S(1)}, bf16[2,512,128]{2,1,0:T(8,128)(2,1)S(1)}, u32[]{:S(2)}, u32[]{:S(2)}) collective-permute-start(bf16[2,512,128]{2,1,0:T(8,128)(2,1)S(1)} %maximum_select_fusion.1), channel_id=1, source_target_pairs={{0,16},{1,65},{2,18},{3,67},{4,20},{5,69},{6,22},{7,71},{8,24},{9,... | collective-permute-start | bytes 786440 | tf_op jit(solution)/shard_map/ppermute | solution.py:33
  93.6 11.1 %collective-permute-start.16 = (bf16[2,512,128]{2,1,0:T(8,128)(2,1)S(1)}, bf16[2,512,128]{2,1,0:T(8,128)(2,1)S(1)}, u32[]{:S(2)}, u32[]{:S(2)}) collective-permute-start(bf16[2,512,128]{2,1,0:T(8,128)(2,1)S(1)} %maximum_select_fusion.1), channel_id=1, source_target_pairs={{0,32},{1,129},{2,34},{3,131},{4,36},{5,133},{6,38},{7,135},{8,40}... | collective-permute-start | bytes 786440 | tf_op jit(solution)/shard_map/ppermute | solution.py:33
  94.7 10.8 %collective-permute-start.15 = (bf16[2,512,128]{2,1,0:T(8,128)(2,1)S(1)}, bf16[2,512,128]{2,1,0:T(8,128)(2,1)S(1)}, u32[]{:S(2)}, u32[]{:S(2)}) collective-permute-start(bf16[2,512,128]{2,1,0:T(8,128)(2,1)S(1)} %maximum_select_fusion.1), channel_id=1, source_target_pairs={{0,48},{1,193},{2,50},{3,195},{4,52},{5,197},{6,54},{7,199},{8,56}... | collective-permute-start | bytes 786440 | tf_op jit(solution)/shard_map/ppermute | solution.py:33
  95.5 40.3 %collective-permute-start.22 = (bf16[4,2,256,128]{3,2,1,0:T(8,128)(2,1)S(1)}, bf16[4,2,256,128]{3,2,1,0:T(8,128)(2,1)S(1)}, u32[]{:S(2)}, u32[]{:S(2)}) collective-permute-start(bf16[4,2,256,128]{3,2,1,0:T(8,128)(2,1)S(1)} %get-tuple-element.71), channel_id=1, source_target_pairs={{0,248},{1,249},{2,250},{3,251},{4,252},{5,253},{6,254},{7,255},{8... | collective-permute-start | bytes 1572872 | tf_op jit(solution)/shard_map/ppermute | solution.py:33
  105.5 47.4 %copy-start.3 = (s32[5]{0:T(128)S(1)}, s32[5]{0:T(128)}, u32[]{:S(2)}) copy-start(s32[5]{0:T(128)} %stack.90.here) | copy-start | bytes 64
  105.5 35.0 %collective-permute-start.20 = (bf16[2,2,512,128]{3,2,1,0:T(8,128)(2,1)S(1)}, bf16[2,2,512,128]{3,2,1,0:T(8,128)(2,1)S(1)}, u32[]{:S(2)}, u32[]{:S(2)}) collective-permute-start(bf16[2,2,512,128]{3,2,1,0:T(8,128)(2,1)S(1)} %pad_maximum_fusion.1.refs_0_), channel_id=1, source_target_pairs={{0,64},{1,17},{2,66},{3,19},{4,68},{5,21},{6,70},{7,23},{8,72},{9,... | collective-permute-start | bytes 1572872 | tf_op jit(solution)/shard_map/ppermute | solution.py:33
  133.8 9.2 %collective-permute-start.21 = (bf16[2,2,512,128]{3,2,1,0:T(8,128)(2,1)S(1)}, bf16[2,2,512,128]{3,2,1,0:T(8,128)(2,1)S(1)}, u32[]{:S(2)}, u32[]{:S(2)}) collective-permute-start(bf16[2,2,512,128]{3,2,1,0:T(8,128)(2,1)S(1)} %pad_maximum_fusion.2.refs_1_), channel_id=1, source_target_pairs={{0,192},{1,49},{2,194},{3,51},{4,196},{5,53},{6,198},{7,55},{8,200... | collective-permute-start | bytes 1572872 | tf_op jit(solution)/shard_map/ppermute | solution.py:33
  133.8 19.1 %collective-permute-start.18 = (bf16[2,2,512,128]{3,2,1,0:T(8,128)(2,1)S(1)}, bf16[2,2,512,128]{3,2,1,0:T(8,128)(2,1)}, u32[]{:S(2)}, u32[]{:S(2)}) collective-permute-start(bf16[2,2,512,128]{3,2,1,0:T(8,128)(2,1)S(1)} %pad_maximum_fusion.1.refs_0_), channel_id=1, source_target_pairs={{0,192},{1,49},{2,194},{3,51},{4,196},{5,53},{6,198},{7,55},{8,200... | collective-permute-start | bytes 1572872 | tf_op jit(solution)/shard_map/ppermute | solution.py:33
  133.8 19.1 %collective-permute-start.19 = (bf16[2,2,512,128]{3,2,1,0:T(8,128)(2,1)S(1)}, bf16[2,2,512,128]{3,2,1,0:T(8,128)(2,1)}, u32[]{:S(2)}, u32[]{:S(2)}) collective-permute-start(bf16[2,2,512,128]{3,2,1,0:T(8,128)(2,1)S(1)} %pad_maximum_fusion.2.refs_1_), channel_id=1, source_target_pairs={{0,64},{1,17},{2,66},{3,19},{4,68},{5,21},{6,70},{7,23},{8,72},{9,... | collective-permute-start | bytes 1572872 | tf_op jit(solution)/shard_map/ppermute | solution.py:33
  143.0 13.0 %collective-permute-start.24 = (bf16[2,2,512,128]{3,2,1,0:T(8,128)(2,1)S(1)}, bf16[2,2,512,128]{3,2,1,0:T(8,128)(2,1)S(1)}, u32[]{:S(2)}, u32[]{:S(2)}) collective-permute-start(bf16[2,2,512,128]{3,2,1,0:T(8,128)(2,1)S(1)} %collective-permute-done.21.refs_3_), channel_id=1, source_target_pairs={{0,192},{1,49},{2,194},{3,51},{4,196},{5,53},{6,198},{7,55},{8,200... | collective-permute-start | bytes 1572872 | tf_op jit(solution)/shard_map/ppermute | solution.py:33
  143.0 13.0 %collective-permute-start.23 = (bf16[2,2,512,128]{3,2,1,0:T(8,128)(2,1)S(1)}, bf16[2,2,512,128]{3,2,1,0:T(8,128)(2,1)S(1)}, u32[]{:S(2)}, u32[]{:S(2)}) collective-permute-start(bf16[2,2,512,128]{3,2,1,0:T(8,128)(2,1)S(1)} %collective-permute-done.20.refs_4_), channel_id=1, source_target_pairs={{0,64},{1,17},{2,66},{3,19},{4,68},{5,21},{6,70},{7,23},{8,72},{9,... | collective-permute-start | bytes 1572872 | tf_op jit(solution)/shard_map/ppermute | solution.py:33
Sparse Core Ops, SparseCore 0:
  36.1 69.1 all-gather.1
